TPU v7x, 512 devices: a whole 4x4x16 slice. The times are simulated.
512 devices in a mesh: chan: 16 (over y, x), stretch: 32 (over z, core).
Axes of the slice: x: 4, y: 4, z: 16, core: 2. Of those that a mesh axis runs over, the one named last changes fastest.
Arguments:
- query_in: bfloat16 [16384, 8192], P('stretch', 'chan'), may hold values from -6 to 6
- key_in: bfloat16 [16384, 8192], P('stretch', 'chan'), may hold values from -6 to 6
- value_in: bfloat16 [16384, 8192], P('stretch', 'chan'), may hold values from -6 to 6
- contig_ids: int32 [16384], P('stretch'), may hold values from 0 to 3, never falling along the last dimension, each value on 1 to 8192 neighbouring positions
- short_taps: float32 [3, 7, 8192], P(None, None, 'chan'), may hold values from -2.4 to 2.4
- medium_taps: float32 [128, 8192], P(None, 'chan'), may hold values from -0.72 to 0.72
- decay_rate: float32 [8192], P('chan'), may hold values from 0.004 to 0.12
- skip_gain: float32 [8192], P('chan'), may hold values from -4 to 4
- out_weight: bfloat16 [8192, 8192], P('stretch', 'chan'), may hold values from -0.0625 to 0.0625
Outputs:
- layer_out: bfloat16 [16384, 8192], P('stretch', 'chan')
Inputs may be any that keep to these rules, and one draw needn't show every extreme that they name: `contig_ids`: contig numbers never fall along the tokens; each of the 4 contigs holds 1 to 8192 tokens, and one holds exactly 8192.
All inputs are finite; a program needn't handle non-finite values.
Results may differ from a plain program's by a relative error of at most 0.0057.
Values may be sent and summed in bfloat16 or wider, within the bound.
No kernel may reach another device: no remote copies, remote signals or barrier semaphores. Data moves between devices by JAX's collectives and lax.ppermute only.
A program may use at most 64 MiB of HBM per device.

v0:
```python
import jax
import jax.numpy as jnp
from jax import lax
from jax.sharding import PartitionSpec as P

MEDIUM = 128
SHORT = 7


def from_behind(value, axis, by):
    size = lax.axis_size(axis)
    pairs = [(i, i + by) for i in range(size) if 0 <= i + by < size]
    return lax.ppermute(value, axis, pairs)


def reach_of(window_ids, lead_rows):
    own_ids = window_ids[lead_rows:]
    before = jnp.sum((window_ids[None, :] < own_ids[:, None]).astype(jnp.int32), axis=1)
    return lead_rows + jnp.arange(own_ids.shape[0], dtype=jnp.int32) - before


def short_filter(source_rows, tap_table, reach_rows, lead_rows, out_rows):
    summed = jnp.zeros((out_rows, source_rows.shape[1]), jnp.float32)
    for offset in range(SHORT):
        shifted = source_rows[lead_rows - offset : lead_rows - offset + out_rows].astype(
            jnp.float32
        )
        summed = summed + jnp.where(
            (reach_rows[:out_rows] >= offset)[:, None], tap_table[offset][None, :] * shifted, 0.0
        )
    return summed


def body(
    query_in,
    key_in,
    value_in,
    contig_ids,
    short_taps,
    medium_taps,
    decay_rate,
    skip_gain,
    out_weight,
):
    tokens, channels = query_in.shape
    tail_rows = MEDIUM - 1
    lead_rows = SHORT - 1
    inputs = (query_in, key_in, value_in)
    local_reach = reach_of(contig_ids, lead_rows)
    late_rows = tokens - lead_rows
    query_late = short_filter(query_in, short_taps[0], local_reach, lead_rows, late_rows)
    key_late = short_filter(key_in, short_taps[1], local_reach, lead_rows, late_rows)
    value_late = short_filter(value_in, short_taps[2], local_reach, lead_rows, late_rows)
    product_late = (key_late * value_late).astype(jnp.bfloat16)
    raw_tail = jnp.stack([stream[tokens - lead_rows :] for stream in inputs])
    product_prev, raw_prev, ids_prev = from_behind(
        (product_late[late_rows - tail_rows :], raw_tail, contig_ids[tokens - tail_rows :]),
        "stretch",
        1,
    )
    reach_rows = reach_of(jnp.concatenate([ids_prev, contig_ids]), tail_rows)
    early_rows = []
    for member in range(3):
        head_rows = jnp.concatenate([raw_prev[member], inputs[member][: 2 * lead_rows]])
        early_rows.append(
            short_filter(head_rows, short_taps[member], reach_rows, lead_rows, lead_rows)
        )
    query_short = jnp.concatenate([early_rows[0], query_late])
    product_early = (early_rows[1] * early_rows[2]).astype(jnp.bfloat16)
    product = jnp.concatenate([product_prev, product_early, product_late])
    lag_steps = jnp.arange(MEDIUM, dtype=jnp.float32)
    filters = medium_taps * jnp.exp(-decay_rate[None, :] * lag_steps[:, None])
    summed = jnp.zeros((tokens, channels), jnp.float32)
    for offset in range(MEDIUM):
        shifted = product[tail_rows - offset : tail_rows - offset + tokens].astype(jnp.float32)
        summed = summed + jnp.where(
            (reach_rows >= offset)[:, None], filters[offset][None, :] * shifted, 0.0
        )
    gated_out = (
        query_short * (summed + skip_gain[None, :] * product[tail_rows:].astype(jnp.float32))
    ).astype(jnp.bfloat16)
    empty = jnp.zeros((tokens, channels), jnp.float32)
    whole_panel = lax.all_gather(gated_out, "chan", axis=1, tiled=True)
    weight_piece = lax.all_gather(out_weight, "stretch", axis=0, tiled=True)
    columns = lax.slice_in_dim(whole_panel, 0, weight_piece.shape[0], axis=1)
    result = empty + jnp.dot(columns, weight_piece, preferred_element_type=jnp.float32)
    return result.astype(jnp.bfloat16)


def solution(mesh):
    placed = (
        P("stretch", "chan"),
        P("stretch", "chan"),
        P("stretch", "chan"),
        P("stretch"),
        P(None, None, "chan"),
        P(None, "chan"),
        P("chan"),
        P("chan"),
        P("stretch", "chan"),
    )
    return jax.shard_map(
        body, mesh=mesh, in_specs=placed, out_specs=P("stretch", "chan"), check_vma=False
    )
```

profile of v0, /device:TPU:1, one launch (start us, length us, event | category | flops | bytes accessed | tf_op | source)
XLA Modules:
  0.0 262.3 jit_solution(8890076005440812113)
XLA Ops:
  6.5 0.0 copy-start.4
  6.5 0.0 copy-start.2
  6.5 0.0 copy-start
  6.6 0.0 slice-start
  6.6 0.0 copy-start.6
  6.6 0.0 copy-start.3
  6.6 0.0 all-gather.3.cloned.1.call-start
  6.6 0.9 slice.1079
  7.5 4.9 %collective-permute-start = (s32[127]{0:T(128)S(1)}, s32[127]{0:T(128)S(1)}, u32[]{:S(2)}, u32[]{:S(2)}) collective-permute-start(s32[127]{0:T(128)S(1)} %slice.1079), channel_id=1, source_target_pairs={{0,1},{1,2},{2,3},{3,4},{4,5},{5,6},{6,7},{7,8},{8,9},{9,10},{10,1... | collective-permute-start | bytes 1532 | tf_op jit(solution)/shard_map/ppermute | solution.py:13
  12.4 0.7 slice_bitcast_fusion.5
  13.1 0.7 slice_bitcast_fusion.3
  13.9 1.9 collective-permute-start.1
  15.8 1.2 fusion.47
  17.0 0.8 fusion.48
  17.8 0.8 slice.1099
  18.5 0.9 convert_reduce_fusion.1
  19.5 8.2 %multiply_convert_fusion = bf16[506,512]{1,0:T(8,128)(2,1)S(1)} fusion(bf16[512,512]{1,0:T(8,128)(2,1)} %param.11, f32[512]{0:T(512)S(1)} %bitcast.203, f32[512]{0:T(512)S(1)} %bitcast.201, f32[512]{0:T(512)S(1)} %bitcast.179, f32[512]{0:T(512)S(1)} %bitcast.181, f32[512]{0:T(512)S(1)} %bitcast.183, f32[512]{0:T(512)S(1)} %bitcast.185, f32[512]{0:T(512)S(1)} %bitcast.187, ...), kind=kLoop, calls=%fused_computation.35 | loop fusion | flops 14508032 | bytes 7804374 | tf_op jit(solution)/shard_map/convert_element_type | solution.py:54
  27.7 3.9 %collective-permute-start.2 = (bf16[127,512]{1,0:T(8,128)(2,1)S(1)}, bf16[127,512]{1,0:T(8,128)(2,1)S(1)}, u32[]{:S(2)}, u32[]{:S(2)}) collective-permute-start(bf16[127,512]{1,0:T(8,128)(2,1)S(1)} %slice.1436), channel_id=1, source_target_pairs={{0,1},{1,2},{2,3},{3,4},{4,5},{5,6},{6,7},{7,8},{8,9},{9,10},{10,1... | collective-permute-start | bytes 390152 | tf_op jit(solution)/shard_map/ppermute | solution.py:13
  31.7 0.0 copy-done.6
  31.7 0.0 copy-done.3
  31.7 0.1 exponential_multiply_fusion
  32.0 0.0 copy-done.2
  32.0 1.5 select_add_fusion.1
  33.5 0.0 collective-permute-done
  33.6 0.0 copy-done.4
  33.6 0.1 pad_add_fusion
  33.6 0.3 convert_reduce_fusion
  33.9 0.3 broadcast_compare_fusion.82
  34.3 0.0 collective-permute-done.1
  34.3 0.0 copy-done.1
  34.3 0.0 slice-done.1
  34.3 0.0 copy-done
  34.3 0.0 slice-done
  34.3 0.1 multiply_convert_fusion.1
  34.4 0.0 slice-done.2
  34.4 0.1 select_add_fusion.2
  34.5 0.0 collective-permute-done.2
  34.5 0.1 pad_maximum_fusion
  34.7 0.0 copy-start.5
  34.7 10.0 %select_add_fusion = f32[512,512]{1,0:T(8,128)S(1)} fusion(bf16[639,512]{1,0:T(8,128)(2,1)S(1)} %pad_maximum_fusion, f32[512]{0:T(512)S(1)} %bitcast.308, f32[512]{0:T(512)S(1)} %bitcast.309, f32[512]{0:T(512)S(1)} %bitcast.310, f32[512]{0:T(512)S(1)} %bitcast.311, f32[512]{0:T(512)S(1)} %bitcast.312, f32[512]{0:T(512)S(1)} %bitcast.313, ...), kind=kLoop, calls=%fused_computation.34 | loop fusion | flops 46661632 | bytes 24229888 | tf_op jit(solution)/shard_map/add | solution.py:76
  44.7 0.0 copy-done.5
  44.7 20.2 %fusion.27 = bf16[512,512]{1,0:T(8,128)(2,1)} fusion(f32[506,512]{1,0:T(8,128)S(1)} %select_add_fusion.1, f32[6,512]{1,0:T(8,128)S(1)} %select_add_fusion.2, f32[512,512]{1,0:T(8,128)S(1)} %select_add_fusion, bf16[639,512]{1,0:T(8,128)(2,1)S(1)} %pad_maximum_fusion, f32[512]{0:T(512)S(1)} %copy-done.5, f32[512]{0:T(512)S(1)} %bitcast.271, ...), kind=kLoop, calls=%fused_computation.31 | loop fusion | flops 90439680 | bytes 47403008 | tf_op jit(solution)/shard_map/convert_element_type | solution.py:81
  64.9 0.0 all-gather.3.cloned.1.call-update
  64.9 0.2 all-gather.5.cloned.1.call-start
  65.2 0.5 all-gather.5.cloned.1.call-update
  65.7 96.3 %all-gather.3.cloned.1.call-done = bf16[512,8192]{1,0:T(8,128)(2,1)} async-done(((bf16[512,512]{1,0:T(8,128)(2,1)}), bf16[512,8192]{1,0:T(8,128)(2,1)}) %all-gather.3.cloned.1.call-update) | async-done | bytes 8388624 | tf_op jit(solution)/shard_map/all_gather | solution.py:83
  162.0 82.5 %all-gather.5.cloned.1.call-done = bf16[8192,512]{1,0:T(8,128)(2,1)} async-done(((bf16[256,512]{1,0:T(8,128)(2,1)}), bf16[8192,512]{1,0:T(8,128)(2,1)}) %all-gather.5.cloned.1.call-update) | async-done | bytes 8388624 | tf_op jit(solution)/shard_map/all_gather | solution.py:84
  244.5 11.0 %convolution_convert_fusion = bf16[512,512]{1,0:T(8,128)(2,1)} fusion(bf16[512,8192]{1,0:T(8,128)(2,1)} %all-gather.3.cloned.1.call-done, bf16[8192,512]{1,0:T(8,128)(2,1)} %all-gather.5.cloned.1.call-done), kind=kOutput, calls=%fused_computation.3 | convolution fusion | flops 4295229440 | bytes 17301504 | tf_op jit(solution)/shard_map/dot_general | solution.py:86
  (17 shorter events, 0.3 us)
Async XLA Ops:
  6.5 27.0 %copy-start.4 = (s32[512]{0:T(512)S(1)}, s32[512]{0:T(512)}, u32[]{:S(2)}) copy-start(s32[512]{0:T(512)} %param.12) | copy-start | bytes 6148
  6.5 25.5 %copy-start.2 = (bf16[512,512]{1,0:T(8,128)(2,1)S(1)}, bf16[512,512]{1,0:T(8,128)(2,1)}, u32[]{:S(2)}) copy-start(bf16[512,512]{1,0:T(8,128)(2,1)} %param.9) | copy-start | bytes 1572868
  6.5 27.9 %slice-start.2 = ((bf16[512,512]{1,0:T(8,128)(2,1)}), bf16[12,512]{1,0:T(8,128)(2,1)S(1)}, s32[]{:S(2)}) async-start(bf16[512,512]{1,0:T(8,128)(2,1)} %param.9), calls=%async_computation.4 | async-start | bytes 32768 | tf_op jit(solution)/shard_map/slice | solution.py:64
  6.5 27.7 %copy-start.1 = (bf16[512,512]{1,0:T(8,128)(2,1)S(1)}, bf16[512,512]{1,0:T(8,128)(2,1)}, u32[]{:S(2)}) copy-start(bf16[512,512]{1,0:T(8,128)(2,1)} %param.10) | copy-start | bytes 1572868
  6.5 27.7 %slice-start.1 = ((bf16[512,512]{1,0:T(8,128)(2,1)}), bf16[12,512]{1,0:T(8,128)(2,1)S(1)}, s32[]{:S(2)}) async-start(bf16[512,512]{1,0:T(8,128)(2,1)} %param.10), calls=%async_computation.3 | async-start | bytes 32768 | tf_op jit(solution)/shard_map/slice | solution.py:64
  6.5 27.8 %copy-start = (bf16[512,512]{1,0:T(8,128)(2,1)S(1)}, bf16[512,512]{1,0:T(8,128)(2,1)}, u32[]{:S(2)}) copy-start(bf16[512,512]{1,0:T(8,128)(2,1)} %param.11) | copy-start | bytes 1572868
  6.6 27.7 %slice-start = ((bf16[512,512]{1,0:T(8,128)(2,1)}), bf16[12,512]{1,0:T(8,128)(2,1)S(1)}, s32[]{:S(2)}) async-start(bf16[512,512]{1,0:T(8,128)(2,1)} %param.11), calls=%async_computation.2 | async-start | bytes 32768 | tf_op jit(solution)/shard_map/slice | solution.py:64
  6.6 25.1 %copy-start.6 = (f32[512]{0:T(512)S(1)}, f32[512]{0:T(512)}, u32[]{:S(2)}) copy-start(f32[512]{0:T(512)} %param.15) | copy-start | bytes 6148
  6.6 25.1 %copy-start.3 = (f32[128,512]{1,0:T(8,128)S(1)}, f32[128,512]{1,0:T(8,128)}, u32[]{:S(2)}) copy-start(f32[128,512]{1,0:T(8,128)} %param.14) | copy-start | bytes 786436
  6.6 155.4 %all-gather.3.cloned.1.call-start = ((), (), s32[]{:S(2)}) async-start(), calls=%async_computation | async-start | bytes 8912896 | tf_op jit(solution)/shard_map/all_gather | solution.py:83
  7.5 26.0 %collective-permute-start = (s32[127]{0:T(128)S(1)}, s32[127]{0:T(128)S(1)}, u32[]{:S(2)}, u32[]{:S(2)}) collective-permute-start(s32[127]{0:T(128)S(1)} %slice.1079), channel_id=1, source_target_pairs={{0,1},{1,2},{2,3},{3,4},{4,5},{5,6},{6,7},{7,8},{8,9},{9,10},{10,1... | collective-permute-start | bytes 1532 | tf_op jit(solution)/shard_map/ppermute | solution.py:13
  13.9 20.4 %collective-permute-start.1 = (bf16[3,6,512]{2,1,0:T(8,128)(2,1)S(1)}, bf16[3,6,512]{2,1,0:T(8,128)(2,1)S(1)}, u32[]{:S(2)}, u32[]{:S(2)}) collective-permute-start(bf16[3,6,512]{2,1,0:T(8,128)(2,1)S(1)} %pad_maximum_fusion.2), channel_id=1, source_target_pairs={{0,1},{1,2},{2,3},{3,4},{4,5},{5,6},{6,7},{7,8},{8,9},{9,10},{10,1... | collective-permute-start | bytes 55304 | tf_op jit(solution)/shard_map/ppermute | solution.py:13
  27.7 6.8 %collective-permute-start.2 = (bf16[127,512]{1,0:T(8,128)(2,1)S(1)}, bf16[127,512]{1,0:T(8,128)(2,1)S(1)}, u32[]{:S(2)}, u32[]{:S(2)}) collective-permute-start(bf16[127,512]{1,0:T(8,128)(2,1)S(1)} %slice.1436), channel_id=1, source_target_pairs={{0,1},{1,2},{2,3},{3,4},{4,5},{5,6},{6,7},{7,8},{8,9},{9,10},{10,1... | collective-permute-start | bytes 390152 | tf_op jit(solution)/shard_map/ppermute | solution.py:13
  34.7 10.0 %copy-start.5 = (f32[512]{0:T(512)S(1)}, f32[512]{0:T(512)}, u32[]{:S(2)}) copy-start(f32[512]{0:T(512)} %param.16) | copy-start | bytes 6148
  64.9 179.5 %all-gather.5.cloned.1.call-start = ((), (), s32[]{:S(2)}) async-start(), calls=%async_computation.1 | async-start | bytes 8650752 | tf_op jit(solution)/shard_map/all_gather | solution.py:84
Sparse Core Ops, SparseCore 0:
  65.1 96.8 all-gather.2
  164.1 80.3 all-gather.4
where the time goes:
time: 263 us; the launch traced here: 262 us
  waiting for transfers between devices  179 us (68%)
  other arithmetic  41.9 us (16%)
  between operations  13.7 us (5%)
  starting transfers between devices  11 us (4%)
  matrix products  11 us (4%)
  local copies, waits for them, and re-layouts  5.32 us (2%)
    all_gather x1, waiting for transfers between devices, body(): whole_panel = lax.all_gather(gated_out, 'chan', axis=1, tiled=True)  96.3 us
    all_gather x1, waiting for transfers between devices, body(): weight_piece = lax.all_gather(out_weight, 'stretch', axis=0, tiled=True)  82.5 us
    convert_element_type x1, other arithmetic, body(): gated_out = (query_short * (summed + skip_gain[None, :] * product[tail_ro...  20.2 us
    dot_general x1, matrix products, body(): jnp.dot(columns, weight_piece, preferred_element_type=jnp.float32)  11 us
    ppermute x3, starting transfers between devices, from_behind(): return lax.ppermute(value, axis, pairs)  10.8 us
    add x1, other arithmetic, body(): summed + jnp.where((reach_rows >= offset)[:, None], filters[offset][None,...  9.99 us
    convert_element_type x1, other arithmetic, body(): product_late = (key_late * value_late).astype(jnp.bfloat16)  8.19 us
  transfers between devices with their start and end apart: 5, of which 2 were waited for; matrix products, arithmetic and copies ran while one was open for 6% of the time, Pallas kernels for 0%

commit v1 on v0

v1 whole, which is shorter than its diff:
```python
import functools

import jax
import jax.numpy as jnp
from jax import lax
from jax.experimental import pallas as pl
from jax.experimental.pallas import tpu as pltpu
from jax.sharding import PartitionSpec as P

MEDIUM = 128
SHORT = 7
SIDE = 4
HALO = 144
HALF = 256
WINDOW = HALO + HALF
LEAD = 16
PRODUCTS = WINDOW - LEAD
TILE = 64
LANES = 128
OFFSETS = (0, -1, 1, 2)


def along_x(value, by):
    pairs = [
        (y * SIDE + x, y * SIDE + (x + by) % SIDE) for y in range(SIDE) for x in range(SIDE)
    ]
    return lax.ppermute(value, "chan", pairs)


def along_y(value, by):
    pairs = [
        (y * SIDE + x, (y + by) % SIDE * SIDE + x) for y in range(SIDE) for x in range(SIDE)
    ]
    return lax.ppermute(value, "chan", pairs)


def id_column(row):
    return jnp.broadcast_to(row, (LANES, LANES)).T


def filter_kernel(late, *refs):
    if late:
        halo_ref = halo_ids_ref = None
    else:
        halo_ref, halo_ids_ref, *refs = refs
    (query_ref, key_ref, value_ref, ids_ref, short_ref, medium_ref, decay_ref, skip_ref) = refs[:8]
    out_ref, query_f, key_f, value_f, ids_f, product_f, masked_f, taps_f, span = refs[8:]
    tiles = HALF // TILE

    @pl.when(pl.program_id(0) == 0)
    def _():
        own = [id_column(ids_ref[i : i + 1, :].astype(jnp.float32)) for i in range(4)]
        if late:
            ids_f[0:16, :] = own[0][112:128]
            for i in range(1, 4):
                ids_f[16 + 128 * (i - 1) : 16 + 128 * i, :] = own[i]
        else:
            before = [
                id_column(halo_ids_ref[0:1, 128 * i : 128 * i + 128].astype(jnp.float32))
                for i in (2, 3)
            ]
            ids_f[0:16, :] = before[0][112:128]
            ids_f[16:144, :] = before[1]
            ids_f[144:272, :] = own[0]
            ids_f[272:400, :] = own[1]
        for tile in range(tiles):
            rows = ids_f[HALO + TILE * tile : HALO + TILE * (tile + 1), :]
            span[2 * tile] = jnp.min(rows).astype(jnp.int32)
            span[2 * tile + 1] = jnp.max(rows).astype(jnp.int32)

    if late:
        first = 512 - WINDOW
        key_f[...] = key_ref[first:, :].astype(jnp.float32)
        value_f[...] = value_ref[first:, :].astype(jnp.float32)
        query_f[...] = query_ref[512 - HALF - 16 :, :].astype(jnp.float32)
    else:
        key_f[0:HALO, :] = halo_ref[0:HALO, :].astype(jnp.float32)
        key_f[HALO:, :] = key_ref[0:HALF, :].astype(jnp.float32)
        value_f[0:HALO, :] = halo_ref[HALO : 2 * HALO, :].astype(jnp.float32)
        value_f[HALO:, :] = value_ref[0:HALF, :].astype(jnp.float32)
        query_f[0:16, :] = halo_ref[2 * HALO : 2 * HALO + 16, :].astype(jnp.float32)
        query_f[16:, :] = query_ref[0:HALF, :].astype(jnp.float32)

    lag = lax.broadcasted_iota(jnp.int32, (MEDIUM, LANES), 0).astype(jnp.float32)
    taps_f[...] = medium_ref[...] * jnp.exp(-decay_ref[...] * lag)

    for tile in range(PRODUCTS // TILE):
        at = LEAD + TILE * tile
        here = ids_f[at : at + TILE, :]
        key_s = key_f[at : at + TILE, :] * short_ref[1, 0:1, :]
        value_s = value_f[at : at + TILE, :] * short_ref[2, 0:1, :]
        for j in range(1, SHORT):
            same = ids_f[at - j : at - j + TILE, :] == here
            key_s += jnp.where(same, key_f[at - j : at - j + TILE, :] * short_ref[1, j : j + 1, :], 0.0)
            value_s += jnp.where(
                same, value_f[at - j : at - j + TILE, :] * short_ref[2, j : j + 1, :], 0.0
            )
        product_f[TILE * tile : TILE * (tile + 1), :] = (
            (key_s * value_s).astype(jnp.bfloat16).astype(jnp.float32)
        )

    for tile in range(tiles):
        at = HALO + TILE * tile
        here = ids_f[at : at + TILE, :]
        query_s = query_f[16 + TILE * tile : 16 + TILE * (tile + 1), :] * short_ref[0, 0:1, :]
        for j in range(1, SHORT):
            same = ids_f[at - j : at - j + TILE, :] == here
            begin = 16 + TILE * tile - j
            query_s += jnp.where(
                same, query_f[begin : begin + TILE, :] * short_ref[0, j : j + 1, :], 0.0
            )

        def one_contig(contig, summed, tile=tile, here=here):
            contig = contig.astype(jnp.float32)
            reach = TILE + MEDIUM
            begin = TILE * tile
            masked_f[...] = jnp.where(
                ids_f[LEAD + begin : LEAD + begin + reach, :] == contig,
                product_f[begin : begin + reach, :],
                0.0,
            )
            total = jnp.zeros((TILE, LANES), jnp.float32)
            for r in range(8):
                shifted = masked_f[8 - r : 8 - r + reach - 8, :]
                for a in range(MEDIUM // 8):
                    total += (
                        taps_f[8 * a + r : 8 * a + r + 1, :]
                        * shifted[8 * (15 - a) : 8 * (15 - a) + TILE]
                    )
            return jnp.where(here == contig, total, summed)

        summed = lax.fori_loop(
            span[2 * tile],
            span[2 * tile + 1] + 1,
            one_contig,
            jnp.zeros((TILE, LANES), jnp.float32),
        )
        product = product_f[MEDIUM + TILE * tile : MEDIUM + TILE * (tile + 1), :]
        out_ref[TILE * tile : TILE * (tile + 1), :] = (
            query_s * (summed + skip_ref[...] * product)
        ).astype(jnp.bfloat16)


def gate(late, halo, query, key, value, ids, short_taps, medium_taps, decay, skip):
    channels = query.shape[1]
    whole = lambda rows: pl.BlockSpec((rows, LANES), lambda i: (0, i))
    specs = [whole(512)] * 3 + [
        pl.BlockSpec((4, LANES), lambda i: (0, 0)),
        pl.BlockSpec((3, SHORT, LANES), lambda i: (0, 0, i)),
        whole(MEDIUM),
        whole(1),
        whole(1),
    ]
    args = [query, key, value, ids, short_taps, medium_taps, decay, skip]
    if not late:
        ids_block = (2 * HALO + 16) // 16
        specs = [whole(halo.shape[0]), pl.BlockSpec((16, channels), lambda i: (ids_block, 0))] + specs
        args = [halo, halo] + args
    f32 = lambda rows: pltpu.VMEM((rows, LANES), jnp.float32)
    return pl.pallas_call(
        functools.partial(filter_kernel, late),
        grid=(channels // LANES,),
        out_shape=jax.ShapeDtypeStruct((HALF, channels), jnp.bfloat16),
        in_specs=specs,
        out_specs=pl.BlockSpec((HALF, LANES), lambda i: (0, i)),
        scratch_shapes=[
            f32(HALF + 16),
            f32(WINDOW),
            f32(WINDOW),
            f32(WINDOW),
            f32(PRODUCTS),
            f32(TILE + MEDIUM),
            f32(MEDIUM),
            pltpu.SMEM((2 * HALF // TILE,), jnp.int32),
        ],
        compiler_params=pltpu.CompilerParams(vmem_limit_bytes=24 << 20),
        cost_estimate=pl.CostEstimate(
            flops=2 * MEDIUM * HALF * channels * 4, bytes_accessed=2 << 20, transcendentals=65536
        ),
        name="gate_late" if late else "gate_early",
    )(*args)


def project_kernel(places, *refs):
    panels = refs[:8]
    weight, out_ref, blocks, weights, total, block_sem, weight_sem = refs[8:]
    copies = []
    for iy in range(SIDE):
        for ix in range(SIDE):
            at = SIDE * iy + ix
            mine = []
            mine.append(
                pltpu.make_async_copy(weight.at[places[at]], weights.at[at], weight_sem.at[at])
            )
            mine.append(
                pltpu.make_async_copy(
                    panels[iy].at[ix], blocks.at[at, pl.ds(HALF, HALF)], block_sem.at[2 * at]
                )
            )
            mine.append(
                pltpu.make_async_copy(
                    panels[4 + ix].at[iy], blocks.at[at, pl.ds(0, HALF)], block_sem.at[2 * at + 1]
                )
            )
            for copy in mine:
                copy.start()
            copies.append(mine)
    total[...] = jnp.zeros_like(total)
    for at in range(SIDE * SIDE):
        for copy in copies[at]:
            copy.wait()
        total[...] += jnp.dot(blocks[at], weights[at], preferred_element_type=jnp.float32)
    out_ref[...] = total[...].astype(jnp.bfloat16)


def project(late, early, weight):
    me = lax.axis_index("chan")
    y, x = me // SIDE, me % SIDE
    places = jnp.stack(
        [(y + oy) % SIDE * SIDE + (x + ox) % SIDE for oy in OFFSETS for ox in OFFSETS]
    ).astype(jnp.int32)
    columns = weight.shape[1]
    slots = SIDE * SIDE
    panels = [p.reshape(SIDE, HALF, -1) for p in (*late, *early)]
    depth = panels[0].shape[-1]
    hbm = pl.BlockSpec(memory_space=pl.ANY)
    return pl.pallas_call(
        project_kernel,
        out_shape=jax.ShapeDtypeStruct((2 * HALF, columns), jnp.bfloat16),
        in_specs=[pl.BlockSpec(memory_space=pltpu.SMEM)] + [hbm] * 9,
        out_specs=pl.BlockSpec(memory_space=pltpu.VMEM),
        scratch_shapes=[
            pltpu.VMEM((slots, 2 * HALF, depth), jnp.bfloat16),
            pltpu.VMEM((slots, depth, columns), jnp.bfloat16),
            pltpu.VMEM((2 * HALF, columns), jnp.float32),
            pltpu.SemaphoreType.DMA((2 * slots,)),
            pltpu.SemaphoreType.DMA((slots,)),
        ],
        compiler_params=pltpu.CompilerParams(vmem_limit_bytes=40 << 20),
        cost_estimate=pl.CostEstimate(
            flops=2 * 2 * HALF * slots * depth * columns, bytes_accessed=17 << 20, transcendentals=0
        ),
        name="project",
    )(places, *panels, weight.reshape(slots, depth, columns))


def body(
    query_in,
    key_in,
    value_in,
    contig_ids,
    short_taps,
    medium_taps,
    decay_rate,
    skip_gain,
    out_weight,
):
    tokens, channels = query_in.shape
    weight = lax.all_gather(out_weight, "stretch", axis=0, tiled=True)
    id_rows = jnp.broadcast_to(contig_ids.astype(jnp.bfloat16)[None, :], (16, tokens))
    pack = jnp.concatenate(
        [key_in[tokens - HALO :], value_in[tokens - HALO :], query_in[tokens - 16 :], id_rows]
    )
    devices = lax.axis_size("stretch")
    halo = lax.ppermute(pack, "stretch", [(i, i + 1) for i in range(devices - 1)])
    rest = (
        query_in,
        key_in,
        value_in,
        contig_ids.reshape(-1, LANES),
        short_taps,
        medium_taps,
        decay_rate[None, :],
        skip_gain[None, :],
    )
    late = gate(True, None, *rest)
    late_x = jnp.concatenate([late] + [along_x(late, -by) for by in OFFSETS[1:]])
    early = gate(False, halo, *rest)
    early_y = jnp.concatenate([early] + [along_y(early, -by) for by in OFFSETS[1:]])
    late_all = [late_x] + [along_y(late_x, -by) for by in OFFSETS[1:]]
    early_all = [early_y] + [along_x(early_y, -by) for by in OFFSETS[1:]]
    return project(late_all, early_all, weight)


def solution(mesh):
    placed = (
        P("stretch", "chan"),
        P("stretch", "chan"),
        P("stretch", "chan"),
        P("stretch"),
        P(None, None, "chan"),
        P(None, "chan"),
        P("chan"),
        P("chan"),
        P("stretch", "chan"),
    )
    return jax.shard_map(
        body, mesh=mesh, in_specs=placed, out_specs=P("stretch", "chan"), check_vma=False
    )
```

time: 263 us -> 153 us (0.58)
  the two profiles are of different devices: /device:TPU:1 before, /device:TPU:225 now
where the time goes in v1:
time: 153 us
  waiting for transfers between devices  64.7 us (42%)
  starting transfers between devices  44.3 us (29%)
  Pallas kernels  22.6 us (15%)
  between operations  13.8 us (9%)
  local copies, waits for them, and re-layouts  7.02 us (5%)
    ppermute x6, waiting for transfers between devices, along_x(): return lax.ppermute(value, 'chan', pairs)  35.5 us
    ppermute x6, starting transfers between devices, along_y(): return lax.ppermute(value, 'chan', pairs)  20 us
    ppermute x6, waiting for transfers between devices, along_y(): return lax.ppermute(value, 'chan', pairs)  17.6 us
    ppermute x6, starting transfers between devices, along_x(): return lax.ppermute(value, 'chan', pairs)  17.3 us
    pallas_call x2, Pallas kernels, gate(): pl.pallas_call(functools.partial(filter_kernel, late), grid=(channels //...  14.5 us
    ppermute x1, waiting for transfers between devices, body(): lax.ppermute(pack, 'stretch', [(i, i + 1) for i in range(devices - 1)])  10.9 us
    pallas_call x1, Pallas kernels, project(): pl.pallas_call(project_kernel, out_shape=jax.ShapeDtypeStruct((2 * HALF,...  8.12 us
    ppermute x1, starting transfers between devices, body(): lax.ppermute(pack, 'stretch', [(i, i + 1) for i in range(devices - 1)])  6.98 us
  transfers between devices with their start and end apart: 14, of which 10 were waited for; matrix products, arithmetic and copies ran while one was open for 0% of the time, Pallas kernels for 10%

profile of v1, /device:TPU:225, one launch (start us, length us, event | category | flops | bytes accessed | tf_op | source)
XLA Modules:
  0.0 152.6 jit_solution(6603377555203877326)
XLA Ops:
  6.5 0.0 all-gather.2.cloned.1.call-start
  6.5 0.7 all-gather.2.cloned.1.call-update
  7.3 0.0 copy-start
  7.3 1.0 copy-done
  8.3 0.0 copy-start.1
  8.3 1.0 copy-done.1
  9.3 0.0 copy-start.2
  9.3 1.0 copy-done.2
  10.4 0.9 copy-done.3
  11.3 0.8 copy-done.4
  12.1 0.7 copy-done.5
  12.8 0.7 copy-done.6
  13.5 0.7 copy-done.7
  14.2 7.2 %gate_late.1 = bf16[256,512]{1,0:T(8,128)(2,1)S(1)} custom-call(bf16[512,512]{1,0:T(8,128)(2,1)S(1)} %copy-done.2, bf16[512,512]{1,0:T(8,128)(2,1)S(1)} %copy-done, bf16[512,512]{1,0:T(8,128)(2,1)S(1)} %copy-done.1, s32[4,128]{1,0:T(4,128)S(1)} %bitcast.31, f32[3,7,512]{2,1,0:T(8,128)S(1)} %copy-done.4, f32[128,512]{1,0:T(8,128)S(1)} %copy-done.3, ...), custom_call_target="tpu_custom_call" | custom-call | flops 134217728 | bytes 2097152 | tf_op jit(solution)/shard_map/gate_late/pallas_call | solution.py:160
  21.4 4.7 %collective-permute-start.2 = (bf16[256,512]{1,0:T(8,128)(2,1)S(1)}, bf16[256,512]{1,0:T(8,128)(2,1)S(1)}, u32[]{:S(2)}, u32[]{:S(2)}) collective-permute-start(bf16[256,512]{1,0:T(8,128)(2,1)S(1)} %gate_late.1), channel_id=1, source_target_pairs={{0,64},{32,96},{64,0},{96,32},{128,192},{160,224},{192,128},{224,1... | collective-permute-start | bytes 786440 | tf_op jit(solution)/shard_map/ppermute | solution.py:27
  26.1 2.8 %collective-permute-start.1 = (bf16[256,512]{1,0:T(8,128)(2,1)S(1)}, bf16[256,512]{1,0:T(8,128)(2,1)S(1)}, u32[]{:S(2)}, u32[]{:S(2)}) collective-permute-start(bf16[256,512]{1,0:T(8,128)(2,1)S(1)} %gate_late.1), channel_id=1, source_target_pairs={{0,96},{32,0},{64,32},{96,64},{128,224},{160,128},{192,160},{224,1... | collective-permute-start | bytes 786440 | tf_op jit(solution)/shard_map/ppermute | solution.py:27
  28.8 2.5 %collective-permute-start = (bf16[256,512]{1,0:T(8,128)(2,1)S(1)}, bf16[256,512]{1,0:T(8,128)(2,1)S(1)}, u32[]{:S(2)}, u32[]{:S(2)}) collective-permute-start(bf16[256,512]{1,0:T(8,128)(2,1)S(1)} %gate_late.1), channel_id=1, source_target_pairs={{0,32},{32,64},{64,96},{96,0},{128,160},{160,192},{192,224},{224,1... | collective-permute-start | bytes 786440 | tf_op jit(solution)/shard_map/ppermute | solution.py:27
  31.4 0.6 collective-permute-done.2
  32.0 5.7 %collective-permute-done.1 = bf16[256,512]{1,0:T(8,128)(2,1)S(1)} collective-permute-done((bf16[256,512]{1,0:T(8,128)(2,1)S(1)}, bf16[256,512]{1,0:T(8,128)(2,1)S(1)}, u32[]{:S(2)}, u32[]{:S(2)}) %collective-permute-start.1) | collective-permute-done | bytes 262176 | tf_op jit(solution)/shard_map/ppermute | solution.py:27
  37.7 0.9 collective-permute-done
  38.6 0.1 pad_maximum_fusion
  38.7 4.8 %collective-permute-start.5 = (bf16[1024,512]{1,0:T(8,128)(2,1)S(1)}, bf16[1024,512]{1,0:T(8,128)(2,1)S(1)}, u32[]{:S(2)}, u32[]{:S(2)}) collective-permute-start(bf16[1024,512]{1,0:T(8,128)(2,1)S(1)} %pad_maximum_fusion), channel_id=1, source_target_pairs={{0,256},{32,288},{64,320},{96,352},{128,384},{160,416},{192,448},{... | collective-permute-start | bytes 3145736 | tf_op jit(solution)/shard_map/ppermute | solution.py:34
  43.5 0.0 slice-done
  43.5 0.0 slice-done.1
  43.6 0.0 slice-done.2
  43.6 7.0 %collective-permute-start.6 = (bf16[320,512]{1,0:T(8,128)(2,1)S(1)}, bf16[320,512]{1,0:T(8,128)(2,1)S(1)}, u32[]{:S(2)}, u32[]{:S(2)}) collective-permute-start(bf16[320,512]{1,0:T(8,128)(2,1)S(1)} %pad_maximum_fusion.2), channel_id=1, source_target_pairs={{0,1},{1,2},{2,3},{3,4},{4,5},{5,6},{6,7},{7,8},{8,9},{9,10},{10,1... | collective-permute-start | bytes 983048 | tf_op jit(solution)/shard_map/ppermute | solution.py:265
  50.6 10.9 %collective-permute-done.6.refs_0_.refs_1_ = bf16[320,512]{1,0:T(8,128)(2,1)S(1)} collective-permute-done((bf16[320,512]{1,0:T(8,128)(2,1)S(1)}, bf16[320,512]{1,0:T(8,128)(2,1)S(1)}, u32[]{:S(2)}, u32[]{:S(2)}) %collective-permute-start.6) | collective-permute-done | bytes 327712 | tf_op jit(solution)/shard_map/ppermute | solution.py:265
  61.5 7.3 %gate_early.1 = bf16[256,512]{1,0:T(8,128)(2,1)S(1)} custom-call(bf16[320,512]{1,0:T(8,128)(2,1)S(1)} %collective-permute-done.6.refs_0_.refs_1_, bf16[320,512]{1,0:T(8,128)(2,1)S(1)} %collective-permute-done.6.refs_0_.refs_1_, bf16[512,512]{1,0:T(8,128)(2,1)S(1)} %copy-done.2, bf16[512,512]{1,0:T(8,128)(2,1)S(1)} %copy-done, ...), custom_call_target="tpu_custom_call" | custom-call | flops 134217728 | bytes 2097152 | tf_op jit(solution)/shard_map/gate_early/pallas_call | solution.py:160
  68.8 1.9 %collective-permute-start.9 = (bf16[256,512]{1,0:T(8,128)(2,1)S(1)}, bf16[256,512]{1,0:T(8,128)(2,1)S(1)}, u32[]{:S(2)}, u32[]{:S(2)}) collective-permute-start(bf16[256,512]{1,0:T(8,128)(2,1)S(1)} %gate_early.1), channel_id=1, source_target_pairs={{0,256},{32,288},{64,320},{96,352},{128,384},{160,416},{192,448},{... | collective-permute-start | bytes 786440 | tf_op jit(solution)/shard_map/ppermute | solution.py:34
  70.7 4.8 %collective-permute-start.8 = (bf16[256,512]{1,0:T(8,128)(2,1)S(1)}, bf16[256,512]{1,0:T(8,128)(2,1)S(1)}, u32[]{:S(2)}, u32[]{:S(2)}) collective-permute-start(bf16[256,512]{1,0:T(8,128)(2,1)S(1)} %gate_early.1), channel_id=1, source_target_pairs={{0,384},{32,416},{64,448},{96,480},{128,0},{160,32},{192,64},{224,... | collective-permute-start | bytes 786440 | tf_op jit(solution)/shard_map/ppermute | solution.py:34
  75.5 1.9 %collective-permute-start.7 = (bf16[256,512]{1,0:T(8,128)(2,1)S(1)}, bf16[256,512]{1,0:T(8,128)(2,1)S(1)}, u32[]{:S(2)}, u32[]{:S(2)}) collective-permute-start(bf16[256,512]{1,0:T(8,128)(2,1)S(1)} %gate_early.1), channel_id=1, source_target_pairs={{0,128},{32,160},{64,192},{96,224},{128,256},{160,288},{192,320},{... | collective-permute-start | bytes 786440 | tf_op jit(solution)/shard_map/ppermute | solution.py:34
  77.4 4.6 %collective-permute-start.4 = (bf16[1024,512]{1,0:T(8,128)(2,1)S(1)}, bf16[1024,512]{1,0:T(8,128)(2,1)}, u32[]{:S(2)}, u32[]{:S(2)}) collective-permute-start(bf16[1024,512]{1,0:T(8,128)(2,1)S(1)} %pad_maximum_fusion), channel_id=1, source_target_pairs={{0,384},{32,416},{64,448},{96,480},{128,0},{160,32},{192,64},{224,... | collective-permute-start | bytes 3145736 | tf_op jit(solution)/shard_map/ppermute | solution.py:34
  82.0 0.0 collective-permute-done.9
  82.0 1.9 %collective-permute-start.3 = (bf16[1024,512]{1,0:T(8,128)(2,1)S(1)}, bf16[1024,512]{1,0:T(8,128)(2,1)}, u32[]{:S(2)}, u32[]{:S(2)}) collective-permute-start(bf16[1024,512]{1,0:T(8,128)(2,1)S(1)} %pad_maximum_fusion), channel_id=1, source_target_pairs={{0,128},{32,160},{64,192},{96,224},{128,256},{160,288},{192,320},{... | collective-permute-start | bytes 3145736 | tf_op jit(solution)/shard_map/ppermute | solution.py:34
  84.0 0.0 collective-permute-done.8
  84.0 2.5 %collective-permute-done.7 = bf16[256,512]{1,0:T(8,128)(2,1)S(1)} collective-permute-done((bf16[256,512]{1,0:T(8,128)(2,1)S(1)}, bf16[256,512]{1,0:T(8,128)(2,1)S(1)}, u32[]{:S(2)}, u32[]{:S(2)}) %collective-permute-start.7) | collective-permute-done | bytes 262176 | tf_op jit(solution)/shard_map/ppermute | solution.py:34
  86.5 0.1 pad_maximum_fusion.1
  86.6 2.1 %collective-permute-start.12 = (bf16[1024,512]{1,0:T(8,128)(2,1)S(1)}, bf16[1024,512]{1,0:T(8,128)(2,1)}, u32[]{:S(2)}, u32[]{:S(2)}) collective-permute-start(bf16[1024,512]{1,0:T(8,128)(2,1)S(1)} %pad_maximum_fusion.1), channel_id=1, source_target_pairs={{0,64},{32,96},{64,0},{96,32},{128,192},{160,224},{192,128},{224,1... | collective-permute-start | bytes 3145736 | tf_op jit(solution)/shard_map/ppermute | solution.py:27
  88.7 2.8 %collective-permute-start.11 = (bf16[1024,512]{1,0:T(8,128)(2,1)S(1)}, bf16[1024,512]{1,0:T(8,128)(2,1)}, u32[]{:S(2)}, u32[]{:S(2)}) collective-permute-start(bf16[1024,512]{1,0:T(8,128)(2,1)S(1)} %pad_maximum_fusion.1), channel_id=1, source_target_pairs={{0,96},{32,0},{64,32},{96,64},{128,224},{160,128},{192,160},{224,1... | collective-permute-start | bytes 3145736 | tf_op jit(solution)/shard_map/ppermute | solution.py:27
  91.5 0.0 collective-permute-done.5
  91.5 2.5 %collective-permute-start.10 = (bf16[1024,512]{1,0:T(8,128)(2,1)S(1)}, bf16[1024,512]{1,0:T(8,128)(2,1)}, u32[]{:S(2)}, u32[]{:S(2)}) collective-permute-start(bf16[1024,512]{1,0:T(8,128)(2,1)S(1)} %pad_maximum_fusion.1), channel_id=1, source_target_pairs={{0,32},{32,64},{64,96},{96,0},{128,160},{160,192},{192,224},{224,1... | collective-permute-start | bytes 3145736 | tf_op jit(solution)/shard_map/ppermute | solution.py:27
  94.2 0.1 stack.67.places
  94.3 11.9 %collective-permute-done.4 = bf16[1024,512]{1,0:T(8,128)(2,1)} collective-permute-done((bf16[1024,512]{1,0:T(8,128)(2,1)S(1)}, bf16[1024,512]{1,0:T(8,128)(2,1)}, u32[]{:S(2)}, u32[]{:S(2)}) %collective-permute-start.4) | collective-permute-done | bytes 1048608 | tf_op jit(solution)/shard_map/ppermute | solution.py:34
  106.2 3.1 %collective-permute-done.3 = bf16[1024,512]{1,0:T(8,128)(2,1)} collective-permute-done((bf16[1024,512]{1,0:T(8,128)(2,1)S(1)}, bf16[1024,512]{1,0:T(8,128)(2,1)}, u32[]{:S(2)}, u32[]{:S(2)}) %collective-permute-start.3) | collective-permute-done | bytes 1048608 | tf_op jit(solution)/shard_map/ppermute | solution.py:34
  109.4 4.6 %collective-permute-done.12 = bf16[1024,512]{1,0:T(8,128)(2,1)} collective-permute-done((bf16[1024,512]{1,0:T(8,128)(2,1)S(1)}, bf16[1024,512]{1,0:T(8,128)(2,1)}, u32[]{:S(2)}, u32[]{:S(2)}) %collective-permute-start.12) | collective-permute-done | bytes 1048608 | tf_op jit(solution)/shard_map/ppermute | solution.py:27
  114.0 20.0 %collective-permute-done.11 = bf16[1024,512]{1,0:T(8,128)(2,1)} collective-permute-done((bf16[1024,512]{1,0:T(8,128)(2,1)S(1)}, bf16[1024,512]{1,0:T(8,128)(2,1)}, u32[]{:S(2)}, u32[]{:S(2)}) %collective-permute-start.11) | collective-permute-done | bytes 1048608 | tf_op jit(solution)/shard_map/ppermute | solution.py:27
  134.0 3.6 %collective-permute-done.10 = bf16[1024,512]{1,0:T(8,128)(2,1)} collective-permute-done((bf16[1024,512]{1,0:T(8,128)(2,1)S(1)}, bf16[1024,512]{1,0:T(8,128)(2,1)}, u32[]{:S(2)}, u32[]{:S(2)}) %collective-permute-start.10) | collective-permute-done | bytes 1048608 | tf_op jit(solution)/shard_map/ppermute | solution.py:27
  137.6 8.1 %project.1 = bf16[512,512]{1,0:T(8,128)(2,1)} custom-call(s32[16]{0:T(128)S(1)} %stack.67.places, bf16[4,256,512]{2,1,0:T(8,128)(2,1)S(1)} %bitcast.28, bf16[4,256,512]{2,1,0:T(8,128)(2,1)} %bitcast.20.refs_1_, bf16[4,256,512]{2,1,0:T(8,128)(2,1)} %bitcast.21.refs_2_, bf16[4,256,512]{2,1,0:T(8,128)(2,1)S(1)} %bitcast.30, bf16[4,256,512]{2,1,0:T(8,128)(2,1)S(1)} %bitcast.29, ...), custom_call_target="tpu_custom_call" | custom-call | flops 4294967296 | bytes 17825792 | tf_op jit(solution)/shard_map/project/pallas_call | solution.py:227
  (12 shorter events, 0.0 us)
Async XLA Ops:
  6.5 131.1 %all-gather.2.cloned.1.call-start = ((), (), s32[]{:S(2)}) async-start(), calls=%async_computation | async-start | bytes 8650752 | tf_op jit(solution)/shard_map/all_gather | solution.py:259
  7.3 1.0 copy-start
  8.3 1.0 copy-start.1
  9.3 1.0 copy-start.2
  10.4 0.9 copy-start.3
  11.3 0.8 copy-start.4
  12.1 0.7 copy-start.5
  12.8 0.7 copy-start.6
  13.5 0.7 copy-start.7
  14.2 29.4 %slice-start = ((bf16[512,512]{1,0:T(8,128)(2,1)}), bf16[144,512]{1,0:T(8,128)(2,1)S(1)}, s32[]{:S(2)}) async-start(bf16[512,512]{1,0:T(8,128)(2,1)} %refs_3_.1), calls=%async_computation.1 | async-start | bytes 294912 | tf_op jit(solution)/shard_map/slice | solution.py:262
  14.2 29.4 %slice-start.1 = ((bf16[512,512]{1,0:T(8,128)(2,1)}), bf16[144,512]{1,0:T(8,128)(2,1)S(1)}, s32[]{:S(2)}) async-start(bf16[512,512]{1,0:T(8,128)(2,1)} %refs_4_.3), calls=%async_computation.2 | async-start | bytes 294912 | tf_op jit(solution)/shard_map/slice | solution.py:262
  14.2 29.4 %slice-start.2 = ((bf16[512,512]{1,0:T(8,128)(2,1)}), bf16[16,512]{1,0:T(8,128)(2,1)S(1)}, s32[]{:S(2)}) async-start(bf16[512,512]{1,0:T(8,128)(2,1)} %refs_2_.3), calls=%async_computation.3 | async-start | bytes 32768 | tf_op jit(solution)/shard_map/slice | solution.py:262
  21.4 10.6 %collective-permute-start.2 = (bf16[256,512]{1,0:T(8,128)(2,1)S(1)}, bf16[256,512]{1,0:T(8,128)(2,1)S(1)}, u32[]{:S(2)}, u32[]{:S(2)}) collective-permute-start(bf16[256,512]{1,0:T(8,128)(2,1)S(1)} %gate_late.1), channel_id=1, source_target_pairs={{0,64},{32,96},{64,0},{96,32},{128,192},{160,224},{192,128},{224,1... | collective-permute-start | bytes 786440 | tf_op jit(solution)/shard_map/ppermute | solution.py:27
  26.1 11.7 %collective-permute-start.1 = (bf16[256,512]{1,0:T(8,128)(2,1)S(1)}, bf16[256,512]{1,0:T(8,128)(2,1)S(1)}, u32[]{:S(2)}, u32[]{:S(2)}) collective-permute-start(bf16[256,512]{1,0:T(8,128)(2,1)S(1)} %gate_late.1), channel_id=1, source_target_pairs={{0,96},{32,0},{64,32},{96,64},{128,224},{160,128},{192,160},{224,1... | collective-permute-start | bytes 786440 | tf_op jit(solution)/shard_map/ppermute | solution.py:27
  28.8 9.8 %collective-permute-start = (bf16[256,512]{1,0:T(8,128)(2,1)S(1)}, bf16[256,512]{1,0:T(8,128)(2,1)S(1)}, u32[]{:S(2)}, u32[]{:S(2)}) collective-permute-start(bf16[256,512]{1,0:T(8,128)(2,1)S(1)} %gate_late.1), channel_id=1, source_target_pairs={{0,32},{32,64},{64,96},{96,0},{128,160},{160,192},{192,224},{224,1... | collective-permute-start | bytes 786440 | tf_op jit(solution)/shard_map/ppermute | solution.py:27
  38.7 52.8 %collective-permute-start.5 = (bf16[1024,512]{1,0:T(8,128)(2,1)S(1)}, bf16[1024,512]{1,0:T(8,128)(2,1)S(1)}, u32[]{:S(2)}, u32[]{:S(2)}) collective-permute-start(bf16[1024,512]{1,0:T(8,128)(2,1)S(1)} %pad_maximum_fusion), channel_id=1, source_target_pairs={{0,256},{32,288},{64,320},{96,352},{128,384},{160,416},{192,448},{... | collective-permute-start | bytes 3145736 | tf_op jit(solution)/shard_map/ppermute | solution.py:34
  43.6 17.9 %collective-permute-start.6 = (bf16[320,512]{1,0:T(8,128)(2,1)S(1)}, bf16[320,512]{1,0:T(8,128)(2,1)S(1)}, u32[]{:S(2)}, u32[]{:S(2)}) collective-permute-start(bf16[320,512]{1,0:T(8,128)(2,1)S(1)} %pad_maximum_fusion.2), channel_id=1, source_target_pairs={{0,1},{1,2},{2,3},{3,4},{4,5},{5,6},{6,7},{7,8},{8,9},{9,10},{10,1... | collective-permute-start | bytes 983048 | tf_op jit(solution)/shard_map/ppermute | solution.py:265
  68.8 13.2 %collective-permute-start.9 = (bf16[256,512]{1,0:T(8,128)(2,1)S(1)}, bf16[256,512]{1,0:T(8,128)(2,1)S(1)}, u32[]{:S(2)}, u32[]{:S(2)}) collective-permute-start(bf16[256,512]{1,0:T(8,128)(2,1)S(1)} %gate_early.1), channel_id=1, source_target_pairs={{0,256},{32,288},{64,320},{96,352},{128,384},{160,416},{192,448},{... | collective-permute-start | bytes 786440 | tf_op jit(solution)/shard_map/ppermute | solution.py:34
  70.7 13.3 %collective-permute-start.8 = (bf16[256,512]{1,0:T(8,128)(2,1)S(1)}, bf16[256,512]{1,0:T(8,128)(2,1)S(1)}, u32[]{:S(2)}, u32[]{:S(2)}) collective-permute-start(bf16[256,512]{1,0:T(8,128)(2,1)S(1)} %gate_early.1), channel_id=1, source_target_pairs={{0,384},{32,416},{64,448},{96,480},{128,0},{160,32},{192,64},{224,... | collective-permute-start | bytes 786440 | tf_op jit(solution)/shard_map/ppermute | solution.py:34
  75.5 11.0 %collective-permute-start.7 = (bf16[256,512]{1,0:T(8,128)(2,1)S(1)}, bf16[256,512]{1,0:T(8,128)(2,1)S(1)}, u32[]{:S(2)}, u32[]{:S(2)}) collective-permute-start(bf16[256,512]{1,0:T(8,128)(2,1)S(1)} %gate_early.1), channel_id=1, source_target_pairs={{0,128},{32,160},{64,192},{96,224},{128,256},{160,288},{192,320},{... | collective-permute-start | bytes 786440 | tf_op jit(solution)/shard_map/ppermute | solution.py:34
  77.4 28.8 %collective-permute-start.4 = (bf16[1024,512]{1,0:T(8,128)(2,1)S(1)}, bf16[1024,512]{1,0:T(8,128)(2,1)}, u32[]{:S(2)}, u32[]{:S(2)}) collective-permute-start(bf16[1024,512]{1,0:T(8,128)(2,1)S(1)} %pad_maximum_fusion), channel_id=1, source_target_pairs={{0,384},{32,416},{64,448},{96,480},{128,0},{160,32},{192,64},{224,... | collective-permute-start | bytes 3145736 | tf_op jit(solution)/shard_map/ppermute | solution.py:34
  82.0 27.3 %collective-permute-start.3 = (bf16[1024,512]{1,0:T(8,128)(2,1)S(1)}, bf16[1024,512]{1,0:T(8,128)(2,1)}, u32[]{:S(2)}, u32[]{:S(2)}) collective-permute-start(bf16[1024,512]{1,0:T(8,128)(2,1)S(1)} %pad_maximum_fusion), channel_id=1, source_target_pairs={{0,128},{32,160},{64,192},{96,224},{128,256},{160,288},{192,320},{... | collective-permute-start | bytes 3145736 | tf_op jit(solution)/shard_map/ppermute | solution.py:34
  86.6 27.4 %collective-permute-start.12 = (bf16[1024,512]{1,0:T(8,128)(2,1)S(1)}, bf16[1024,512]{1,0:T(8,128)(2,1)}, u32[]{:S(2)}, u32[]{:S(2)}) collective-permute-start(bf16[1024,512]{1,0:T(8,128)(2,1)S(1)} %pad_maximum_fusion.1), channel_id=1, source_target_pairs={{0,64},{32,96},{64,0},{96,32},{128,192},{160,224},{192,128},{224,1... | collective-permute-start | bytes 3145736 | tf_op jit(solution)/shard_map/ppermute | solution.py:27
  88.7 45.3 %collective-permute-start.11 = (bf16[1024,512]{1,0:T(8,128)(2,1)S(1)}, bf16[1024,512]{1,0:T(8,128)(2,1)}, u32[]{:S(2)}, u32[]{:S(2)}) collective-permute-start(bf16[1024,512]{1,0:T(8,128)(2,1)S(1)} %pad_maximum_fusion.1), channel_id=1, source_target_pairs={{0,96},{32,0},{64,32},{96,64},{128,224},{160,128},{192,160},{224,1... | collective-permute-start | bytes 3145736 | tf_op jit(solution)/shard_map/ppermute | solution.py:27
  91.5 46.1 %collective-permute-start.10 = (bf16[1024,512]{1,0:T(8,128)(2,1)S(1)}, bf16[1024,512]{1,0:T(8,128)(2,1)}, u32[]{:S(2)}, u32[]{:S(2)}) collective-permute-start(bf16[1024,512]{1,0:T(8,128)(2,1)S(1)} %pad_maximum_fusion.1), channel_id=1, source_target_pairs={{0,32},{32,64},{64,96},{96,0},{128,160},{160,192},{192,224},{224,1... | collective-permute-start | bytes 3145736 | tf_op jit(solution)/shard_map/ppermute | solution.py:27
Sparse Core Ops, SparseCore 0:
  9.5 79.0 all-gather.1

commit v2 on v1

--- a/solution.py
+++ b/solution.py
@@ -13,6 +13,7 @@
 HALO = 144
 HALF = 256
 WINDOW = HALO + HALF
+PACK = 2 * HALO + 16 + 16
 LEAD = 16
 PRODUCTS = WINDOW - LEAD
 TILE = 64
@@ -20,18 +21,26 @@
 OFFSETS = (0, -1, 1, 2)
 
 
-def along_x(value, by):
-    pairs = [
-        (y * SIDE + x, y * SIDE + (x + by) % SIDE) for y in range(SIDE) for x in range(SIDE)
-    ]
-    return lax.ppermute(value, "chan", pairs)
-
-
-def along_y(value, by):
-    pairs = [
-        (y * SIDE + x, (y + by) % SIDE * SIDE + x) for y in range(SIDE) for x in range(SIDE)
-    ]
-    return lax.ppermute(value, "chan", pairs)
+def first_way(value, by):
+    return lax.ppermute(value, ("chan", "stretch"), moves(by, 0))
+
+
+def second_way(value, by):
+    return lax.ppermute(value, ("chan", "stretch"), moves(by, 1))
+
+
+def moves(by, way):
+    stretch = lax.axis_size("stretch")
+    pairs = []
+    for y in range(SIDE):
+        for x in range(SIDE):
+            for place in range(stretch):
+                if place % 2 == way:
+                    to = y * SIDE + (x + by) % SIDE
+                else:
+                    to = (y + by) % SIDE * SIDE + x
+                pairs.append(((y * SIDE + x) * stretch + place, to * stretch + place))
+    return pairs
 
 
 def id_column(row):
@@ -141,7 +150,42 @@
         ).astype(jnp.bfloat16)
 
 
-def gate(late, halo, query, key, value, ids, short_taps, medium_taps, decay, skip):
+def pack_kernel(key, value, query, ids_ref, out, sem):
+    copies = [
+        pltpu.make_async_copy(key.at[512 - HALO : 512], out.at[0:HALO], sem.at[0]),
+        pltpu.make_async_copy(value.at[512 - HALO : 512], out.at[HALO : 2 * HALO], sem.at[1]),
+        pltpu.make_async_copy(
+            query.at[512 - 16 : 512], out.at[2 * HALO : 2 * HALO + 16], sem.at[2]
+        ),
+    ]
+    for copy in copies:
+        copy.start()
+    for i in range(4):
+        row = ids_ref[i : i + 1, :].astype(jnp.float32)
+        out[2 * HALO + 16 : PACK, LANES * i : LANES * (i + 1)] = jnp.broadcast_to(
+            row, (16, LANES)
+        ).astype(jnp.bfloat16)
+    for copy in copies:
+        copy.wait()
+
+
+def pack_tail(key, value, query, ids):
+    hbm = pl.BlockSpec(memory_space=pl.ANY)
+    channels = key.shape[1]
+    return pl.pallas_call(
+        pack_kernel,
+        out_shape=jax.ShapeDtypeStruct((PACK, channels), jnp.bfloat16),
+        in_specs=[hbm, hbm, hbm, pl.BlockSpec(memory_space=pltpu.VMEM)],
+        out_specs=pl.BlockSpec(memory_space=pltpu.VMEM),
+        scratch_shapes=[pltpu.SemaphoreType.DMA((3,))],
+        compiler_params=pltpu.CompilerParams(vmem_limit_bytes=60 << 20),
+        cost_estimate=pl.CostEstimate(flops=0, bytes_accessed=700000, transcendentals=0),
+        name="pack_tail",
+    )(key, value, query, ids)
+
+
+def gate(halo, query, key, value, ids, short_taps, medium_taps, decay, skip):
+    late = halo is None
     channels = query.shape[1]
     whole = lambda rows: pl.BlockSpec((rows, LANES), lambda i: (0, i))
     specs = [whole(512)] * 3 + [
@@ -154,7 +198,7 @@
     args = [query, key, value, ids, short_taps, medium_taps, decay, skip]
     if not late:
         ids_block = (2 * HALO + 16) // 16
-        specs = [whole(halo.shape[0]), pl.BlockSpec((16, channels), lambda i: (ids_block, 0))] + specs
+        specs = [whole(PACK), pl.BlockSpec((16, channels), lambda i: (ids_block, 0))] + specs
         args = [halo, halo] + args
     f32 = lambda rows: pltpu.VMEM((rows, LANES), jnp.float32)
     return pl.pallas_call(
@@ -162,7 +206,7 @@
         grid=(channels // LANES,),
         out_shape=jax.ShapeDtypeStruct((HALF, channels), jnp.bfloat16),
         in_specs=specs,
-        out_specs=pl.BlockSpec((HALF, LANES), lambda i: (0, i)),
+        out_specs=whole(HALF),
         scratch_shapes=[
             f32(HALF + 16),
             f32(WINDOW),
@@ -173,7 +217,7 @@
             f32(MEDIUM),
             pltpu.SMEM((2 * HALF // TILE,), jnp.int32),
         ],
-        compiler_params=pltpu.CompilerParams(vmem_limit_bytes=24 << 20),
+        compiler_params=pltpu.CompilerParams(vmem_limit_bytes=60 << 20),
         cost_estimate=pl.CostEstimate(
             flops=2 * MEDIUM * HALF * channels * 4, bytes_accessed=2 << 20, transcendentals=65536
         ),
@@ -182,66 +226,68 @@
 
 
 def project_kernel(places, *refs):
-    panels = refs[:8]
-    weight, out_ref, blocks, weights, total, block_sem, weight_sem = refs[8:]
+    lates, earlies = refs[:SIDE], refs[SIDE : 2 * SIDE]
+    weight, out_ref, blocks, weights, total, block_sem, weight_sem = refs[2 * SIDE :]
+    slots = SIDE * SIDE
     copies = []
-    for iy in range(SIDE):
-        for ix in range(SIDE):
-            at = SIDE * iy + ix
-            mine = []
-            mine.append(
-                pltpu.make_async_copy(weight.at[places[at]], weights.at[at], weight_sem.at[at])
+    for at in range(slots):
+        group, member = at // SIDE, at % SIDE
+        copies.append(
+            (
+                pltpu.make_async_copy(
+                    earlies[group].at[member], blocks.at[at, 0:HALF], block_sem.at[2 * at]
+                ),
+                pltpu.make_async_copy(
+                    lates[group].at[member], blocks.at[at, HALF:], block_sem.at[2 * at + 1]
+                ),
+                pltpu.make_async_copy(weight.at[places[at]], weights.at[at], weight_sem.at[at]),
             )
-            mine.append(
-                pltpu.make_async_copy(
-                    panels[iy].at[ix], blocks.at[at, pl.ds(HALF, HALF)], block_sem.at[2 * at]
-                )
-            )
-            mine.append(
-                pltpu.make_async_copy(
-                    panels[4 + ix].at[iy], blocks.at[at, pl.ds(0, HALF)], block_sem.at[2 * at + 1]
-                )
-            )
-            for copy in mine:
-                copy.start()
-            copies.append(mine)
-    total[...] = jnp.zeros_like(total)
-    for at in range(SIDE * SIDE):
+        )
+        for copy in copies[at]:
+            copy.start()
+    for at in range(slots):
         for copy in copies[at]:
             copy.wait()
-        total[...] += jnp.dot(blocks[at], weights[at], preferred_element_type=jnp.float32)
-    out_ref[...] = total[...].astype(jnp.bfloat16)
-
-
-def project(late, early, weight):
-    me = lax.axis_index("chan")
-    y, x = me // SIDE, me % SIDE
-    places = jnp.stack(
-        [(y + oy) % SIDE * SIDE + (x + ox) % SIDE for oy in OFFSETS for ox in OFFSETS]
-    ).astype(jnp.int32)
+        part = jnp.dot(blocks[at], weights[at], preferred_element_type=jnp.float32)
+        if at == 0:
+            total[...] = part
+        elif at < slots - 1:
+            total[...] += part
+        else:
+            out_ref[...] = (total[...] + part).astype(jnp.bfloat16)
+
+
+def project(lates, earlies, weight):
+    chan = lax.axis_index("chan")
+    y, x = chan // SIDE, chan % SIDE
+    core = lax.axis_index("stretch") % 2
+    outer = jnp.repeat(jnp.array(OFFSETS, jnp.int32), SIDE)
+    inner = jnp.tile(jnp.array(OFFSETS, jnp.int32), SIDE)
+    oy = jnp.where(core == 0, outer, inner)
+    ox = jnp.where(core == 0, inner, outer)
+    places = (y + oy + SIDE) % SIDE * SIDE + (x + ox + SIDE) % SIDE
+    slots = SIDE * SIDE
     columns = weight.shape[1]
-    slots = SIDE * SIDE
-    panels = [p.reshape(SIDE, HALF, -1) for p in (*late, *early)]
-    depth = panels[0].shape[-1]
+    tokens, depth = 2 * HALF, lates[0].shape[2]
     hbm = pl.BlockSpec(memory_space=pl.ANY)
     return pl.pallas_call(
         project_kernel,
-        out_shape=jax.ShapeDtypeStruct((2 * HALF, columns), jnp.bfloat16),
+        out_shape=jax.ShapeDtypeStruct((tokens, columns), jnp.bfloat16),
         in_specs=[pl.BlockSpec(memory_space=pltpu.SMEM)] + [hbm] * 9,
         out_specs=pl.BlockSpec(memory_space=pltpu.VMEM),
         scratch_shapes=[
-            pltpu.VMEM((slots, 2 * HALF, depth), jnp.bfloat16),
+            pltpu.VMEM((slots, tokens, depth), jnp.bfloat16),
             pltpu.VMEM((slots, depth, columns), jnp.bfloat16),
-            pltpu.VMEM((2 * HALF, columns), jnp.float32),
+            pltpu.VMEM((tokens, columns), jnp.float32),
             pltpu.SemaphoreType.DMA((2 * slots,)),
             pltpu.SemaphoreType.DMA((slots,)),
         ],
-        compiler_params=pltpu.CompilerParams(vmem_limit_bytes=40 << 20),
+        compiler_params=pltpu.CompilerParams(vmem_limit_bytes=60 << 20),
         cost_estimate=pl.CostEstimate(
-            flops=2 * 2 * HALF * slots * depth * columns, bytes_accessed=17 << 20, transcendentals=0
+            flops=2 * tokens * slots * depth * columns, bytes_accessed=17 << 20, transcendentals=0
         ),
         name="project",
-    )(places, *panels, weight.reshape(slots, depth, columns))
+    )(places.astype(jnp.int32), *lates, *earlies, weight.reshape(slots, depth, columns))
 
 
 def body(
@@ -255,14 +301,7 @@
     skip_gain,
     out_weight,
 ):
-    tokens, channels = query_in.shape
     weight = lax.all_gather(out_weight, "stretch", axis=0, tiled=True)
-    id_rows = jnp.broadcast_to(contig_ids.astype(jnp.bfloat16)[None, :], (16, tokens))
-    pack = jnp.concatenate(
-        [key_in[tokens - HALO :], value_in[tokens - HALO :], query_in[tokens - 16 :], id_rows]
-    )
-    devices = lax.axis_size("stretch")
-    halo = lax.ppermute(pack, "stretch", [(i, i + 1) for i in range(devices - 1)])
     rest = (
         query_in,
         key_in,
@@ -273,13 +312,18 @@
         decay_rate[None, :],
         skip_gain[None, :],
     )
-    late = gate(True, None, *rest)
-    late_x = jnp.concatenate([late] + [along_x(late, -by) for by in OFFSETS[1:]])
-    early = gate(False, halo, *rest)
-    early_y = jnp.concatenate([early] + [along_y(early, -by) for by in OFFSETS[1:]])
-    late_all = [late_x] + [along_y(late_x, -by) for by in OFFSETS[1:]]
-    early_all = [early_y] + [along_x(early_y, -by) for by in OFFSETS[1:]]
-    return project(late_all, early_all, weight)
+    devices = lax.axis_size("stretch")
+    pack = pack_tail(key_in, value_in, query_in, rest[3])
+    halo = lax.ppermute(pack, "stretch", [(i, i + 1) for i in range(devices - 1)])
+    late = gate(None, *rest)
+    late_line = [late] + [first_way(late, -by) for by in OFFSETS[1:]]
+    early = gate(halo, *rest)
+    late_line, early = lax.optimization_barrier((late_line, early))
+    early_line = [early] + [first_way(early, -by) for by in OFFSETS[1:]]
+    late_line, early_line = jnp.stack(late_line), jnp.stack(early_line)
+    late_panels = [late_line] + [second_way(late_line, -by) for by in OFFSETS[1:]]
+    early_panels = [early_line] + [second_way(early_line, -by) for by in OFFSETS[1:]]
+    return project(late_panels, early_panels, weight)
 
 
 def solution(mesh):

time: 153 us -> 119 us (0.78)
  the two profiles are of different devices: /device:TPU:225 before, /device:TPU:1 now
where the time goes in v2:
time: 119 us; the launch traced here: 117 us
  starting transfers between devices  43.8 us (37%)
  Pallas kernels  29.2 us (25%)
  waiting for transfers between devices  27.1 us (23%)
  between operations  13.6 us (11%)
  other arithmetic  2.83 us (2%)
    ppermute x6, starting transfers between devices, second_way(): return lax.ppermute(value, ('chan', 'stretch'), moves(by, 1))  20.2 us
    ppermute x6, waiting for transfers between devices, second_way(): return lax.ppermute(value, ('chan', 'stretch'), moves(by, 1))  19.7 us
    ppermute x6, starting transfers between devices, first_way(): return lax.ppermute(value, ('chan', 'stretch'), moves(by, 0))  18.6 us
    pallas_call x2, Pallas kernels, gate(): pl.pallas_call(functools.partial(filter_kernel, late), grid=(channels //...  17.3 us
    pallas_call x1, Pallas kernels, project(): pl.pallas_call(project_kernel, out_shape=jax.ShapeDtypeStruct((tokens, co...  9.51 us
    ppermute x6, waiting for transfers between devices, first_way(): return lax.ppermute(value, ('chan', 'stretch'), moves(by, 0))  6.71 us
    ppermute x1, starting transfers between devices, body(): lax.ppermute(pack, 'stretch', [(i, i + 1) for i in range(devices - 1)])  4.94 us
    pallas_call x1, Pallas kernels, pack_tail(): pl.pallas_call(pack_kernel, out_shape=jax.ShapeDtypeStruct((PACK, channel...  2.42 us
  transfers between devices with their start and end apart: 14, of which 6 were waited for; matrix products, arithmetic and copies ran while one was open for 3% of the time, Pallas kernels for 17%

profile of v2, /device:TPU:1, one launch (start us, length us, event | category | flops | bytes accessed | tf_op | source)
XLA Modules:
  0.0 117.5 jit_solution(15466333775338117883)
XLA Ops:
  6.5 0.0 all-gather.2.cloned.1.call-start
  6.5 0.7 all-gather.2.cloned.1.call-update
  7.3 2.4 %pack_tail.1 = bf16[320,512]{1,0:T(8,128)(2,1)} custom-call(bf16[512,512]{1,0:T(8,128)(2,1)} %refs_3_.1, bf16[512,512]{1,0:T(8,128)(2,1)} %refs_4_.3, bf16[512,512]{1,0:T(8,128)(2,1)} %refs_2_.3, s32[4,128]{1,0:T(4,128)} %bitcast.21), custom_call_target="tpu_custom_call" | custom-call | bytes 700000 | tf_op jit(solution)/shard_map/pack_tail/pallas_call | solution.py:175
  9.7 4.9 %collective-permute-start.3 = (bf16[320,512]{1,0:T(8,128)(2,1)}, bf16[320,512]{1,0:T(8,128)(2,1)S(1)}, u32[]{:S(2)}, u32[]{:S(2)}) collective-permute-start(bf16[320,512]{1,0:T(8,128)(2,1)} %pack_tail.1), channel_id=1, source_target_pairs={{0,1},{1,2},{2,3},{3,4},{4,5},{5,6},{6,7},{7,8},{8,9},{9,10},{10,1... | collective-permute-start | bytes 983048 | tf_op jit(solution)/shard_map/ppermute | solution.py:317
  14.6 8.6 %gate_late.1 = bf16[256,512]{1,0:T(8,128)(2,1)} custom-call(bf16[512,512]{1,0:T(8,128)(2,1)} %refs_2_.3, bf16[512,512]{1,0:T(8,128)(2,1)} %refs_3_.1, bf16[512,512]{1,0:T(8,128)(2,1)} %refs_4_.3, s32[4,128]{1,0:T(4,128)} %bitcast.22, f32[3,7,512]{2,1,0:T(8,128)} %refs_6_.1, f32[128,512]{1,0:T(8,128)} %refs_7_.1, f32[1,512]{1,0:T(1,128)} %bitcast.24, ...), custom_call_target="tpu_custom_call" | custom-call | flops 134217728 | bytes 2097152 | tf_op jit(solution)/shard_map/gate_late/pallas_call | solution.py:204
  23.2 4.8 %collective-permute-start.2 = (bf16[256,512]{1,0:T(8,128)(2,1)}, bf16[256,512]{1,0:T(8,128)(2,1)S(1)}, u32[]{:S(2)}, u32[]{:S(2)}) collective-permute-start(bf16[256,512]{1,0:T(8,128)(2,1)} %gate_late.1), channel_id=1, source_target_pairs={{0,64},{1,257},{2,66},{3,259},{4,68},{5,261},{6,70},{7,263},{8,72}... | collective-permute-start | bytes 786440 | tf_op jit(solution)/shard_map/ppermute | solution.py:25
  28.0 2.7 %collective-permute-start.1 = (bf16[256,512]{1,0:T(8,128)(2,1)}, bf16[256,512]{1,0:T(8,128)(2,1)S(1)}, u32[]{:S(2)}, u32[]{:S(2)}) collective-permute-start(bf16[256,512]{1,0:T(8,128)(2,1)} %gate_late.1), channel_id=1, source_target_pairs={{0,96},{1,385},{2,98},{3,387},{4,100},{5,389},{6,102},{7,391},{8,1... | collective-permute-start | bytes 786440 | tf_op jit(solution)/shard_map/ppermute | solution.py:25
  30.7 2.6 %collective-permute-start = (bf16[256,512]{1,0:T(8,128)(2,1)}, bf16[256,512]{1,0:T(8,128)(2,1)S(1)}, u32[]{:S(2)}, u32[]{:S(2)}) collective-permute-start(bf16[256,512]{1,0:T(8,128)(2,1)} %gate_late.1), channel_id=1, source_target_pairs={{0,32},{1,129},{2,34},{3,131},{4,36},{5,133},{6,38},{7,135},{8,40}... | collective-permute-start | bytes 786440 | tf_op jit(solution)/shard_map/ppermute | solution.py:25
  33.3 0.0 collective-permute-done.3.refs_0_.refs_1_
  33.4 0.0 copy-start.2
  33.4 0.7 copy-done.2
  34.1 8.7 %gate_early.1 = bf16[256,512]{1,0:T(8,128)(2,1)} custom-call(bf16[320,512]{1,0:T(8,128)(2,1)} %copy-done.2, bf16[320,512]{1,0:T(8,128)(2,1)} %copy-done.2, bf16[512,512]{1,0:T(8,128)(2,1)} %refs_2_.3, bf16[512,512]{1,0:T(8,128)(2,1)} %refs_3_.1, bf16[512,512]{1,0:T(8,128)(2,1)} %refs_4_.3, s32[4,128]{1,0:T(4,128)} %bitcast.23, f32[3,7,512]{2,1,0:T(8,128)} %refs_6_.1, ...), custom_call_target="tpu_custom_call" | custom-call | flops 134217728 | bytes 2097152 | tf_op jit(solution)/shard_map/gate_early/pallas_call | solution.py:204
  42.8 0.0 collective-permute-done.2
  42.8 0.0 collective-permute-done.1
  42.8 0.0 collective-permute-done
  42.8 1.1 pad_maximum_fusion.refs_0_
  43.9 0.0 copy-start
  43.9 4.7 %collective-permute-start.6 = (bf16[4,256,512]{2,1,0:T(8,128)(2,1)S(1)}, bf16[4,256,512]{2,1,0:T(8,128)(2,1)S(1)}, u32[]{:S(2)}, u32[]{:S(2)}) collective-permute-start(bf16[4,256,512]{2,1,0:T(8,128)(2,1)S(1)} %pad_maximum_fusion.refs_0_), channel_id=1, source_target_pairs={{0,256},{1,65},{2,258},{3,67},{4,260},{5,69},{6,262},{7,71},{8,264... | collective-permute-start | bytes 3145736 | tf_op jit(solution)/shard_map/ppermute | solution.py:29
  48.6 2.6 %collective-permute-start.9 = (bf16[256,512]{1,0:T(8,128)(2,1)}, bf16[256,512]{1,0:T(8,128)(2,1)S(1)}, u32[]{:S(2)}, u32[]{:S(2)}) collective-permute-start(bf16[256,512]{1,0:T(8,128)(2,1)} %gate_early.1), channel_id=1, source_target_pairs={{0,64},{1,257},{2,66},{3,259},{4,68},{5,261},{6,70},{7,263},{8,72}... | collective-permute-start | bytes 786440 | tf_op jit(solution)/shard_map/ppermute | solution.py:25
  51.2 4.0 %collective-permute-start.8 = (bf16[256,512]{1,0:T(8,128)(2,1)}, bf16[256,512]{1,0:T(8,128)(2,1)S(1)}, u32[]{:S(2)}, u32[]{:S(2)}) collective-permute-start(bf16[256,512]{1,0:T(8,128)(2,1)} %gate_early.1), channel_id=1, source_target_pairs={{0,96},{1,385},{2,98},{3,387},{4,100},{5,389},{6,102},{7,391},{8,1... | collective-permute-start | bytes 786440 | tf_op jit(solution)/shard_map/ppermute | solution.py:25
  55.2 1.9 %collective-permute-start.7 = (bf16[256,512]{1,0:T(8,128)(2,1)}, bf16[256,512]{1,0:T(8,128)(2,1)S(1)}, u32[]{:S(2)}, u32[]{:S(2)}) collective-permute-start(bf16[256,512]{1,0:T(8,128)(2,1)} %gate_early.1), channel_id=1, source_target_pairs={{0,32},{1,129},{2,34},{3,131},{4,36},{5,133},{6,38},{7,135},{8,40}... | collective-permute-start | bytes 786440 | tf_op jit(solution)/shard_map/ppermute | solution.py:25
  57.1 2.8 %collective-permute-start.5 = (bf16[4,256,512]{2,1,0:T(8,128)(2,1)S(1)}, bf16[4,256,512]{2,1,0:T(8,128)(2,1)}, u32[]{:S(2)}, u32[]{:S(2)}) collective-permute-start(bf16[4,256,512]{2,1,0:T(8,128)(2,1)S(1)} %pad_maximum_fusion.refs_0_), channel_id=1, source_target_pairs={{0,384},{1,97},{2,386},{3,99},{4,388},{5,101},{6,390},{7,103},{8,3... | collective-permute-start | bytes 3145736 | tf_op jit(solution)/shard_map/ppermute | solution.py:29
  59.9 0.7 collective-permute-done.9
  60.6 2.2 %collective-permute-start.4 = (bf16[4,256,512]{2,1,0:T(8,128)(2,1)S(1)}, bf16[4,256,512]{2,1,0:T(8,128)(2,1)}, u32[]{:S(2)}, u32[]{:S(2)}) collective-permute-start(bf16[4,256,512]{2,1,0:T(8,128)(2,1)S(1)} %pad_maximum_fusion.refs_0_), channel_id=1, source_target_pairs={{0,128},{1,33},{2,130},{3,35},{4,132},{5,37},{6,134},{7,39},{8,136... | collective-permute-start | bytes 3145736 | tf_op jit(solution)/shard_map/ppermute | solution.py:29
  62.8 4.9 %collective-permute-done.8 = bf16[256,512]{1,0:T(8,128)(2,1)S(1)} collective-permute-done((bf16[256,512]{1,0:T(8,128)(2,1)}, bf16[256,512]{1,0:T(8,128)(2,1)S(1)}, u32[]{:S(2)}, u32[]{:S(2)}) %collective-permute-start.8) | collective-permute-done | bytes 262176 | tf_op jit(solution)/shard_map/ppermute | solution.py:25
  67.7 1.1 collective-permute-done.7
  68.8 1.1 pad_maximum_fusion.1.refs_4_
  69.9 0.0 copy-start.1
  69.9 5.3 %collective-permute-start.12 = (bf16[4,256,512]{2,1,0:T(8,128)(2,1)S(1)}, bf16[4,256,512]{2,1,0:T(8,128)(2,1)}, u32[]{:S(2)}, u32[]{:S(2)}) collective-permute-start(bf16[4,256,512]{2,1,0:T(8,128)(2,1)S(1)} %pad_maximum_fusion.1.refs_4_), channel_id=1, source_target_pairs={{0,256},{1,65},{2,258},{3,67},{4,260},{5,69},{6,262},{7,71},{8,264... | collective-permute-start | bytes 3145736 | tf_op jit(solution)/shard_map/ppermute | solution.py:29
  75.2 2.1 %collective-permute-start.11 = (bf16[4,256,512]{2,1,0:T(8,128)(2,1)S(1)}, bf16[4,256,512]{2,1,0:T(8,128)(2,1)}, u32[]{:S(2)}, u32[]{:S(2)}) collective-permute-start(bf16[4,256,512]{2,1,0:T(8,128)(2,1)S(1)} %pad_maximum_fusion.1.refs_4_), channel_id=1, source_target_pairs={{0,384},{1,97},{2,386},{3,99},{4,388},{5,101},{6,390},{7,103},{8,3... | collective-permute-start | bytes 3145736 | tf_op jit(solution)/shard_map/ppermute | solution.py:29
  77.3 0.0 collective-permute-done.6.refs_3_
  77.3 0.0 copy-start.3
  77.4 3.2 %collective-permute-start.10 = (bf16[4,256,512]{2,1,0:T(8,128)(2,1)S(1)}, bf16[4,256,512]{2,1,0:T(8,128)(2,1)}, u32[]{:S(2)}, u32[]{:S(2)}) collective-permute-start(bf16[4,256,512]{2,1,0:T(8,128)(2,1)S(1)} %pad_maximum_fusion.1.refs_4_), channel_id=1, source_target_pairs={{0,128},{1,33},{2,130},{3,35},{4,132},{5,37},{6,134},{7,39},{8,136... | collective-permute-start | bytes 3145736 | tf_op jit(solution)/shard_map/ppermute | solution.py:29
  80.6 0.0 copy-done.4
  80.6 0.1 add_add_fusion
  80.6 0.1 add.57
  80.7 0.1 add.51
  80.8 0.6 fusion.places
  81.4 0.0 collective-permute-done.5.refs_2_
  81.4 8.5 %collective-permute-done.4.refs_1_ = bf16[4,256,512]{2,1,0:T(8,128)(2,1)} collective-permute-done((bf16[4,256,512]{2,1,0:T(8,128)(2,1)S(1)}, bf16[4,256,512]{2,1,0:T(8,128)(2,1)}, u32[]{:S(2)}, u32[]{:S(2)}) %collective-permute-start.4) | collective-permute-done | bytes 1048608 | tf_op jit(solution)/shard_map/ppermute | solution.py:29
  89.9 0.0 collective-permute-done.12.refs_7_
  89.9 11.0 %collective-permute-done.11.refs_6_ = bf16[4,256,512]{2,1,0:T(8,128)(2,1)} collective-permute-done((bf16[4,256,512]{2,1,0:T(8,128)(2,1)S(1)}, bf16[4,256,512]{2,1,0:T(8,128)(2,1)}, u32[]{:S(2)}, u32[]{:S(2)}) %collective-permute-start.11) | collective-permute-done | bytes 1048608 | tf_op jit(solution)/shard_map/ppermute | solution.py:29
  100.9 0.3 collective-permute-done.10.refs_5_
  101.1 0.0 all-gather.2.cloned.1.call-done
  101.1 0.0 copy-done
  101.1 0.0 copy-done.1
  101.1 0.0 copy-done.3
  101.1 9.5 %project.1 = bf16[512,512]{1,0:T(8,128)(2,1)} custom-call(s32[16]{0:T(128)} %fusion.places, bf16[4,256,512]{2,1,0:T(8,128)(2,1)} %copy-done, bf16[4,256,512]{2,1,0:T(8,128)(2,1)} %collective-permute-done.4.refs_1_, bf16[4,256,512]{2,1,0:T(8,128)(2,1)} %collective-permute-done.5.refs_2_, bf16[4,256,512]{2,1,0:T(8,128)(2,1)} %copy-done.3, ...), custom_call_target="tpu_custom_call" | custom-call | flops 4294967296 | bytes 17825792 | tf_op jit(solution)/shard_map/project/pallas_call | solution.py:273
  (1 shorter events, 0.0 us)
Async XLA Ops:
  6.5 74.0 %copy-start.4 = (s32[4]{0:T(128)S(1)}, s32[4]{0:T(128)}, u32[]{:S(2)}) copy-start(s32[4]{0:T(128)} %constant.60.clone) | copy-start | bytes 52
  6.5 94.6 %all-gather.2.cloned.1.call-start = ((), (), s32[]{:S(2)}) async-start(), calls=%async_computation | async-start | bytes 8650752 | tf_op jit(solution)/shard_map/all_gather | solution.py:304
  9.7 23.7 %collective-permute-start.3 = (bf16[320,512]{1,0:T(8,128)(2,1)}, bf16[320,512]{1,0:T(8,128)(2,1)S(1)}, u32[]{:S(2)}, u32[]{:S(2)}) collective-permute-start(bf16[320,512]{1,0:T(8,128)(2,1)} %pack_tail.1), channel_id=1, source_target_pairs={{0,1},{1,2},{2,3},{3,4},{4,5},{5,6},{6,7},{7,8},{8,9},{9,10},{10,1... | collective-permute-start | bytes 983048 | tf_op jit(solution)/shard_map/ppermute | solution.py:317
  23.2 19.6 %collective-permute-start.2 = (bf16[256,512]{1,0:T(8,128)(2,1)}, bf16[256,512]{1,0:T(8,128)(2,1)S(1)}, u32[]{:S(2)}, u32[]{:S(2)}) collective-permute-start(bf16[256,512]{1,0:T(8,128)(2,1)} %gate_late.1), channel_id=1, source_target_pairs={{0,64},{1,257},{2,66},{3,259},{4,68},{5,261},{6,70},{7,263},{8,72}... | collective-permute-start | bytes 786440 | tf_op jit(solution)/shard_map/ppermute | solution.py:25
  28.0 14.7 %collective-permute-start.1 = (bf16[256,512]{1,0:T(8,128)(2,1)}, bf16[256,512]{1,0:T(8,128)(2,1)S(1)}, u32[]{:S(2)}, u32[]{:S(2)}) collective-permute-start(bf16[256,512]{1,0:T(8,128)(2,1)} %gate_late.1), channel_id=1, source_target_pairs={{0,96},{1,385},{2,98},{3,387},{4,100},{5,389},{6,102},{7,391},{8,1... | collective-permute-start | bytes 786440 | tf_op jit(solution)/shard_map/ppermute | solution.py:25
  30.7 12.1 %collective-permute-start = (bf16[256,512]{1,0:T(8,128)(2,1)}, bf16[256,512]{1,0:T(8,128)(2,1)S(1)}, u32[]{:S(2)}, u32[]{:S(2)}) collective-permute-start(bf16[256,512]{1,0:T(8,128)(2,1)} %gate_late.1), channel_id=1, source_target_pairs={{0,32},{1,129},{2,34},{3,131},{4,36},{5,133},{6,38},{7,135},{8,40}... | collective-permute-start | bytes 786440 | tf_op jit(solution)/shard_map/ppermute | solution.py:25
  33.4 0.7 copy-start.2
  43.9 57.2 %copy-start = (bf16[4,256,512]{2,1,0:T(8,128)(2,1)}, bf16[4,256,512]{2,1,0:T(8,128)(2,1)S(1)}, u32[]{:S(2)}) copy-start(bf16[4,256,512]{2,1,0:T(8,128)(2,1)S(1)} %pad_maximum_fusion.refs_0_) | copy-start | bytes 3145732
  43.9 33.4 %collective-permute-start.6 = (bf16[4,256,512]{2,1,0:T(8,128)(2,1)S(1)}, bf16[4,256,512]{2,1,0:T(8,128)(2,1)S(1)}, u32[]{:S(2)}, u32[]{:S(2)}) collective-permute-start(bf16[4,256,512]{2,1,0:T(8,128)(2,1)S(1)} %pad_maximum_fusion.refs_0_), channel_id=1, source_target_pairs={{0,256},{1,65},{2,258},{3,67},{4,260},{5,69},{6,262},{7,71},{8,264... | collective-permute-start | bytes 3145736 | tf_op jit(solution)/shard_map/ppermute | solution.py:29
  48.6 12.0 %collective-permute-start.9 = (bf16[256,512]{1,0:T(8,128)(2,1)}, bf16[256,512]{1,0:T(8,128)(2,1)S(1)}, u32[]{:S(2)}, u32[]{:S(2)}) collective-permute-start(bf16[256,512]{1,0:T(8,128)(2,1)} %gate_early.1), channel_id=1, source_target_pairs={{0,64},{1,257},{2,66},{3,259},{4,68},{5,261},{6,70},{7,263},{8,72}... | collective-permute-start | bytes 786440 | tf_op jit(solution)/shard_map/ppermute | solution.py:25
  51.2 16.5 %collective-permute-start.8 = (bf16[256,512]{1,0:T(8,128)(2,1)}, bf16[256,512]{1,0:T(8,128)(2,1)S(1)}, u32[]{:S(2)}, u32[]{:S(2)}) collective-permute-start(bf16[256,512]{1,0:T(8,128)(2,1)} %gate_early.1), channel_id=1, source_target_pairs={{0,96},{1,385},{2,98},{3,387},{4,100},{5,389},{6,102},{7,391},{8,1... | collective-permute-start | bytes 786440 | tf_op jit(solution)/shard_map/ppermute | solution.py:25
  55.2 13.6 %collective-permute-start.7 = (bf16[256,512]{1,0:T(8,128)(2,1)}, bf16[256,512]{1,0:T(8,128)(2,1)S(1)}, u32[]{:S(2)}, u32[]{:S(2)}) collective-permute-start(bf16[256,512]{1,0:T(8,128)(2,1)} %gate_early.1), channel_id=1, source_target_pairs={{0,32},{1,129},{2,34},{3,131},{4,36},{5,133},{6,38},{7,135},{8,40}... | collective-permute-start | bytes 786440 | tf_op jit(solution)/shard_map/ppermute | solution.py:25
  57.1 24.3 %collective-permute-start.5 = (bf16[4,256,512]{2,1,0:T(8,128)(2,1)S(1)}, bf16[4,256,512]{2,1,0:T(8,128)(2,1)}, u32[]{:S(2)}, u32[]{:S(2)}) collective-permute-start(bf16[4,256,512]{2,1,0:T(8,128)(2,1)S(1)} %pad_maximum_fusion.refs_0_), channel_id=1, source_target_pairs={{0,384},{1,97},{2,386},{3,99},{4,388},{5,101},{6,390},{7,103},{8,3... | collective-permute-start | bytes 3145736 | tf_op jit(solution)/shard_map/ppermute | solution.py:29
  60.6 29.3 %collective-permute-start.4 = (bf16[4,256,512]{2,1,0:T(8,128)(2,1)S(1)}, bf16[4,256,512]{2,1,0:T(8,128)(2,1)}, u32[]{:S(2)}, u32[]{:S(2)}) collective-permute-start(bf16[4,256,512]{2,1,0:T(8,128)(2,1)S(1)} %pad_maximum_fusion.refs_0_), channel_id=1, source_target_pairs={{0,128},{1,33},{2,130},{3,35},{4,132},{5,37},{6,134},{7,39},{8,136... | collective-permute-start | bytes 3145736 | tf_op jit(solution)/shard_map/ppermute | solution.py:29
  69.9 31.2 %copy-start.1 = (bf16[4,256,512]{2,1,0:T(8,128)(2,1)}, bf16[4,256,512]{2,1,0:T(8,128)(2,1)S(1)}, u32[]{:S(2)}) copy-start(bf16[4,256,512]{2,1,0:T(8,128)(2,1)S(1)} %pad_maximum_fusion.1.refs_4_) | copy-start | bytes 3145732
  69.9 20.0 %collective-permute-start.12 = (bf16[4,256,512]{2,1,0:T(8,128)(2,1)S(1)}, bf16[4,256,512]{2,1,0:T(8,128)(2,1)}, u32[]{:S(2)}, u32[]{:S(2)}) collective-permute-start(bf16[4,256,512]{2,1,0:T(8,128)(2,1)S(1)} %pad_maximum_fusion.1.refs_4_), channel_id=1, source_target_pairs={{0,256},{1,65},{2,258},{3,67},{4,260},{5,69},{6,262},{7,71},{8,264... | collective-permute-start | bytes 3145736 | tf_op jit(solution)/shard_map/ppermute | solution.py:29
  75.2 25.6 %collective-permute-start.11 = (bf16[4,256,512]{2,1,0:T(8,128)(2,1)S(1)}, bf16[4,256,512]{2,1,0:T(8,128)(2,1)}, u32[]{:S(2)}, u32[]{:S(2)}) collective-permute-start(bf16[4,256,512]{2,1,0:T(8,128)(2,1)S(1)} %pad_maximum_fusion.1.refs_4_), channel_id=1, source_target_pairs={{0,384},{1,97},{2,386},{3,99},{4,388},{5,101},{6,390},{7,103},{8,3... | collective-permute-start | bytes 3145736 | tf_op jit(solution)/shard_map/ppermute | solution.py:29
  77.3 23.8 %copy-start.3 = (bf16[4,256,512]{2,1,0:T(8,128)(2,1)}, bf16[4,256,512]{2,1,0:T(8,128)(2,1)S(1)}, u32[]{:S(2)}) copy-start(bf16[4,256,512]{2,1,0:T(8,128)(2,1)S(1)} %collective-permute-done.6.refs_3_) | copy-start | bytes 3145732
  77.4 23.8 %collective-permute-start.10 = (bf16[4,256,512]{2,1,0:T(8,128)(2,1)S(1)}, bf16[4,256,512]{2,1,0:T(8,128)(2,1)}, u32[]{:S(2)}, u32[]{:S(2)}) collective-permute-start(bf16[4,256,512]{2,1,0:T(8,128)(2,1)S(1)} %pad_maximum_fusion.1.refs_4_), channel_id=1, source_target_pairs={{0,128},{1,33},{2,130},{3,35},{4,132},{5,37},{6,134},{7,39},{8,136... | collective-permute-start | bytes 3145736 | tf_op jit(solution)/shard_map/ppermute | solution.py:29
Sparse Core Ops, SparseCore 0:
  9.5 85.1 all-gather.1

commit v3 on v2

--- a/solution.py
+++ b/solution.py
@@ -51,7 +51,7 @@
     if late:
         halo_ref = halo_ids_ref = None
     else:
-        halo_ref, halo_ids_ref, *refs = refs
+        _, halo_ref, halo_ids_ref, *refs = refs
     (query_ref, key_ref, value_ref, ids_ref, short_ref, medium_ref, decay_ref, skip_ref) = refs[:8]
     out_ref, query_f, key_f, value_f, ids_f, product_f, masked_f, taps_f, span = refs[8:]
     tiles = HALF // TILE
@@ -184,8 +184,8 @@
     )(key, value, query, ids)
 
 
-def gate(halo, query, key, value, ids, short_taps, medium_taps, decay, skip):
-    late = halo is None
+def gate(whole_gated, halo, query, key, value, ids, short_taps, medium_taps, decay, skip):
+    late = whole_gated is None
     channels = query.shape[1]
     whole = lambda rows: pl.BlockSpec((rows, LANES), lambda i: (0, i))
     specs = [whole(512)] * 3 + [
@@ -198,15 +198,16 @@
     args = [query, key, value, ids, short_taps, medium_taps, decay, skip]
     if not late:
         ids_block = (2 * HALO + 16) // 16
-        specs = [whole(PACK), pl.BlockSpec((16, channels), lambda i: (ids_block, 0))] + specs
-        args = [halo, halo] + args
+        specs = [pl.BlockSpec(memory_space=pl.ANY), whole(halo.shape[0]), pl.BlockSpec((16, channels), lambda i: (ids_block, 0))] + specs
+        args = [whole_gated, halo, halo] + args
     f32 = lambda rows: pltpu.VMEM((rows, LANES), jnp.float32)
     return pl.pallas_call(
         functools.partial(filter_kernel, late),
         grid=(channels // LANES,),
-        out_shape=jax.ShapeDtypeStruct((HALF, channels), jnp.bfloat16),
+        out_shape=jax.ShapeDtypeStruct((2 * HALF, channels), jnp.bfloat16),
         in_specs=specs,
-        out_specs=whole(HALF),
+        out_specs=pl.BlockSpec((HALF, LANES), lambda i: (int(late), i)),
+        input_output_aliases={} if late else {0: 0},
         scratch_shapes=[
             f32(HALF + 16),
             f32(WINDOW),
@@ -225,39 +226,59 @@
     )(*args)
 
 
-def project_kernel(places, *refs):
-    lates, earlies = refs[:SIDE], refs[SIDE : 2 * SIDE]
-    weight, out_ref, blocks, weights, total, block_sem, weight_sem = refs[2 * SIDE :]
-    slots = SIDE * SIDE
+def near_kernel(places, *refs):
+    count = 2 * (SIDE - 1)
+    panels = refs[:count]
+    weight, total, far_weights, blocks, weights, block_sem, weight_sem = refs[count:]
+    near = 2 * count
     copies = []
-    for at in range(slots):
-        group, member = at // SIDE, at % SIDE
+    for at in range(near):
+        panel = panels[at // 2].at[at % 2]
         copies.append(
             (
-                pltpu.make_async_copy(
-                    earlies[group].at[member], blocks.at[at, 0:HALF], block_sem.at[2 * at]
-                ),
-                pltpu.make_async_copy(
-                    lates[group].at[member], blocks.at[at, HALF:], block_sem.at[2 * at + 1]
-                ),
                 pltpu.make_async_copy(weight.at[places[at]], weights.at[at], weight_sem.at[at]),
+                pltpu.make_async_copy(panel, blocks.at[at], block_sem.at[at]),
             )
         )
-        for copy in copies[at]:
+    later = [
+        pltpu.make_async_copy(
+            weight.at[places[near + i]], far_weights.at[i], weight_sem.at[near + i]
+        )
+        for i in range(SIDE)
+    ]
+    for pair in copies:
+        for copy in pair:
             copy.start()
-    for at in range(slots):
+    for copy in later:
+        copy.start()
+    for at in range(near):
         for copy in copies[at]:
             copy.wait()
         part = jnp.dot(blocks[at], weights[at], preferred_element_type=jnp.float32)
-        if at == 0:
-            total[...] = part
-        elif at < slots - 1:
-            total[...] += part
+        total[...] = part if at == 0 else total[...] + part
+    for copy in later:
+        copy.wait()
+
+
+def far_kernel(total, weights, low, high, out_ref, blocks, summed, sem):
+    copies = [
+        pltpu.make_async_copy((low, high)[i // 2].at[i % 2], blocks.at[i], sem.at[i])
+        for i in range(SIDE)
+    ]
+    for copy in copies:
+        copy.start()
+    for i in range(SIDE):
+        copies[i].wait()
+        part = jnp.dot(blocks[i], weights[i], preferred_element_type=jnp.float32)
+        if i == 0:
+            summed[...] = total[...] + part
+        elif i < SIDE - 1:
+            summed[...] += part
         else:
-            out_ref[...] = (total[...] + part).astype(jnp.bfloat16)
-
-
-def project(lates, earlies, weight):
+            out_ref[...] = (summed[...] + part).astype(jnp.bfloat16)
+
+
+def project(near, far, weight):
     chan = lax.axis_index("chan")
     y, x = chan // SIDE, chan % SIDE
     core = lax.axis_index("stretch") % 2
@@ -268,26 +289,47 @@
     places = (y + oy + SIDE) % SIDE * SIDE + (x + ox + SIDE) % SIDE
     slots = SIDE * SIDE
     columns = weight.shape[1]
-    tokens, depth = 2 * HALF, lates[0].shape[2]
+    tokens, depth = near[0].shape[1:]
     hbm = pl.BlockSpec(memory_space=pl.ANY)
-    return pl.pallas_call(
-        project_kernel,
-        out_shape=jax.ShapeDtypeStruct((tokens, columns), jnp.bfloat16),
-        in_specs=[pl.BlockSpec(memory_space=pltpu.SMEM)] + [hbm] * 9,
-        out_specs=pl.BlockSpec(memory_space=pltpu.VMEM),
+    vmem = pl.BlockSpec(memory_space=pltpu.VMEM)
+    params = pltpu.CompilerParams(vmem_limit_bytes=54 << 20)
+    cost = lambda blocks: pl.CostEstimate(
+        flops=2 * tokens * blocks * depth * columns, bytes_accessed=blocks << 20, transcendentals=0
+    )
+    count = slots - SIDE
+    total, weights = pl.pallas_call(
+        near_kernel,
+        out_shape=[
+            pltpu.VMEM((tokens, columns), jnp.float32),
+            pltpu.VMEM((SIDE, depth, columns), jnp.bfloat16),
+        ],
+        in_specs=[pl.BlockSpec(memory_space=pltpu.SMEM)] + [hbm] * (len(near) + 1),
+        out_specs=[vmem, vmem],
         scratch_shapes=[
-            pltpu.VMEM((slots, tokens, depth), jnp.bfloat16),
-            pltpu.VMEM((slots, depth, columns), jnp.bfloat16),
-            pltpu.VMEM((tokens, columns), jnp.float32),
-            pltpu.SemaphoreType.DMA((2 * slots,)),
+            pltpu.VMEM((count, tokens, depth), jnp.bfloat16),
+            pltpu.VMEM((count, depth, columns), jnp.bfloat16),
+            pltpu.SemaphoreType.DMA((count,)),
             pltpu.SemaphoreType.DMA((slots,)),
         ],
-        compiler_params=pltpu.CompilerParams(vmem_limit_bytes=60 << 20),
-        cost_estimate=pl.CostEstimate(
-            flops=2 * tokens * slots * depth * columns, bytes_accessed=17 << 20, transcendentals=0
-        ),
-        name="project",
-    )(places.astype(jnp.int32), *lates, *earlies, weight.reshape(slots, depth, columns))
+        compiler_params=params,
+        cost_estimate=cost(count),
+        name="project_near",
+    )(places.astype(jnp.int32), *near, weight.reshape(slots, depth, columns))
+    in_vmem = lambda value: pltpu.with_memory_space_constraint(value, pltpu.VMEM)
+    return pl.pallas_call(
+        far_kernel,
+        out_shape=jax.ShapeDtypeStruct((tokens, columns), jnp.bfloat16),
+        in_specs=[vmem, vmem, hbm, hbm],
+        out_specs=vmem,
+        scratch_shapes=[
+            pltpu.VMEM((SIDE, tokens, depth), jnp.bfloat16),
+            pltpu.VMEM((tokens, columns), jnp.float32),
+            pltpu.SemaphoreType.DMA((SIDE,)),
+        ],
+        compiler_params=params,
+        cost_estimate=cost(SIDE),
+        name="project_far",
+    )(in_vmem(total), in_vmem(weights), *far)
 
 
 def body(
@@ -315,15 +357,18 @@
     devices = lax.axis_size("stretch")
     pack = pack_tail(key_in, value_in, query_in, rest[3])
     halo = lax.ppermute(pack, "stretch", [(i, i + 1) for i in range(devices - 1)])
-    late = gate(None, *rest)
-    late_line = [late] + [first_way(late, -by) for by in OFFSETS[1:]]
-    early = gate(halo, *rest)
-    late_line, early = lax.optimization_barrier((late_line, early))
-    early_line = [early] + [first_way(early, -by) for by in OFFSETS[1:]]
-    late_line, early_line = jnp.stack(late_line), jnp.stack(early_line)
-    late_panels = [late_line] + [second_way(late_line, -by) for by in OFFSETS[1:]]
-    early_panels = [early_line] + [second_way(early_line, -by) for by in OFFSETS[1:]]
-    return project(late_panels, early_panels, weight)
+    gated = gate(None, None, *rest)
+    gated = gate(gated, halo, *rest)
+    line = [gated] + [first_way(gated, -by) for by in OFFSETS[1:]]
+    low, high = jnp.stack(line[:2]), jnp.stack(line[2:])
+    below_low = second_way(low, 1)
+    above_high = second_way(high, -1)
+    below_high = second_way(high, 1)
+    above_low = second_way(low, -1)
+    far_low = second_way(below_low, 1)
+    far_high = second_way(above_high, -1)
+    near = [low, high, below_low, below_high, above_low, above_high]
+    return project(near, [far_low, far_high], weight)
 
 
 def solution(mesh):

time: 119 us -> 112 us (0.941)
  starting transfers between devices: 43.8 us -> 35.6 us
  waiting for transfers between devices: 27.1 us -> 30 us
    all_gather x1, waiting for transfers between devices: 0.01 us -> 10.2 us  [body(): weight = lax.all_gather(out_weight, 'stretch', axis=0, tiled=True)]
    ppermute x6 -> x3, starting transfers between devices: 18.6 us -> 9.49 us  [first_way(): return lax.ppermute(value, ('chan', 'stretch'), moves(by, 0))]
    ppermute x6, waiting for transfers between devices: 19.7 us -> 10.8 us  [second_way(): return lax.ppermute(value, ('chan', 'stretch'), moves(by, 1))]
    ppermute x6 -> x3, waiting for transfers between devices: 6.71 us -> 8.28 us  [first_way(): return lax.ppermute(value, ('chan', 'stretch'), moves(by, 0))]
    pallas_call x1 -> x2, Pallas kernels: 9.51 us -> 9.92 us  [the longest x1 6.59 us: project(): pl.pallas_call(near_kernel, out_shape=[pltpu.VMEM((tokens, columns), jnp....]
  transfers between devices with their start and end apart: 14 -> 11, of which waited for: 6 -> 5; matrix products, arithmetic and copies ran while one was open for 3% -> 2% of each run, Pallas kernels for 17% -> 24%
where the time goes in v3:
time: 112 us
  starting transfers between devices  35.6 us (32%)
  waiting for transfers between devices  30 us (27%)
  Pallas kernels  29.6 us (26%)
  between operations  13.6 us (12%)
  other arithmetic  1.84 us (2%)
    ppermute x6, starting transfers between devices, second_way(): return lax.ppermute(value, ('chan', 'stretch'), moves(by, 1))  21.1 us
    pallas_call x2, Pallas kernels, gate(): pl.pallas_call(functools.partial(filter_kernel, late), grid=(channels //...  17.3 us
    ppermute x6, waiting for transfers between devices, second_way(): return lax.ppermute(value, ('chan', 'stretch'), moves(by, 1))  10.8 us
    all_gather x1, waiting for transfers between devices, body(): weight = lax.all_gather(out_weight, 'stretch', axis=0, tiled=True)  10.2 us
    ppermute x3, starting transfers between devices, first_way(): return lax.ppermute(value, ('chan', 'stretch'), moves(by, 0))  9.49 us
    ppermute x3, waiting for transfers between devices, first_way(): return lax.ppermute(value, ('chan', 'stretch'), moves(by, 0))  8.28 us
    pallas_call x1, Pallas kernels, project(): pl.pallas_call(near_kernel, out_shape=[pltpu.VMEM((tokens, columns), jnp....  6.59 us
    ppermute x1, starting transfers between devices, body(): lax.ppermute(pack, 'stretch', [(i, i + 1) for i in range(devices - 1)])  4.94 us
  transfers between devices with their start and end apart: 11, of which 5 were waited for; matrix products, arithmetic and copies ran while one was open for 2% of the time, Pallas kernels for 24%

profile of v3, /device:TPU:1, one launch (start us, length us, event | category | flops | bytes accessed | tf_op | source)
XLA Modules:
  0.0 111.5 jit_solution(316554549501421684)
XLA Ops:
  6.5 0.0 copy-start.4
  6.5 0.0 all-gather.2.cloned.1.call-start
  6.5 0.7 all-gather.2.cloned.1.call-update
  7.3 2.4 %pack_tail.1 = bf16[320,512]{1,0:T(8,128)(2,1)} custom-call(bf16[512,512]{1,0:T(8,128)(2,1)} %refs_4_.3, bf16[512,512]{1,0:T(8,128)(2,1)} %refs_5_.3, bf16[512,512]{1,0:T(8,128)(2,1)} %refs_3_.1, s32[4,128]{1,0:T(4,128)} %bitcast.13), custom_call_target="tpu_custom_call" | custom-call | bytes 700000 | tf_op jit(solution)/shard_map/pack_tail/pallas_call | solution.py:175
  9.7 4.9 %collective-permute-start = (bf16[320,512]{1,0:T(8,128)(2,1)}, bf16[320,512]{1,0:T(8,128)(2,1)S(1)}, u32[]{:S(2)}, u32[]{:S(2)}) collective-permute-start(bf16[320,512]{1,0:T(8,128)(2,1)} %pack_tail.1), channel_id=1, source_target_pairs={{0,1},{1,2},{2,3},{3,4},{4,5},{5,6},{6,7},{7,8},{8,9},{9,10},{10,1... | collective-permute-start | bytes 983048 | tf_op jit(solution)/shard_map/ppermute | solution.py:359
  14.6 8.6 %gate_late.1.refs_0_ = bf16[512,512]{1,0:T(8,128)(2,1)} custom-call(bf16[512,512]{1,0:T(8,128)(2,1)} %refs_3_.1, bf16[512,512]{1,0:T(8,128)(2,1)} %refs_4_.3, bf16[512,512]{1,0:T(8,128)(2,1)} %refs_5_.3, s32[4,128]{1,0:T(4,128)} %bitcast.14, f32[3,7,512]{2,1,0:T(8,128)} %refs_7_.1, f32[128,512]{1,0:T(8,128)} %refs_8_.1, f32[1,512]{1,0:T(1,128)} %bitcast.16, ...), custom_call_target="tpu_custom_call" | custom-call | flops 134217728 | bytes 2097152 | tf_op jit(solution)/shard_map/gate_late/pallas_call | solution.py:204
  23.2 0.0 collective-permute-done.refs_1_.refs_2_
  23.3 0.0 copy-start.2
  23.3 0.7 copy-done.2
  24.0 8.7 %gate_early.1 = bf16[512,512]{1,0:T(8,128)(2,1)} custom-call(bf16[512,512]{1,0:T(8,128)(2,1)} %gate_late.1.refs_0_, bf16[320,512]{1,0:T(8,128)(2,1)} %copy-done.2, bf16[320,512]{1,0:T(8,128)(2,1)} %copy-done.2, bf16[512,512]{1,0:T(8,128)(2,1)} %refs_3_.1, bf16[512,512]{1,0:T(8,128)(2,1)} %refs_4_.3, ...), custom_call_target="tpu_custom_call", output_to_operand_aliasing={{}: (0, {})} | custom-call | flops 134217728 | bytes 2097152 | tf_op jit(solution)/shard_map/gate_early/pallas_call | solution.py:204
  32.7 4.6 %collective-permute-start.2 = (bf16[512,512]{1,0:T(8,128)(2,1)}, bf16[512,512]{1,0:T(8,128)(2,1)S(1)}, u32[]{:S(2)}, u32[]{:S(2)}) collective-permute-start(bf16[512,512]{1,0:T(8,128)(2,1)} %gate_early.1), channel_id=1, source_target_pairs={{0,96},{1,385},{2,98},{3,387},{4,100},{5,389},{6,102},{7,391},{8,1... | collective-permute-start | bytes 1572872 | tf_op jit(solution)/shard_map/ppermute | solution.py:25
  37.3 2.3 %collective-permute-start.3 = (bf16[512,512]{1,0:T(8,128)(2,1)}, bf16[512,512]{1,0:T(8,128)(2,1)S(1)}, u32[]{:S(2)}, u32[]{:S(2)}) collective-permute-start(bf16[512,512]{1,0:T(8,128)(2,1)} %gate_early.1), channel_id=1, source_target_pairs={{0,64},{1,257},{2,66},{3,259},{4,68},{5,261},{6,70},{7,263},{8,72}... | collective-permute-start | bytes 1572872 | tf_op jit(solution)/shard_map/ppermute | solution.py:25
  39.6 2.6 %collective-permute-start.1 = (bf16[512,512]{1,0:T(8,128)(2,1)}, bf16[512,512]{1,0:T(8,128)(2,1)S(1)}, u32[]{:S(2)}, u32[]{:S(2)}) collective-permute-start(bf16[512,512]{1,0:T(8,128)(2,1)} %gate_early.1), channel_id=1, source_target_pairs={{0,32},{1,129},{2,34},{3,131},{4,36},{5,133},{6,38},{7,135},{8,40}... | collective-permute-start | bytes 1572872 | tf_op jit(solution)/shard_map/ppermute | solution.py:25
  42.2 7.2 %collective-permute-done.2 = bf16[512,512]{1,0:T(8,128)(2,1)S(1)} collective-permute-done((bf16[512,512]{1,0:T(8,128)(2,1)}, bf16[512,512]{1,0:T(8,128)(2,1)S(1)}, u32[]{:S(2)}, u32[]{:S(2)}) %collective-permute-start.2) | collective-permute-done | bytes 524320 | tf_op jit(solution)/shard_map/ppermute | solution.py:25
  49.4 0.0 collective-permute-done.3
  49.4 0.1 pad_maximum_fusion.1.refs_1_
  49.5 0.0 copy-start
  49.5 4.4 %collective-permute-start.7 = (bf16[2,512,512]{2,1,0:T(8,128)(2,1)S(1)}, bf16[2,512,512]{2,1,0:T(8,128)(2,1)S(1)}, u32[]{:S(2)}, u32[]{:S(2)}) collective-permute-start(bf16[2,512,512]{2,1,0:T(8,128)(2,1)S(1)} %pad_maximum_fusion.1.refs_1_), channel_id=1, source_target_pairs={{0,384},{1,97},{2,386},{3,99},{4,388},{5,101},{6,390},{7,103},{8,3... | collective-permute-start | bytes 3145736 | tf_op jit(solution)/shard_map/ppermute | solution.py:29
  53.9 1.1 collective-permute-done.1
  55.0 1.1 %pad_maximum_fusion.refs_0_ = bf16[2,512,512]{2,1,0:T(8,128)(2,1)S(1)} fusion(bf16[1,512,512]{2,1,0:T(8,128)(2,1)S(1)} %bitcast.10, bf16[1,512,512]{2,1,0:T(8,128)(2,1)} %bitcast.9), kind=kLoop, calls=%fused_computation | loop fusion | flops 524288 | bytes 2097152 | tf_op jit(solution)/shard_map/stack | solution.py:363
  56.1 0.0 copy-start.1
  56.1 3.1 %collective-permute-start.4 = (bf16[2,512,512]{2,1,0:T(8,128)(2,1)S(1)}, bf16[2,512,512]{2,1,0:T(8,128)(2,1)}, u32[]{:S(2)}, u32[]{:S(2)}) collective-permute-start(bf16[2,512,512]{2,1,0:T(8,128)(2,1)S(1)} %pad_maximum_fusion.refs_0_), channel_id=1, source_target_pairs={{0,128},{1,33},{2,130},{3,35},{4,132},{5,37},{6,134},{7,39},{8,136... | collective-permute-start | bytes 3145736 | tf_op jit(solution)/shard_map/ppermute | solution.py:29
  59.3 3.1 %collective-permute-start.5 = (bf16[2,512,512]{2,1,0:T(8,128)(2,1)S(1)}, bf16[2,512,512]{2,1,0:T(8,128)(2,1)}, u32[]{:S(2)}, u32[]{:S(2)}) collective-permute-start(bf16[2,512,512]{2,1,0:T(8,128)(2,1)S(1)} %pad_maximum_fusion.1.refs_1_), channel_id=1, source_target_pairs={{0,128},{1,33},{2,130},{3,35},{4,132},{5,37},{6,134},{7,39},{8,136... | collective-permute-start | bytes 3145736 | tf_op jit(solution)/shard_map/ppermute | solution.py:29
  62.4 3.4 %collective-permute-start.6 = (bf16[2,512,512]{2,1,0:T(8,128)(2,1)S(1)}, bf16[2,512,512]{2,1,0:T(8,128)(2,1)}, u32[]{:S(2)}, u32[]{:S(2)}) collective-permute-start(bf16[2,512,512]{2,1,0:T(8,128)(2,1)S(1)} %pad_maximum_fusion.refs_0_), channel_id=1, source_target_pairs={{0,384},{1,97},{2,386},{3,99},{4,388},{5,101},{6,390},{7,103},{8,3... | collective-permute-start | bytes 3145736 | tf_op jit(solution)/shard_map/ppermute | solution.py:29
  65.8 0.0 collective-permute-done.7.refs_5_
  65.8 0.0 copy-start.3
  65.8 5.2 %collective-permute-start.9 = (bf16[2,512,512]{2,1,0:T(8,128)(2,1)S(1)}, bf16[2,512,512]{2,1,0:T(8,128)(2,1)}, u32[]{:S(2)}, u32[]{:S(2)}) collective-permute-start(bf16[2,512,512]{2,1,0:T(8,128)(2,1)S(1)} %collective-permute-done.7.refs_5_), channel_id=1, source_target_pairs={{0,384},{1,97},{2,386},{3,99},{4,388},{5,101},{6,390},{7,103},{8,3... | collective-permute-start | bytes 3145736 | tf_op jit(solution)/shard_map/ppermute | solution.py:29
  71.0 2.3 %collective-permute-done.4.refs_2_ = bf16[2,512,512]{2,1,0:T(8,128)(2,1)} collective-permute-done((bf16[2,512,512]{2,1,0:T(8,128)(2,1)S(1)}, bf16[2,512,512]{2,1,0:T(8,128)(2,1)}, u32[]{:S(2)}, u32[]{:S(2)}) %collective-permute-start.4) | collective-permute-done | bytes 1048608 | tf_op jit(solution)/shard_map/ppermute | solution.py:29
  73.3 1.9 %collective-permute-start.8 = (bf16[2,512,512]{2,1,0:T(8,128)(2,1)}, bf16[2,512,512]{2,1,0:T(8,128)(2,1)}, u32[]{:S(2)}, u32[]{:S(2)}) collective-permute-start(bf16[2,512,512]{2,1,0:T(8,128)(2,1)} %collective-permute-done.4.refs_2_), channel_id=1, source_target_pairs={{0,128},{1,33},{2,130},{3,35},{4,132},{5,37},{6,134},{7,39},{8,136... | collective-permute-start | bytes 3145736 | tf_op jit(solution)/shard_map/ppermute | solution.py:29
  75.2 0.0 copy-done.4
  75.2 0.1 add_add_fusion
  75.3 0.1 add.51
  75.4 0.1 add.57
  75.5 0.5 fusion.places
  76.0 8.5 %collective-permute-done.5.refs_3_ = bf16[2,512,512]{2,1,0:T(8,128)(2,1)} collective-permute-done((bf16[2,512,512]{2,1,0:T(8,128)(2,1)S(1)}, bf16[2,512,512]{2,1,0:T(8,128)(2,1)}, u32[]{:S(2)}, u32[]{:S(2)}) %collective-permute-start.5) | collective-permute-done | bytes 1048608 | tf_op jit(solution)/shard_map/ppermute | solution.py:29
  84.5 0.0 collective-permute-done.6.refs_4_
  84.5 10.2 %all-gather.2.cloned.1.call-done = bf16[8192,512]{1,0:T(8,128)(2,1)} async-done(((bf16[256,512]{1,0:T(8,128)(2,1)}), bf16[8192,512]{1,0:T(8,128)(2,1)}) %all-gather.2.cloned.1.call-update) | async-done | bytes 8388624 | tf_op jit(solution)/shard_map/all_gather | solution.py:346
  94.7 0.0 copy-done
  94.7 0.0 copy-done.1
  94.7 0.0 copy-done.3
  94.7 6.6 %project_near.1 = (f32[512,512]{1,0:T(8,128)S(1)}, bf16[4,512,512]{2,1,0:T(8,128)(2,1)S(1)}) custom-call(s32[16]{0:T(128)} %fusion.places, bf16[2,512,512]{2,1,0:T(8,128)(2,1)} %copy-done.1, bf16[2,512,512]{2,1,0:T(8,128)(2,1)} %copy-done, bf16[2,512,512]{2,1,0:T(8,128)(2,1)} %collective-permute-done.4.refs_2_, ...), custom_call_target="tpu_custom_call" | custom-call | flops 3221225472 | bytes 12582912 | tf_op jit(solution)/shard_map/project_near/pallas_call | solution.py:300
  101.3 0.0 collective-permute-done.9.high
  101.3 0.0 collective-permute-done.8.low
  101.3 3.3 %project_far.1 = bf16[512,512]{1,0:T(8,128)(2,1)} custom-call(f32[512,512]{1,0:T(8,128)S(1)} %get-tuple-element.7.total, bf16[4,512,512]{2,1,0:T(8,128)(2,1)S(1)} %get-tuple-element.8.weights, bf16[2,512,512]{2,1,0:T(8,128)(2,1)} %collective-permute-done.8.low, bf16[2,512,512]{2,1,0:T(8,128)(2,1)} %collective-permute-done.9.high), custom_call_target="tpu_custom_call" | custom-call | flops 1073741824 | bytes 4194304 | tf_op jit(solution)/shard_map/project_far/pallas_call | solution.py:319
Async XLA Ops:
  6.5 68.7 %copy-start.4 = (s32[4]{0:T(128)S(1)}, s32[4]{0:T(128)}, u32[]{:S(2)}) copy-start(s32[4]{0:T(128)} %constant.60.clone) | copy-start | bytes 52
  6.5 88.2 %all-gather.2.cloned.1.call-start = ((), (), s32[]{:S(2)}) async-start(), calls=%async_computation | async-start | bytes 8650752 | tf_op jit(solution)/shard_map/all_gather | solution.py:346
  9.7 13.6 %collective-permute-start = (bf16[320,512]{1,0:T(8,128)(2,1)}, bf16[320,512]{1,0:T(8,128)(2,1)S(1)}, u32[]{:S(2)}, u32[]{:S(2)}) collective-permute-start(bf16[320,512]{1,0:T(8,128)(2,1)} %pack_tail.1), channel_id=1, source_target_pairs={{0,1},{1,2},{2,3},{3,4},{4,5},{5,6},{6,7},{7,8},{8,9},{9,10},{10,1... | collective-permute-start | bytes 983048 | tf_op jit(solution)/shard_map/ppermute | solution.py:359
  23.3 0.7 copy-start.2
  32.7 16.7 %collective-permute-start.2 = (bf16[512,512]{1,0:T(8,128)(2,1)}, bf16[512,512]{1,0:T(8,128)(2,1)S(1)}, u32[]{:S(2)}, u32[]{:S(2)}) collective-permute-start(bf16[512,512]{1,0:T(8,128)(2,1)} %gate_early.1), channel_id=1, source_target_pairs={{0,96},{1,385},{2,98},{3,387},{4,100},{5,389},{6,102},{7,391},{8,1... | collective-permute-start | bytes 1572872 | tf_op jit(solution)/shard_map/ppermute | solution.py:25
  37.3 12.0 %collective-permute-start.3 = (bf16[512,512]{1,0:T(8,128)(2,1)}, bf16[512,512]{1,0:T(8,128)(2,1)S(1)}, u32[]{:S(2)}, u32[]{:S(2)}) collective-permute-start(bf16[512,512]{1,0:T(8,128)(2,1)} %gate_early.1), channel_id=1, source_target_pairs={{0,64},{1,257},{2,66},{3,259},{4,68},{5,261},{6,70},{7,263},{8,72}... | collective-permute-start | bytes 1572872 | tf_op jit(solution)/shard_map/ppermute | solution.py:25
  39.6 15.4 %collective-permute-start.1 = (bf16[512,512]{1,0:T(8,128)(2,1)}, bf16[512,512]{1,0:T(8,128)(2,1)S(1)}, u32[]{:S(2)}, u32[]{:S(2)}) collective-permute-start(bf16[512,512]{1,0:T(8,128)(2,1)} %gate_early.1), channel_id=1, source_target_pairs={{0,32},{1,129},{2,34},{3,131},{4,36},{5,133},{6,38},{7,135},{8,40}... | collective-permute-start | bytes 1572872 | tf_op jit(solution)/shard_map/ppermute | solution.py:25
  49.5 45.3 %copy-start = (bf16[2,512,512]{2,1,0:T(8,128)(2,1)}, bf16[2,512,512]{2,1,0:T(8,128)(2,1)S(1)}, u32[]{:S(2)}) copy-start(bf16[2,512,512]{2,1,0:T(8,128)(2,1)S(1)} %pad_maximum_fusion.1.refs_1_) | copy-start | bytes 3145732
  49.5 16.3 %collective-permute-start.7 = (bf16[2,512,512]{2,1,0:T(8,128)(2,1)S(1)}, bf16[2,512,512]{2,1,0:T(8,128)(2,1)S(1)}, u32[]{:S(2)}, u32[]{:S(2)}) collective-permute-start(bf16[2,512,512]{2,1,0:T(8,128)(2,1)S(1)} %pad_maximum_fusion.1.refs_1_), channel_id=1, source_target_pairs={{0,384},{1,97},{2,386},{3,99},{4,388},{5,101},{6,390},{7,103},{8,3... | collective-permute-start | bytes 3145736 | tf_op jit(solution)/shard_map/ppermute | solution.py:29
  56.1 38.6 %copy-start.1 = (bf16[2,512,512]{2,1,0:T(8,128)(2,1)}, bf16[2,512,512]{2,1,0:T(8,128)(2,1)S(1)}, u32[]{:S(2)}) copy-start(bf16[2,512,512]{2,1,0:T(8,128)(2,1)S(1)} %pad_maximum_fusion.refs_0_) | copy-start | bytes 3145732
  56.1 17.2 %collective-permute-start.4 = (bf16[2,512,512]{2,1,0:T(8,128)(2,1)S(1)}, bf16[2,512,512]{2,1,0:T(8,128)(2,1)}, u32[]{:S(2)}, u32[]{:S(2)}) collective-permute-start(bf16[2,512,512]{2,1,0:T(8,128)(2,1)S(1)} %pad_maximum_fusion.refs_0_), channel_id=1, source_target_pairs={{0,128},{1,33},{2,130},{3,35},{4,132},{5,37},{6,134},{7,39},{8,136... | collective-permute-start | bytes 3145736 | tf_op jit(solution)/shard_map/ppermute | solution.py:29
  59.3 25.3 %collective-permute-start.5 = (bf16[2,512,512]{2,1,0:T(8,128)(2,1)S(1)}, bf16[2,512,512]{2,1,0:T(8,128)(2,1)}, u32[]{:S(2)}, u32[]{:S(2)}) collective-permute-start(bf16[2,512,512]{2,1,0:T(8,128)(2,1)S(1)} %pad_maximum_fusion.1.refs_1_), channel_id=1, source_target_pairs={{0,128},{1,33},{2,130},{3,35},{4,132},{5,37},{6,134},{7,39},{8,136... | collective-permute-start | bytes 3145736 | tf_op jit(solution)/shard_map/ppermute | solution.py:29
  62.4 22.1 %collective-permute-start.6 = (bf16[2,512,512]{2,1,0:T(8,128)(2,1)S(1)}, bf16[2,512,512]{2,1,0:T(8,128)(2,1)}, u32[]{:S(2)}, u32[]{:S(2)}) collective-permute-start(bf16[2,512,512]{2,1,0:T(8,128)(2,1)S(1)} %pad_maximum_fusion.refs_0_), channel_id=1, source_target_pairs={{0,384},{1,97},{2,386},{3,99},{4,388},{5,101},{6,390},{7,103},{8,3... | collective-permute-start | bytes 3145736 | tf_op jit(solution)/shard_map/ppermute | solution.py:29
  65.8 28.9 %copy-start.3 = (bf16[2,512,512]{2,1,0:T(8,128)(2,1)}, bf16[2,512,512]{2,1,0:T(8,128)(2,1)S(1)}, u32[]{:S(2)}) copy-start(bf16[2,512,512]{2,1,0:T(8,128)(2,1)S(1)} %collective-permute-done.7.refs_5_) | copy-start | bytes 3145732
  65.8 35.5 %collective-permute-start.9 = (bf16[2,512,512]{2,1,0:T(8,128)(2,1)S(1)}, bf16[2,512,512]{2,1,0:T(8,128)(2,1)}, u32[]{:S(2)}, u32[]{:S(2)}) collective-permute-start(bf16[2,512,512]{2,1,0:T(8,128)(2,1)S(1)} %collective-permute-done.7.refs_5_), channel_id=1, source_target_pairs={{0,384},{1,97},{2,386},{3,99},{4,388},{5,101},{6,390},{7,103},{8,3... | collective-permute-start | bytes 3145736 | tf_op jit(solution)/shard_map/ppermute | solution.py:29
  73.3 28.0 %collective-permute-start.8 = (bf16[2,512,512]{2,1,0:T(8,128)(2,1)}, bf16[2,512,512]{2,1,0:T(8,128)(2,1)}, u32[]{:S(2)}, u32[]{:S(2)}) collective-permute-start(bf16[2,512,512]{2,1,0:T(8,128)(2,1)} %collective-permute-done.4.refs_2_), channel_id=1, source_target_pairs={{0,128},{1,33},{2,130},{3,35},{4,132},{5,37},{6,134},{7,39},{8,136... | collective-permute-start | bytes 3145736 | tf_op jit(solution)/shard_map/ppermute | solution.py:29
Sparse Core Ops, SparseCore 0:
  9.5 85.1 all-gather.1

commit v4 on v3

--- a/solution.py
+++ b/solution.py
@@ -227,7 +227,7 @@
 
 
 def near_kernel(places, *refs):
-    count = 2 * (SIDE - 1)
+    count = 2 * SIDE - 1
     panels = refs[:count]
     weight, total, far_weights, blocks, weights, block_sem, weight_sem = refs[count:]
     near = 2 * count
@@ -244,7 +244,7 @@
         pltpu.make_async_copy(
             weight.at[places[near + i]], far_weights.at[i], weight_sem.at[near + i]
         )
-        for i in range(SIDE)
+        for i in range(2)
     ]
     for pair in copies:
         for copy in pair:
@@ -260,22 +260,24 @@
         copy.wait()
 
 
-def far_kernel(total, weights, low, high, out_ref, blocks, summed, sem):
-    copies = [
-        pltpu.make_async_copy((low, high)[i // 2].at[i % 2], blocks.at[i], sem.at[i])
-        for i in range(SIDE)
-    ]
+def far_kernel(total, weights, panel, out_ref, blocks, rounded, sem, out_sem):
+    copies = [pltpu.make_async_copy(panel.at[i], blocks.at[i], sem.at[i]) for i in range(2)]
     for copy in copies:
         copy.start()
-    for i in range(SIDE):
-        copies[i].wait()
-        part = jnp.dot(blocks[i], weights[i], preferred_element_type=jnp.float32)
-        if i == 0:
-            summed[...] = total[...] + part
-        elif i < SIDE - 1:
-            summed[...] += part
-        else:
-            out_ref[...] = (summed[...] + part).astype(jnp.bfloat16)
+    for copy in copies:
+        copy.wait()
+    tokens = total.shape[0]
+    gives = []
+    for half in range(2):
+        rows = slice(tokens // 2 * half, tokens // 2 * (half + 1))
+        summed = total[rows]
+        for i in range(2):
+            summed += jnp.dot(blocks[i, rows], weights[i], preferred_element_type=jnp.float32)
+        rounded[rows] = summed.astype(jnp.bfloat16)
+        gives.append(pltpu.make_async_copy(rounded.at[rows], out_ref.at[rows], out_sem.at[half]))
+        gives[half].start()
+    for give in gives:
+        give.wait()
 
 
 def project(near, far, weight):
@@ -296,12 +298,12 @@
     cost = lambda blocks: pl.CostEstimate(
         flops=2 * tokens * blocks * depth * columns, bytes_accessed=blocks << 20, transcendentals=0
     )
-    count = slots - SIDE
+    count = slots - 2
     total, weights = pl.pallas_call(
         near_kernel,
         out_shape=[
             pltpu.VMEM((tokens, columns), jnp.float32),
-            pltpu.VMEM((SIDE, depth, columns), jnp.bfloat16),
+            pltpu.VMEM((2, depth, columns), jnp.bfloat16),
         ],
         in_specs=[pl.BlockSpec(memory_space=pltpu.SMEM)] + [hbm] * (len(near) + 1),
         out_specs=[vmem, vmem],
@@ -319,17 +321,18 @@
     return pl.pallas_call(
         far_kernel,
         out_shape=jax.ShapeDtypeStruct((tokens, columns), jnp.bfloat16),
-        in_specs=[vmem, vmem, hbm, hbm],
-        out_specs=vmem,
+        in_specs=[vmem, vmem, hbm],
+        out_specs=hbm,
         scratch_shapes=[
-            pltpu.VMEM((SIDE, tokens, depth), jnp.bfloat16),
-            pltpu.VMEM((tokens, columns), jnp.float32),
-            pltpu.SemaphoreType.DMA((SIDE,)),
+            pltpu.VMEM((2, tokens, depth), jnp.bfloat16),
+            pltpu.VMEM((tokens, columns), jnp.bfloat16),
+            pltpu.SemaphoreType.DMA((2,)),
+            pltpu.SemaphoreType.DMA((2,)),
         ],
         compiler_params=params,
-        cost_estimate=cost(SIDE),
+        cost_estimate=cost(2),
         name="project_far",
-    )(in_vmem(total), in_vmem(weights), *far)
+    )(in_vmem(total), in_vmem(weights), far)
 
 
 def body(
@@ -367,8 +370,8 @@
     above_low = second_way(low, -1)
     far_low = second_way(below_low, 1)
     far_high = second_way(above_high, -1)
-    near = [low, high, below_low, below_high, above_low, above_high]
-    return project(near, [far_low, far_high], weight)
+    near = [low, high, below_low, below_high, above_low, above_high, far_low]
+    return project(near, far_high, weight)
 
 
 def solution(mesh):

time: 112 us -> 112 us (level)
    ppermute x6, waiting for transfers between devices: 10.8 us -> 19.5 us  [second_way(): return lax.ppermute(value, ('chan', 'stretch'), moves(by, 1))]
    all_gather x1, waiting for transfers between devices: 10.2 us -> 5.45 us  [body(): weight = lax.all_gather(out_weight, 'stretch', axis=0, tiled=True)]
    ppermute x3, waiting for transfers between devices: 8.28 us -> 4.1 us  [first_way(): return lax.ppermute(value, ('chan', 'stretch'), moves(by, 0))]
  transfers between devices with their start and end apart: 11 -> 11, of which waited for: 5 -> 7; matrix products, arithmetic and copies ran while one was open for 2% -> 2% of each run, Pallas kernels for 24% -> 24%
where the time goes in v4:
time: 112 us; the launch traced here: 111 us
  starting transfers between devices  35.7 us (32%)
  waiting for transfers between devices  29.8 us (27%)
  Pallas kernels  29.3 us (26%)
  between operations  13.6 us (12%)
  other arithmetic  1.84 us (2%)
    ppermute x6, starting transfers between devices, second_way(): return lax.ppermute(value, ('chan', 'stretch'), moves(by, 1))  20.6 us
    ppermute x6, waiting for transfers between devices, second_way(): return lax.ppermute(value, ('chan', 'stretch'), moves(by, 1))  19.5 us
    pallas_call x2, Pallas kernels, gate(): pl.pallas_call(functools.partial(filter_kernel, late), grid=(channels //...  17.3 us
    ppermute x3, starting transfers between devices, first_way(): return lax.ppermute(value, ('chan', 'stretch'), moves(by, 0))  10.1 us
    pallas_call x1, Pallas kernels, project(): pl.pallas_call(near_kernel, out_shape=[pltpu.VMEM((tokens, columns), jnp....  6.94 us
    all_gather x1, waiting for transfers between devices, body(): weight = lax.all_gather(out_weight, 'stretch', axis=0, tiled=True)  5.45 us
    ppermute x1, starting transfers between devices, body(): lax.ppermute(pack, 'stretch', [(i, i + 1) for i in range(devices - 1)])  4.94 us
    ppermute x3, waiting for transfers between devices, first_way(): return lax.ppermute(value, ('chan', 'stretch'), moves(by, 0))  4.1 us
  transfers between devices with their start and end apart: 11, of which 7 were waited for; matrix products, arithmetic and copies ran while one was open for 2% of the time, Pallas kernels for 24%

profile of v4, /device:TPU:1, one launch (start us, length us, event | category | flops | bytes accessed | tf_op | source)
XLA Modules:
  0.0 111.1 jit_solution(15612588037274972962)
XLA Ops:
  6.5 0.0 copy-start.4
  6.5 0.0 all-gather.2.cloned.1.call-start
  6.5 0.7 all-gather.2.cloned.1.call-update
  7.3 2.4 %pack_tail.1 = bf16[320,512]{1,0:T(8,128)(2,1)} custom-call(bf16[512,512]{1,0:T(8,128)(2,1)} %refs_4_.3, bf16[512,512]{1,0:T(8,128)(2,1)} %refs_5_.3, bf16[512,512]{1,0:T(8,128)(2,1)} %refs_3_.1, s32[4,128]{1,0:T(4,128)} %bitcast.13), custom_call_target="tpu_custom_call" | custom-call | bytes 700000 | tf_op jit(solution)/shard_map/pack_tail/pallas_call | solution.py:175
  9.7 4.9 %collective-permute-start = (bf16[320,512]{1,0:T(8,128)(2,1)}, bf16[320,512]{1,0:T(8,128)(2,1)S(1)}, u32[]{:S(2)}, u32[]{:S(2)}) collective-permute-start(bf16[320,512]{1,0:T(8,128)(2,1)} %pack_tail.1), channel_id=1, source_target_pairs={{0,1},{1,2},{2,3},{3,4},{4,5},{5,6},{6,7},{7,8},{8,9},{9,10},{10,1... | collective-permute-start | bytes 983048 | tf_op jit(solution)/shard_map/ppermute | solution.py:362
  14.6 8.6 %gate_late.1.refs_0_ = bf16[512,512]{1,0:T(8,128)(2,1)} custom-call(bf16[512,512]{1,0:T(8,128)(2,1)} %refs_3_.1, bf16[512,512]{1,0:T(8,128)(2,1)} %refs_4_.3, bf16[512,512]{1,0:T(8,128)(2,1)} %refs_5_.3, s32[4,128]{1,0:T(4,128)} %bitcast.14, f32[3,7,512]{2,1,0:T(8,128)} %refs_7_.1, f32[128,512]{1,0:T(8,128)} %refs_8_.1, f32[1,512]{1,0:T(1,128)} %bitcast.16, ...), custom_call_target="tpu_custom_call" | custom-call | flops 134217728 | bytes 2097152 | tf_op jit(solution)/shard_map/gate_late/pallas_call | solution.py:204
  23.2 0.0 collective-permute-done.refs_1_.refs_2_
  23.3 0.0 copy-start.2
  23.3 0.7 copy-done.2
  24.0 8.7 %gate_early.1 = bf16[512,512]{1,0:T(8,128)(2,1)} custom-call(bf16[512,512]{1,0:T(8,128)(2,1)} %gate_late.1.refs_0_, bf16[320,512]{1,0:T(8,128)(2,1)} %copy-done.2, bf16[320,512]{1,0:T(8,128)(2,1)} %copy-done.2, bf16[512,512]{1,0:T(8,128)(2,1)} %refs_3_.1, bf16[512,512]{1,0:T(8,128)(2,1)} %refs_4_.3, ...), custom_call_target="tpu_custom_call", output_to_operand_aliasing={{}: (0, {})} | custom-call | flops 134217728 | bytes 2097152 | tf_op jit(solution)/shard_map/gate_early/pallas_call | solution.py:204
  32.7 3.2 %collective-permute-start.1 = (bf16[512,512]{1,0:T(8,128)(2,1)}, bf16[512,512]{1,0:T(8,128)(2,1)S(1)}, u32[]{:S(2)}, u32[]{:S(2)}) collective-permute-start(bf16[512,512]{1,0:T(8,128)(2,1)} %gate_early.1), channel_id=1, source_target_pairs={{0,32},{1,129},{2,34},{3,131},{4,36},{5,133},{6,38},{7,135},{8,40}... | collective-permute-start | bytes 1572872 | tf_op jit(solution)/shard_map/ppermute | solution.py:25
  35.9 3.4 %collective-permute-start.2 = (bf16[512,512]{1,0:T(8,128)(2,1)}, bf16[512,512]{1,0:T(8,128)(2,1)S(1)}, u32[]{:S(2)}, u32[]{:S(2)}) collective-permute-start(bf16[512,512]{1,0:T(8,128)(2,1)} %gate_early.1), channel_id=1, source_target_pairs={{0,96},{1,385},{2,98},{3,387},{4,100},{5,389},{6,102},{7,391},{8,1... | collective-permute-start | bytes 1572872 | tf_op jit(solution)/shard_map/ppermute | solution.py:25
  39.2 3.5 %collective-permute-start.3 = (bf16[512,512]{1,0:T(8,128)(2,1)}, bf16[512,512]{1,0:T(8,128)(2,1)S(1)}, u32[]{:S(2)}, u32[]{:S(2)}) collective-permute-start(bf16[512,512]{1,0:T(8,128)(2,1)} %gate_early.1), channel_id=1, source_target_pairs={{0,64},{1,257},{2,66},{3,259},{4,68},{5,261},{6,70},{7,263},{8,72}... | collective-permute-start | bytes 1572872 | tf_op jit(solution)/shard_map/ppermute | solution.py:25
  42.8 1.7 %collective-permute-done.1 = bf16[512,512]{1,0:T(8,128)(2,1)S(1)} collective-permute-done((bf16[512,512]{1,0:T(8,128)(2,1)}, bf16[512,512]{1,0:T(8,128)(2,1)S(1)}, u32[]{:S(2)}, u32[]{:S(2)}) %collective-permute-start.1) | collective-permute-done | bytes 524320 | tf_op jit(solution)/shard_map/ppermute | solution.py:25
  44.5 1.1 %pad_maximum_fusion.refs_0_ = bf16[2,512,512]{2,1,0:T(8,128)(2,1)S(1)} fusion(bf16[1,512,512]{2,1,0:T(8,128)(2,1)S(1)} %bitcast.12, bf16[1,512,512]{2,1,0:T(8,128)(2,1)} %bitcast.9), kind=kLoop, calls=%fused_computation | loop fusion | flops 524288 | bytes 2097152 | tf_op jit(solution)/shard_map/stack | solution.py:366
  45.6 0.0 copy-start
  45.6 3.1 %collective-permute-start.4 = (bf16[2,512,512]{2,1,0:T(8,128)(2,1)S(1)}, bf16[2,512,512]{2,1,0:T(8,128)(2,1)S(1)}, u32[]{:S(2)}, u32[]{:S(2)}) collective-permute-start(bf16[2,512,512]{2,1,0:T(8,128)(2,1)S(1)} %pad_maximum_fusion.refs_0_), channel_id=1, source_target_pairs={{0,128},{1,33},{2,130},{3,35},{4,132},{5,37},{6,134},{7,39},{8,136... | collective-permute-start | bytes 3145736 | tf_op jit(solution)/shard_map/ppermute | solution.py:29
  48.8 0.0 collective-permute-done.2
  48.8 2.4 %collective-permute-done.3 = bf16[512,512]{1,0:T(8,128)(2,1)S(1)} collective-permute-done((bf16[512,512]{1,0:T(8,128)(2,1)}, bf16[512,512]{1,0:T(8,128)(2,1)S(1)}, u32[]{:S(2)}, u32[]{:S(2)}) %collective-permute-start.3) | collective-permute-done | bytes 524320 | tf_op jit(solution)/shard_map/ppermute | solution.py:25
  51.2 0.1 pad_maximum_fusion.1.refs_1_
  51.3 0.0 copy-start.1
  51.3 4.5 %collective-permute-start.7 = (bf16[2,512,512]{2,1,0:T(8,128)(2,1)S(1)}, bf16[2,512,512]{2,1,0:T(8,128)(2,1)}, u32[]{:S(2)}, u32[]{:S(2)}) collective-permute-start(bf16[2,512,512]{2,1,0:T(8,128)(2,1)S(1)} %pad_maximum_fusion.1.refs_1_), channel_id=1, source_target_pairs={{0,384},{1,97},{2,386},{3,99},{4,388},{5,101},{6,390},{7,103},{8,3... | collective-permute-start | bytes 3145736 | tf_op jit(solution)/shard_map/ppermute | solution.py:29
  55.8 1.9 %collective-permute-start.5 = (bf16[2,512,512]{2,1,0:T(8,128)(2,1)S(1)}, bf16[2,512,512]{2,1,0:T(8,128)(2,1)}, u32[]{:S(2)}, u32[]{:S(2)}) collective-permute-start(bf16[2,512,512]{2,1,0:T(8,128)(2,1)S(1)} %pad_maximum_fusion.1.refs_1_), channel_id=1, source_target_pairs={{0,128},{1,33},{2,130},{3,35},{4,132},{5,37},{6,134},{7,39},{8,136... | collective-permute-start | bytes 3145736 | tf_op jit(solution)/shard_map/ppermute | solution.py:29
  57.8 4.6 %collective-permute-start.6 = (bf16[2,512,512]{2,1,0:T(8,128)(2,1)S(1)}, bf16[2,512,512]{2,1,0:T(8,128)(2,1)}, u32[]{:S(2)}, u32[]{:S(2)}) collective-permute-start(bf16[2,512,512]{2,1,0:T(8,128)(2,1)S(1)} %pad_maximum_fusion.refs_0_), channel_id=1, source_target_pairs={{0,384},{1,97},{2,386},{3,99},{4,388},{5,101},{6,390},{7,103},{8,3... | collective-permute-start | bytes 3145736 | tf_op jit(solution)/shard_map/ppermute | solution.py:29
  62.3 4.4 %collective-permute-done.4.refs_2_ = bf16[2,512,512]{2,1,0:T(8,128)(2,1)S(1)} collective-permute-done((bf16[2,512,512]{2,1,0:T(8,128)(2,1)S(1)}, bf16[2,512,512]{2,1,0:T(8,128)(2,1)S(1)}, u32[]{:S(2)}, u32[]{:S(2)}) %collective-permute-start.4) | collective-permute-done | bytes 1048608 | tf_op jit(solution)/shard_map/ppermute | solution.py:29
  66.7 0.0 copy-start.3
  66.7 1.9 %collective-permute-start.8 = (bf16[2,512,512]{2,1,0:T(8,128)(2,1)S(1)}, bf16[2,512,512]{2,1,0:T(8,128)(2,1)}, u32[]{:S(2)}, u32[]{:S(2)}) collective-permute-start(bf16[2,512,512]{2,1,0:T(8,128)(2,1)S(1)} %collective-permute-done.4.refs_2_), channel_id=1, source_target_pairs={{0,128},{1,33},{2,130},{3,35},{4,132},{5,37},{6,134},{7,39},{8,136... | collective-permute-start | bytes 3145736 | tf_op jit(solution)/shard_map/ppermute | solution.py:29
  68.6 0.0 collective-permute-done.7.refs_5_
  68.7 4.6 %collective-permute-start.9 = (bf16[2,512,512]{2,1,0:T(8,128)(2,1)}, bf16[2,512,512]{2,1,0:T(8,128)(2,1)}, u32[]{:S(2)}, u32[]{:S(2)}) collective-permute-start(bf16[2,512,512]{2,1,0:T(8,128)(2,1)} %collective-permute-done.7.refs_5_), channel_id=1, source_target_pairs={{0,384},{1,97},{2,386},{3,99},{4,388},{5,101},{6,390},{7,103},{8,3... | collective-permute-start | bytes 3145736 | tf_op jit(solution)/shard_map/ppermute | solution.py:29
  73.3 0.0 copy-done.4
  73.3 0.1 add_add_fusion
  73.3 0.1 add.51
  73.4 0.1 add.57
  73.5 0.5 fusion.places
  74.0 3.9 %collective-permute-done.5.refs_3_ = bf16[2,512,512]{2,1,0:T(8,128)(2,1)} collective-permute-done((bf16[2,512,512]{2,1,0:T(8,128)(2,1)S(1)}, bf16[2,512,512]{2,1,0:T(8,128)(2,1)}, u32[]{:S(2)}, u32[]{:S(2)}) %collective-permute-start.5) | collective-permute-done | bytes 1048608 | tf_op jit(solution)/shard_map/ppermute | solution.py:29
  78.0 0.8 collective-permute-done.6.refs_4_
  78.8 10.4 %collective-permute-done.8.refs_6_ = bf16[2,512,512]{2,1,0:T(8,128)(2,1)} collective-permute-done((bf16[2,512,512]{2,1,0:T(8,128)(2,1)S(1)}, bf16[2,512,512]{2,1,0:T(8,128)(2,1)}, u32[]{:S(2)}, u32[]{:S(2)}) %collective-permute-start.8) | collective-permute-done | bytes 1048608 | tf_op jit(solution)/shard_map/ppermute | solution.py:29
  89.2 5.5 %all-gather.2.cloned.1.call-done = bf16[8192,512]{1,0:T(8,128)(2,1)} async-done(((bf16[256,512]{1,0:T(8,128)(2,1)}), bf16[8192,512]{1,0:T(8,128)(2,1)}) %all-gather.2.cloned.1.call-update) | async-done | bytes 8388624 | tf_op jit(solution)/shard_map/all_gather | solution.py:349
  94.6 0.0 copy-done
  94.6 0.0 copy-done.1
  94.7 0.0 copy-done.3
  94.7 6.9 %project_near.1 = (f32[512,512]{1,0:T(8,128)S(1)}, bf16[2,512,512]{2,1,0:T(8,128)(2,1)S(1)}) custom-call(s32[16]{0:T(128)} %fusion.places, bf16[2,512,512]{2,1,0:T(8,128)(2,1)} %copy-done, bf16[2,512,512]{2,1,0:T(8,128)(2,1)} %copy-done.1, bf16[2,512,512]{2,1,0:T(8,128)(2,1)} %copy-done.3, bf16[2,512,512]{2,1,0:T(8,128)(2,1)} %collective-permute-done.5.refs_3_, ...), custom_call_target="tpu_custom_call" | custom-call | flops 3758096384 | bytes 14680064 | tf_op jit(solution)/shard_map/project_near/pallas_call | solution.py:302
  101.6 0.0 collective-permute-done.9.panel
  101.6 2.6 %project_far.1 = bf16[512,512]{1,0:T(8,128)(2,1)} custom-call(f32[512,512]{1,0:T(8,128)S(1)} %get-tuple-element.7.total, bf16[2,512,512]{2,1,0:T(8,128)(2,1)S(1)} %get-tuple-element.8.weights, bf16[2,512,512]{2,1,0:T(8,128)(2,1)} %collective-permute-done.9.panel), custom_call_target="tpu_custom_call" | custom-call | flops 536870912 | bytes 2097152 | tf_op jit(solution)/shard_map/project_far/pallas_call | solution.py:321
Async XLA Ops:
  6.5 66.7 %copy-start.4 = (s32[4]{0:T(128)S(1)}, s32[4]{0:T(128)}, u32[]{:S(2)}) copy-start(s32[4]{0:T(128)} %constant.60.clone) | copy-start | bytes 52
  6.5 88.1 %all-gather.2.cloned.1.call-start = ((), (), s32[]{:S(2)}) async-start(), calls=%async_computation | async-start | bytes 8650752 | tf_op jit(solution)/shard_map/all_gather | solution.py:349
  9.7 13.6 %collective-permute-start = (bf16[320,512]{1,0:T(8,128)(2,1)}, bf16[320,512]{1,0:T(8,128)(2,1)S(1)}, u32[]{:S(2)}, u32[]{:S(2)}) collective-permute-start(bf16[320,512]{1,0:T(8,128)(2,1)} %pack_tail.1), channel_id=1, source_target_pairs={{0,1},{1,2},{2,3},{3,4},{4,5},{5,6},{6,7},{7,8},{8,9},{9,10},{10,1... | collective-permute-start | bytes 983048 | tf_op jit(solution)/shard_map/ppermute | solution.py:362
  23.3 0.7 copy-start.2
  32.7 11.8 %collective-permute-start.1 = (bf16[512,512]{1,0:T(8,128)(2,1)}, bf16[512,512]{1,0:T(8,128)(2,1)S(1)}, u32[]{:S(2)}, u32[]{:S(2)}) collective-permute-start(bf16[512,512]{1,0:T(8,128)(2,1)} %gate_early.1), channel_id=1, source_target_pairs={{0,32},{1,129},{2,34},{3,131},{4,36},{5,133},{6,38},{7,135},{8,40}... | collective-permute-start | bytes 1572872 | tf_op jit(solution)/shard_map/ppermute | solution.py:25
  35.9 12.9 %collective-permute-start.2 = (bf16[512,512]{1,0:T(8,128)(2,1)}, bf16[512,512]{1,0:T(8,128)(2,1)S(1)}, u32[]{:S(2)}, u32[]{:S(2)}) collective-permute-start(bf16[512,512]{1,0:T(8,128)(2,1)} %gate_early.1), channel_id=1, source_target_pairs={{0,96},{1,385},{2,98},{3,387},{4,100},{5,389},{6,102},{7,391},{8,1... | collective-permute-start | bytes 1572872 | tf_op jit(solution)/shard_map/ppermute | solution.py:25
  39.2 11.9 %collective-permute-start.3 = (bf16[512,512]{1,0:T(8,128)(2,1)}, bf16[512,512]{1,0:T(8,128)(2,1)S(1)}, u32[]{:S(2)}, u32[]{:S(2)}) collective-permute-start(bf16[512,512]{1,0:T(8,128)(2,1)} %gate_early.1), channel_id=1, source_target_pairs={{0,64},{1,257},{2,66},{3,259},{4,68},{5,261},{6,70},{7,263},{8,72}... | collective-permute-start | bytes 1572872 | tf_op jit(solution)/shard_map/ppermute | solution.py:25
  45.6 49.0 %copy-start = (bf16[2,512,512]{2,1,0:T(8,128)(2,1)}, bf16[2,512,512]{2,1,0:T(8,128)(2,1)S(1)}, u32[]{:S(2)}) copy-start(bf16[2,512,512]{2,1,0:T(8,128)(2,1)S(1)} %pad_maximum_fusion.refs_0_) | copy-start | bytes 3145732
  45.6 21.1 %collective-permute-start.4 = (bf16[2,512,512]{2,1,0:T(8,128)(2,1)S(1)}, bf16[2,512,512]{2,1,0:T(8,128)(2,1)S(1)}, u32[]{:S(2)}, u32[]{:S(2)}) collective-permute-start(bf16[2,512,512]{2,1,0:T(8,128)(2,1)S(1)} %pad_maximum_fusion.refs_0_), channel_id=1, source_target_pairs={{0,128},{1,33},{2,130},{3,35},{4,132},{5,37},{6,134},{7,39},{8,136... | collective-permute-start | bytes 3145736 | tf_op jit(solution)/shard_map/ppermute | solution.py:29
  51.3 43.4 %copy-start.1 = (bf16[2,512,512]{2,1,0:T(8,128)(2,1)}, bf16[2,512,512]{2,1,0:T(8,128)(2,1)S(1)}, u32[]{:S(2)}) copy-start(bf16[2,512,512]{2,1,0:T(8,128)(2,1)S(1)} %pad_maximum_fusion.1.refs_1_) | copy-start | bytes 3145732
  51.3 17.4 %collective-permute-start.7 = (bf16[2,512,512]{2,1,0:T(8,128)(2,1)S(1)}, bf16[2,512,512]{2,1,0:T(8,128)(2,1)}, u32[]{:S(2)}, u32[]{:S(2)}) collective-permute-start(bf16[2,512,512]{2,1,0:T(8,128)(2,1)S(1)} %pad_maximum_fusion.1.refs_1_), channel_id=1, source_target_pairs={{0,384},{1,97},{2,386},{3,99},{4,388},{5,101},{6,390},{7,103},{8,3... | collective-permute-start | bytes 3145736 | tf_op jit(solution)/shard_map/ppermute | solution.py:29
  55.8 22.1 %collective-permute-start.5 = (bf16[2,512,512]{2,1,0:T(8,128)(2,1)S(1)}, bf16[2,512,512]{2,1,0:T(8,128)(2,1)}, u32[]{:S(2)}, u32[]{:S(2)}) collective-permute-start(bf16[2,512,512]{2,1,0:T(8,128)(2,1)S(1)} %pad_maximum_fusion.1.refs_1_), channel_id=1, source_target_pairs={{0,128},{1,33},{2,130},{3,35},{4,132},{5,37},{6,134},{7,39},{8,136... | collective-permute-start | bytes 3145736 | tf_op jit(solution)/shard_map/ppermute | solution.py:29
  57.8 21.0 %collective-permute-start.6 = (bf16[2,512,512]{2,1,0:T(8,128)(2,1)S(1)}, bf16[2,512,512]{2,1,0:T(8,128)(2,1)}, u32[]{:S(2)}, u32[]{:S(2)}) collective-permute-start(bf16[2,512,512]{2,1,0:T(8,128)(2,1)S(1)} %pad_maximum_fusion.refs_0_), channel_id=1, source_target_pairs={{0,384},{1,97},{2,386},{3,99},{4,388},{5,101},{6,390},{7,103},{8,3... | collective-permute-start | bytes 3145736 | tf_op jit(solution)/shard_map/ppermute | solution.py:29
  66.7 27.9 %copy-start.3 = (bf16[2,512,512]{2,1,0:T(8,128)(2,1)}, bf16[2,512,512]{2,1,0:T(8,128)(2,1)S(1)}, u32[]{:S(2)}) copy-start(bf16[2,512,512]{2,1,0:T(8,128)(2,1)S(1)} %collective-permute-done.4.refs_2_) | copy-start | bytes 3145732
  66.7 22.5 %collective-permute-start.8 = (bf16[2,512,512]{2,1,0:T(8,128)(2,1)S(1)}, bf16[2,512,512]{2,1,0:T(8,128)(2,1)}, u32[]{:S(2)}, u32[]{:S(2)}) collective-permute-start(bf16[2,512,512]{2,1,0:T(8,128)(2,1)S(1)} %collective-permute-done.4.refs_2_), channel_id=1, source_target_pairs={{0,128},{1,33},{2,130},{3,35},{4,132},{5,37},{6,134},{7,39},{8,136... | collective-permute-start | bytes 3145736 | tf_op jit(solution)/shard_map/ppermute | solution.py:29
  68.7 32.9 %collective-permute-start.9 = (bf16[2,512,512]{2,1,0:T(8,128)(2,1)}, bf16[2,512,512]{2,1,0:T(8,128)(2,1)}, u32[]{:S(2)}, u32[]{:S(2)}) collective-permute-start(bf16[2,512,512]{2,1,0:T(8,128)(2,1)} %collective-permute-done.7.refs_5_), channel_id=1, source_target_pairs={{0,384},{1,97},{2,386},{3,99},{4,388},{5,101},{6,390},{7,103},{8,3... | collective-permute-start | bytes 3145736 | tf_op jit(solution)/shard_map/ppermute | solution.py:29
Sparse Core Ops, SparseCore 0:
  9.5 85.1 all-gather.1

commit v5 on v4

--- a/solution.py
+++ b/solution.py
@@ -261,15 +261,22 @@
 
 
 def far_kernel(total, weights, panel, out_ref, blocks, rounded, sem, out_sem):
-    copies = [pltpu.make_async_copy(panel.at[i], blocks.at[i], sem.at[i]) for i in range(2)]
-    for copy in copies:
-        copy.start()
-    for copy in copies:
-        copy.wait()
     tokens = total.shape[0]
+    halves = [slice(tokens // 2 * half, tokens // 2 * (half + 1)) for half in range(2)]
+    copies = [
+        [
+            pltpu.make_async_copy(panel.at[i, rows], blocks.at[i, rows], sem.at[2 * half + i])
+            for i in range(2)
+        ]
+        for half, rows in enumerate(halves)
+    ]
+    for pair in copies:
+        for copy in pair:
+            copy.start()
     gives = []
-    for half in range(2):
-        rows = slice(tokens // 2 * half, tokens // 2 * (half + 1))
+    for half, rows in enumerate(halves):
+        for copy in copies[half]:
+            copy.wait()
         summed = total[rows]
         for i in range(2):
             summed += jnp.dot(blocks[i, rows], weights[i], preferred_element_type=jnp.float32)
@@ -326,7 +333,7 @@
         scratch_shapes=[
             pltpu.VMEM((2, tokens, depth), jnp.bfloat16),
             pltpu.VMEM((tokens, columns), jnp.bfloat16),
-            pltpu.SemaphoreType.DMA((2,)),
+            pltpu.SemaphoreType.DMA((4,)),
             pltpu.SemaphoreType.DMA((2,)),
         ],
         compiler_params=params,

time: 112 us -> 112 us (level)
  no operation moved by 1% of the time
where the time goes in v5:
time: 112 us; the launch traced here: 111 us
  starting transfers between devices  35.7 us (32%)
  waiting for transfers between devices  29.8 us (27%)
  Pallas kernels  29.3 us (26%)
  between operations  13.6 us (12%)
  other arithmetic  1.84 us (2%)
    ppermute x6, starting transfers between devices, second_way(): return lax.ppermute(value, ('chan', 'stretch'), moves(by, 1))  20.6 us
    ppermute x6, waiting for transfers between devices, second_way(): return lax.ppermute(value, ('chan', 'stretch'), moves(by, 1))  19.5 us
    pallas_call x2, Pallas kernels, gate(): pl.pallas_call(functools.partial(filter_kernel, late), grid=(channels //...  17.3 us
    ppermute x3, starting transfers between devices, first_way(): return lax.ppermute(value, ('chan', 'stretch'), moves(by, 0))  10.1 us
    pallas_call x1, Pallas kernels, project(): pl.pallas_call(near_kernel, out_shape=[pltpu.VMEM((tokens, columns), jnp....  6.94 us
    all_gather x1, waiting for transfers between devices, body(): weight = lax.all_gather(out_weight, 'stretch', axis=0, tiled=True)  5.45 us
    ppermute x1, starting transfers between devices, body(): lax.ppermute(pack, 'stretch', [(i, i + 1) for i in range(devices - 1)])  4.94 us
    ppermute x3, waiting for transfers between devices, first_way(): return lax.ppermute(value, ('chan', 'stretch'), moves(by, 0))  4.1 us
  transfers between devices with their start and end apart: 11, of which 7 were waited for; matrix products, arithmetic and copies ran while one was open for 2% of the time, Pallas kernels for 24%

profile of v5, /device:TPU:1, one launch (start us, length us, event | category | flops | bytes accessed | tf_op | source)
XLA Modules:
  0.0 111.1 jit_solution(822496493636976383)
XLA Ops:
  6.5 0.0 copy-start.4
  6.5 0.0 all-gather.2.cloned.1.call-start
  6.5 0.7 all-gather.2.cloned.1.call-update
  7.3 2.4 %pack_tail.1 = bf16[320,512]{1,0:T(8,128)(2,1)} custom-call(bf16[512,512]{1,0:T(8,128)(2,1)} %refs_4_.3, bf16[512,512]{1,0:T(8,128)(2,1)} %refs_5_.3, bf16[512,512]{1,0:T(8,128)(2,1)} %refs_3_.1, s32[4,128]{1,0:T(4,128)} %bitcast.13), custom_call_target="tpu_custom_call" | custom-call | bytes 700000 | tf_op jit(solution)/shard_map/pack_tail/pallas_call | solution.py:175
  9.7 4.9 %collective-permute-start = (bf16[320,512]{1,0:T(8,128)(2,1)}, bf16[320,512]{1,0:T(8,128)(2,1)S(1)}, u32[]{:S(2)}, u32[]{:S(2)}) collective-permute-start(bf16[320,512]{1,0:T(8,128)(2,1)} %pack_tail.1), channel_id=1, source_target_pairs={{0,1},{1,2},{2,3},{3,4},{4,5},{5,6},{6,7},{7,8},{8,9},{9,10},{10,1... | collective-permute-start | bytes 983048 | tf_op jit(solution)/shard_map/ppermute | solution.py:369
  14.6 8.6 %gate_late.1.refs_0_ = bf16[512,512]{1,0:T(8,128)(2,1)} custom-call(bf16[512,512]{1,0:T(8,128)(2,1)} %refs_3_.1, bf16[512,512]{1,0:T(8,128)(2,1)} %refs_4_.3, bf16[512,512]{1,0:T(8,128)(2,1)} %refs_5_.3, s32[4,128]{1,0:T(4,128)} %bitcast.14, f32[3,7,512]{2,1,0:T(8,128)} %refs_7_.1, f32[128,512]{1,0:T(8,128)} %refs_8_.1, f32[1,512]{1,0:T(1,128)} %bitcast.16, ...), custom_call_target="tpu_custom_call" | custom-call | flops 134217728 | bytes 2097152 | tf_op jit(solution)/shard_map/gate_late/pallas_call | solution.py:204
  23.2 0.0 collective-permute-done.refs_1_.refs_2_
  23.3 0.0 copy-start.2
  23.3 0.7 copy-done.2
  24.0 8.7 %gate_early.1 = bf16[512,512]{1,0:T(8,128)(2,1)} custom-call(bf16[512,512]{1,0:T(8,128)(2,1)} %gate_late.1.refs_0_, bf16[320,512]{1,0:T(8,128)(2,1)} %copy-done.2, bf16[320,512]{1,0:T(8,128)(2,1)} %copy-done.2, bf16[512,512]{1,0:T(8,128)(2,1)} %refs_3_.1, bf16[512,512]{1,0:T(8,128)(2,1)} %refs_4_.3, ...), custom_call_target="tpu_custom_call", output_to_operand_aliasing={{}: (0, {})} | custom-call | flops 134217728 | bytes 2097152 | tf_op jit(solution)/shard_map/gate_early/pallas_call | solution.py:204
  32.7 3.2 %collective-permute-start.1 = (bf16[512,512]{1,0:T(8,128)(2,1)}, bf16[512,512]{1,0:T(8,128)(2,1)S(1)}, u32[]{:S(2)}, u32[]{:S(2)}) collective-permute-start(bf16[512,512]{1,0:T(8,128)(2,1)} %gate_early.1), channel_id=1, source_target_pairs={{0,32},{1,129},{2,34},{3,131},{4,36},{5,133},{6,38},{7,135},{8,40}... | collective-permute-start | bytes 1572872 | tf_op jit(solution)/shard_map/ppermute | solution.py:25
  35.9 3.4 %collective-permute-start.2 = (bf16[512,512]{1,0:T(8,128)(2,1)}, bf16[512,512]{1,0:T(8,128)(2,1)S(1)}, u32[]{:S(2)}, u32[]{:S(2)}) collective-permute-start(bf16[512,512]{1,0:T(8,128)(2,1)} %gate_early.1), channel_id=1, source_target_pairs={{0,96},{1,385},{2,98},{3,387},{4,100},{5,389},{6,102},{7,391},{8,1... | collective-permute-start | bytes 1572872 | tf_op jit(solution)/shard_map/ppermute | solution.py:25
  39.2 3.5 %collective-permute-start.3 = (bf16[512,512]{1,0:T(8,128)(2,1)}, bf16[512,512]{1,0:T(8,128)(2,1)S(1)}, u32[]{:S(2)}, u32[]{:S(2)}) collective-permute-start(bf16[512,512]{1,0:T(8,128)(2,1)} %gate_early.1), channel_id=1, source_target_pairs={{0,64},{1,257},{2,66},{3,259},{4,68},{5,261},{6,70},{7,263},{8,72}... | collective-permute-start | bytes 1572872 | tf_op jit(solution)/shard_map/ppermute | solution.py:25
  42.8 1.7 %collective-permute-done.1 = bf16[512,512]{1,0:T(8,128)(2,1)S(1)} collective-permute-done((bf16[512,512]{1,0:T(8,128)(2,1)}, bf16[512,512]{1,0:T(8,128)(2,1)S(1)}, u32[]{:S(2)}, u32[]{:S(2)}) %collective-permute-start.1) | collective-permute-done | bytes 524320 | tf_op jit(solution)/shard_map/ppermute | solution.py:25
  44.5 1.1 %pad_maximum_fusion.refs_0_ = bf16[2,512,512]{2,1,0:T(8,128)(2,1)S(1)} fusion(bf16[1,512,512]{2,1,0:T(8,128)(2,1)S(1)} %bitcast.12, bf16[1,512,512]{2,1,0:T(8,128)(2,1)} %bitcast.9), kind=kLoop, calls=%fused_computation | loop fusion | flops 524288 | bytes 2097152 | tf_op jit(solution)/shard_map/stack | solution.py:373
  45.6 0.0 copy-start
  45.6 3.1 %collective-permute-start.4 = (bf16[2,512,512]{2,1,0:T(8,128)(2,1)S(1)}, bf16[2,512,512]{2,1,0:T(8,128)(2,1)S(1)}, u32[]{:S(2)}, u32[]{:S(2)}) collective-permute-start(bf16[2,512,512]{2,1,0:T(8,128)(2,1)S(1)} %pad_maximum_fusion.refs_0_), channel_id=1, source_target_pairs={{0,128},{1,33},{2,130},{3,35},{4,132},{5,37},{6,134},{7,39},{8,136... | collective-permute-start | bytes 3145736 | tf_op jit(solution)/shard_map/ppermute | solution.py:29
  48.8 0.0 collective-permute-done.2
  48.8 2.4 %collective-permute-done.3 = bf16[512,512]{1,0:T(8,128)(2,1)S(1)} collective-permute-done((bf16[512,512]{1,0:T(8,128)(2,1)}, bf16[512,512]{1,0:T(8,128)(2,1)S(1)}, u32[]{:S(2)}, u32[]{:S(2)}) %collective-permute-start.3) | collective-permute-done | bytes 524320 | tf_op jit(solution)/shard_map/ppermute | solution.py:25
  51.2 0.1 pad_maximum_fusion.1.refs_1_
  51.3 0.0 copy-start.1
  51.3 4.5 %collective-permute-start.7 = (bf16[2,512,512]{2,1,0:T(8,128)(2,1)S(1)}, bf16[2,512,512]{2,1,0:T(8,128)(2,1)}, u32[]{:S(2)}, u32[]{:S(2)}) collective-permute-start(bf16[2,512,512]{2,1,0:T(8,128)(2,1)S(1)} %pad_maximum_fusion.1.refs_1_), channel_id=1, source_target_pairs={{0,384},{1,97},{2,386},{3,99},{4,388},{5,101},{6,390},{7,103},{8,3... | collective-permute-start | bytes 3145736 | tf_op jit(solution)/shard_map/ppermute | solution.py:29
  55.8 1.9 %collective-permute-start.5 = (bf16[2,512,512]{2,1,0:T(8,128)(2,1)S(1)}, bf16[2,512,512]{2,1,0:T(8,128)(2,1)}, u32[]{:S(2)}, u32[]{:S(2)}) collective-permute-start(bf16[2,512,512]{2,1,0:T(8,128)(2,1)S(1)} %pad_maximum_fusion.1.refs_1_), channel_id=1, source_target_pairs={{0,128},{1,33},{2,130},{3,35},{4,132},{5,37},{6,134},{7,39},{8,136... | collective-permute-start | bytes 3145736 | tf_op jit(solution)/shard_map/ppermute | solution.py:29
  57.8 4.6 %collective-permute-start.6 = (bf16[2,512,512]{2,1,0:T(8,128)(2,1)S(1)}, bf16[2,512,512]{2,1,0:T(8,128)(2,1)}, u32[]{:S(2)}, u32[]{:S(2)}) collective-permute-start(bf16[2,512,512]{2,1,0:T(8,128)(2,1)S(1)} %pad_maximum_fusion.refs_0_), channel_id=1, source_target_pairs={{0,384},{1,97},{2,386},{3,99},{4,388},{5,101},{6,390},{7,103},{8,3... | collective-permute-start | bytes 3145736 | tf_op jit(solution)/shard_map/ppermute | solution.py:29
  62.3 4.4 %collective-permute-done.4.refs_2_ = bf16[2,512,512]{2,1,0:T(8,128)(2,1)S(1)} collective-permute-done((bf16[2,512,512]{2,1,0:T(8,128)(2,1)S(1)}, bf16[2,512,512]{2,1,0:T(8,128)(2,1)S(1)}, u32[]{:S(2)}, u32[]{:S(2)}) %collective-permute-start.4) | collective-permute-done | bytes 1048608 | tf_op jit(solution)/shard_map/ppermute | solution.py:29
  66.7 0.0 copy-start.3
  66.7 1.9 %collective-permute-start.8 = (bf16[2,512,512]{2,1,0:T(8,128)(2,1)S(1)}, bf16[2,512,512]{2,1,0:T(8,128)(2,1)}, u32[]{:S(2)}, u32[]{:S(2)}) collective-permute-start(bf16[2,512,512]{2,1,0:T(8,128)(2,1)S(1)} %collective-permute-done.4.refs_2_), channel_id=1, source_target_pairs={{0,128},{1,33},{2,130},{3,35},{4,132},{5,37},{6,134},{7,39},{8,136... | collective-permute-start | bytes 3145736 | tf_op jit(solution)/shard_map/ppermute | solution.py:29
  68.6 0.0 collective-permute-done.7.refs_5_
  68.7 4.6 %collective-permute-start.9 = (bf16[2,512,512]{2,1,0:T(8,128)(2,1)}, bf16[2,512,512]{2,1,0:T(8,128)(2,1)}, u32[]{:S(2)}, u32[]{:S(2)}) collective-permute-start(bf16[2,512,512]{2,1,0:T(8,128)(2,1)} %collective-permute-done.7.refs_5_), channel_id=1, source_target_pairs={{0,384},{1,97},{2,386},{3,99},{4,388},{5,101},{6,390},{7,103},{8,3... | collective-permute-start | bytes 3145736 | tf_op jit(solution)/shard_map/ppermute | solution.py:29
  73.3 0.0 copy-done.4
  73.3 0.1 add_add_fusion
  73.3 0.1 add.51
  73.4 0.1 add.57
  73.5 0.5 fusion.places
  74.0 3.9 %collective-permute-done.5.refs_3_ = bf16[2,512,512]{2,1,0:T(8,128)(2,1)} collective-permute-done((bf16[2,512,512]{2,1,0:T(8,128)(2,1)S(1)}, bf16[2,512,512]{2,1,0:T(8,128)(2,1)}, u32[]{:S(2)}, u32[]{:S(2)}) %collective-permute-start.5) | collective-permute-done | bytes 1048608 | tf_op jit(solution)/shard_map/ppermute | solution.py:29
  78.0 0.8 collective-permute-done.6.refs_4_
  78.8 10.4 %collective-permute-done.8.refs_6_ = bf16[2,512,512]{2,1,0:T(8,128)(2,1)} collective-permute-done((bf16[2,512,512]{2,1,0:T(8,128)(2,1)S(1)}, bf16[2,512,512]{2,1,0:T(8,128)(2,1)}, u32[]{:S(2)}, u32[]{:S(2)}) %collective-permute-start.8) | collective-permute-done | bytes 1048608 | tf_op jit(solution)/shard_map/ppermute | solution.py:29
  89.2 5.5 %all-gather.2.cloned.1.call-done = bf16[8192,512]{1,0:T(8,128)(2,1)} async-done(((bf16[256,512]{1,0:T(8,128)(2,1)}), bf16[8192,512]{1,0:T(8,128)(2,1)}) %all-gather.2.cloned.1.call-update) | async-done | bytes 8388624 | tf_op jit(solution)/shard_map/all_gather | solution.py:356
  94.6 0.0 copy-done
  94.6 0.0 copy-done.1
  94.7 0.0 copy-done.3
  94.7 6.9 %project_near.1 = (f32[512,512]{1,0:T(8,128)S(1)}, bf16[2,512,512]{2,1,0:T(8,128)(2,1)S(1)}) custom-call(s32[16]{0:T(128)} %fusion.places, bf16[2,512,512]{2,1,0:T(8,128)(2,1)} %copy-done, bf16[2,512,512]{2,1,0:T(8,128)(2,1)} %copy-done.1, bf16[2,512,512]{2,1,0:T(8,128)(2,1)} %copy-done.3, bf16[2,512,512]{2,1,0:T(8,128)(2,1)} %collective-permute-done.5.refs_3_, ...), custom_call_target="tpu_custom_call" | custom-call | flops 3758096384 | bytes 14680064 | tf_op jit(solution)/shard_map/project_near/pallas_call | solution.py:309
  101.6 0.0 collective-permute-done.9.panel
  101.6 2.7 %project_far.1 = bf16[512,512]{1,0:T(8,128)(2,1)} custom-call(f32[512,512]{1,0:T(8,128)S(1)} %get-tuple-element.7.total, bf16[2,512,512]{2,1,0:T(8,128)(2,1)S(1)} %get-tuple-element.8.weights, bf16[2,512,512]{2,1,0:T(8,128)(2,1)} %collective-permute-done.9.panel), custom_call_target="tpu_custom_call" | custom-call | flops 536870912 | bytes 2097152 | tf_op jit(solution)/shard_map/project_far/pallas_call | solution.py:328
Async XLA Ops:
  6.5 66.7 %copy-start.4 = (s32[4]{0:T(128)S(1)}, s32[4]{0:T(128)}, u32[]{:S(2)}) copy-start(s32[4]{0:T(128)} %constant.60.clone) | copy-start | bytes 52
  6.5 88.1 %all-gather.2.cloned.1.call-start = ((), (), s32[]{:S(2)}) async-start(), calls=%async_computation | async-start | bytes 8650752 | tf_op jit(solution)/shard_map/all_gather | solution.py:356
  9.7 13.6 %collective-permute-start = (bf16[320,512]{1,0:T(8,128)(2,1)}, bf16[320,512]{1,0:T(8,128)(2,1)S(1)}, u32[]{:S(2)}, u32[]{:S(2)}) collective-permute-start(bf16[320,512]{1,0:T(8,128)(2,1)} %pack_tail.1), channel_id=1, source_target_pairs={{0,1},{1,2},{2,3},{3,4},{4,5},{5,6},{6,7},{7,8},{8,9},{9,10},{10,1... | collective-permute-start | bytes 983048 | tf_op jit(solution)/shard_map/ppermute | solution.py:369
  23.3 0.7 copy-start.2
  32.7 11.8 %collective-permute-start.1 = (bf16[512,512]{1,0:T(8,128)(2,1)}, bf16[512,512]{1,0:T(8,128)(2,1)S(1)}, u32[]{:S(2)}, u32[]{:S(2)}) collective-permute-start(bf16[512,512]{1,0:T(8,128)(2,1)} %gate_early.1), channel_id=1, source_target_pairs={{0,32},{1,129},{2,34},{3,131},{4,36},{5,133},{6,38},{7,135},{8,40}... | collective-permute-start | bytes 1572872 | tf_op jit(solution)/shard_map/ppermute | solution.py:25
  35.9 12.9 %collective-permute-start.2 = (bf16[512,512]{1,0:T(8,128)(2,1)}, bf16[512,512]{1,0:T(8,128)(2,1)S(1)}, u32[]{:S(2)}, u32[]{:S(2)}) collective-permute-start(bf16[512,512]{1,0:T(8,128)(2,1)} %gate_early.1), channel_id=1, source_target_pairs={{0,96},{1,385},{2,98},{3,387},{4,100},{5,389},{6,102},{7,391},{8,1... | collective-permute-start | bytes 1572872 | tf_op jit(solution)/shard_map/ppermute | solution.py:25
  39.2 11.9 %collective-permute-start.3 = (bf16[512,512]{1,0:T(8,128)(2,1)}, bf16[512,512]{1,0:T(8,128)(2,1)S(1)}, u32[]{:S(2)}, u32[]{:S(2)}) collective-permute-start(bf16[512,512]{1,0:T(8,128)(2,1)} %gate_early.1), channel_id=1, source_target_pairs={{0,64},{1,257},{2,66},{3,259},{4,68},{5,261},{6,70},{7,263},{8,72}... | collective-permute-start | bytes 1572872 | tf_op jit(solution)/shard_map/ppermute | solution.py:25
  45.6 49.0 %copy-start = (bf16[2,512,512]{2,1,0:T(8,128)(2,1)}, bf16[2,512,512]{2,1,0:T(8,128)(2,1)S(1)}, u32[]{:S(2)}) copy-start(bf16[2,512,512]{2,1,0:T(8,128)(2,1)S(1)} %pad_maximum_fusion.refs_0_) | copy-start | bytes 3145732
  45.6 21.1 %collective-permute-start.4 = (bf16[2,512,512]{2,1,0:T(8,128)(2,1)S(1)}, bf16[2,512,512]{2,1,0:T(8,128)(2,1)S(1)}, u32[]{:S(2)}, u32[]{:S(2)}) collective-permute-start(bf16[2,512,512]{2,1,0:T(8,128)(2,1)S(1)} %pad_maximum_fusion.refs_0_), channel_id=1, source_target_pairs={{0,128},{1,33},{2,130},{3,35},{4,132},{5,37},{6,134},{7,39},{8,136... | collective-permute-start | bytes 3145736 | tf_op jit(solution)/shard_map/ppermute | solution.py:29
  51.3 43.4 %copy-start.1 = (bf16[2,512,512]{2,1,0:T(8,128)(2,1)}, bf16[2,512,512]{2,1,0:T(8,128)(2,1)S(1)}, u32[]{:S(2)}) copy-start(bf16[2,512,512]{2,1,0:T(8,128)(2,1)S(1)} %pad_maximum_fusion.1.refs_1_) | copy-start | bytes 3145732
  51.3 17.4 %collective-permute-start.7 = (bf16[2,512,512]{2,1,0:T(8,128)(2,1)S(1)}, bf16[2,512,512]{2,1,0:T(8,128)(2,1)}, u32[]{:S(2)}, u32[]{:S(2)}) collective-permute-start(bf16[2,512,512]{2,1,0:T(8,128)(2,1)S(1)} %pad_maximum_fusion.1.refs_1_), channel_id=1, source_target_pairs={{0,384},{1,97},{2,386},{3,99},{4,388},{5,101},{6,390},{7,103},{8,3... | collective-permute-start | bytes 3145736 | tf_op jit(solution)/shard_map/ppermute | solution.py:29
  55.8 22.1 %collective-permute-start.5 = (bf16[2,512,512]{2,1,0:T(8,128)(2,1)S(1)}, bf16[2,512,512]{2,1,0:T(8,128)(2,1)}, u32[]{:S(2)}, u32[]{:S(2)}) collective-permute-start(bf16[2,512,512]{2,1,0:T(8,128)(2,1)S(1)} %pad_maximum_fusion.1.refs_1_), channel_id=1, source_target_pairs={{0,128},{1,33},{2,130},{3,35},{4,132},{5,37},{6,134},{7,39},{8,136... | collective-permute-start | bytes 3145736 | tf_op jit(solution)/shard_map/ppermute | solution.py:29
  57.8 21.0 %collective-permute-start.6 = (bf16[2,512,512]{2,1,0:T(8,128)(2,1)S(1)}, bf16[2,512,512]{2,1,0:T(8,128)(2,1)}, u32[]{:S(2)}, u32[]{:S(2)}) collective-permute-start(bf16[2,512,512]{2,1,0:T(8,128)(2,1)S(1)} %pad_maximum_fusion.refs_0_), channel_id=1, source_target_pairs={{0,384},{1,97},{2,386},{3,99},{4,388},{5,101},{6,390},{7,103},{8,3... | collective-permute-start | bytes 3145736 | tf_op jit(solution)/shard_map/ppermute | solution.py:29
  66.7 27.9 %copy-start.3 = (bf16[2,512,512]{2,1,0:T(8,128)(2,1)}, bf16[2,512,512]{2,1,0:T(8,128)(2,1)S(1)}, u32[]{:S(2)}) copy-start(bf16[2,512,512]{2,1,0:T(8,128)(2,1)S(1)} %collective-permute-done.4.refs_2_) | copy-start | bytes 3145732
  66.7 22.5 %collective-permute-start.8 = (bf16[2,512,512]{2,1,0:T(8,128)(2,1)S(1)}, bf16[2,512,512]{2,1,0:T(8,128)(2,1)}, u32[]{:S(2)}, u32[]{:S(2)}) collective-permute-start(bf16[2,512,512]{2,1,0:T(8,128)(2,1)S(1)} %collective-permute-done.4.refs_2_), channel_id=1, source_target_pairs={{0,128},{1,33},{2,130},{3,35},{4,132},{5,37},{6,134},{7,39},{8,136... | collective-permute-start | bytes 3145736 | tf_op jit(solution)/shard_map/ppermute | solution.py:29
  68.7 32.9 %collective-permute-start.9 = (bf16[2,512,512]{2,1,0:T(8,128)(2,1)}, bf16[2,512,512]{2,1,0:T(8,128)(2,1)}, u32[]{:S(2)}, u32[]{:S(2)}) collective-permute-start(bf16[2,512,512]{2,1,0:T(8,128)(2,1)} %collective-permute-done.7.refs_5_), channel_id=1, source_target_pairs={{0,384},{1,97},{2,386},{3,99},{4,388},{5,101},{6,390},{7,103},{8,3... | collective-permute-start | bytes 3145736 | tf_op jit(solution)/shard_map/ppermute | solution.py:29
Sparse Core Ops, SparseCore 0:
  9.5 85.1 all-gather.1

commit v6 on v4

--- a/solution.py
+++ b/solution.py
@@ -229,7 +229,7 @@
 def near_kernel(places, *refs):
     count = 2 * SIDE - 1
     panels = refs[:count]
-    weight, total, far_weights, blocks, weights, block_sem, weight_sem = refs[count:]
+    weight, total, blocks, weights, block_sem, weight_sem = refs[count:]
     near = 2 * count
     copies = []
     for at in range(near):
@@ -240,28 +240,22 @@
                 pltpu.make_async_copy(panel, blocks.at[at], block_sem.at[at]),
             )
         )
-    later = [
-        pltpu.make_async_copy(
-            weight.at[places[near + i]], far_weights.at[i], weight_sem.at[near + i]
-        )
-        for i in range(2)
-    ]
     for pair in copies:
         for copy in pair:
             copy.start()
-    for copy in later:
-        copy.start()
     for at in range(near):
         for copy in copies[at]:
             copy.wait()
         part = jnp.dot(blocks[at], weights[at], preferred_element_type=jnp.float32)
         total[...] = part if at == 0 else total[...] + part
-    for copy in later:
-        copy.wait()
-
-
-def far_kernel(total, weights, panel, out_ref, blocks, rounded, sem, out_sem):
-    copies = [pltpu.make_async_copy(panel.at[i], blocks.at[i], sem.at[i]) for i in range(2)]
+
+
+def far_kernel(places, total, panel, weight, out_ref, blocks, weights, rounded, sem, out_sem):
+    first = 4 * SIDE - 2
+    copies = [pltpu.make_async_copy(panel.at[i], blocks.at[i], sem.at[i]) for i in range(2)] + [
+        pltpu.make_async_copy(weight.at[places[first + i]], weights.at[i], sem.at[2 + i])
+        for i in range(2)
+    ]
     for copy in copies:
         copy.start()
     for copy in copies:
@@ -299,14 +293,13 @@
         flops=2 * tokens * blocks * depth * columns, bytes_accessed=blocks << 20, transcendentals=0
     )
     count = slots - 2
-    total, weights = pl.pallas_call(
+    places = places.astype(jnp.int32)
+    weight = weight.reshape(slots, depth, columns)
+    total = pl.pallas_call(
         near_kernel,
-        out_shape=[
-            pltpu.VMEM((tokens, columns), jnp.float32),
-            pltpu.VMEM((2, depth, columns), jnp.bfloat16),
-        ],
+        out_shape=pltpu.VMEM((tokens, columns), jnp.float32),
         in_specs=[pl.BlockSpec(memory_space=pltpu.SMEM)] + [hbm] * (len(near) + 1),
-        out_specs=[vmem, vmem],
+        out_specs=vmem,
         scratch_shapes=[
             pltpu.VMEM((count, tokens, depth), jnp.bfloat16),
             pltpu.VMEM((count, depth, columns), jnp.bfloat16),
@@ -316,23 +309,24 @@
         compiler_params=params,
         cost_estimate=cost(count),
         name="project_near",
-    )(places.astype(jnp.int32), *near, weight.reshape(slots, depth, columns))
+    )(places, *near, weight)
     in_vmem = lambda value: pltpu.with_memory_space_constraint(value, pltpu.VMEM)
     return pl.pallas_call(
         far_kernel,
         out_shape=jax.ShapeDtypeStruct((tokens, columns), jnp.bfloat16),
-        in_specs=[vmem, vmem, hbm],
+        in_specs=[pl.BlockSpec(memory_space=pltpu.SMEM), vmem, hbm, hbm],
         out_specs=hbm,
         scratch_shapes=[
             pltpu.VMEM((2, tokens, depth), jnp.bfloat16),
+            pltpu.VMEM((2, depth, columns), jnp.bfloat16),
             pltpu.VMEM((tokens, columns), jnp.bfloat16),
-            pltpu.SemaphoreType.DMA((2,)),
+            pltpu.SemaphoreType.DMA((4,)),
             pltpu.SemaphoreType.DMA((2,)),
         ],
         compiler_params=params,
         cost_estimate=cost(2),
         name="project_far",
-    )(in_vmem(total), in_vmem(weights), far)
+    )(places, in_vmem(total), far, weight)
 
 
 def body(

time: 112 us -> 113 us (level)
  waiting for transfers between devices: 29.8 us -> 26.9 us
  Pallas kernels: 29.3 us -> 31.3 us
  starting transfers between devices: 35.7 us -> 37.5 us
    ppermute x6, waiting for transfers between devices: 19.5 us -> 16.5 us  [second_way(): return lax.ppermute(value, ('chan', 'stretch'), moves(by, 1))]
    ppermute x6, starting transfers between devices: 20.6 us -> 22.5 us  [second_way(): return lax.ppermute(value, ('chan', 'stretch'), moves(by, 1))]
    pallas_call x2, Pallas kernels: 17.3 us -> 18.4 us  [gate(): pl.pallas_call(functools.partial(filter_kernel, late), grid=(channels //...]
  transfers between devices with their start and end apart: 11 -> 11, of which waited for: 7 -> 8; matrix products, arithmetic and copies ran while one was open for 2% -> 2% of each run, Pallas kernels for 24% -> 25%
where the time goes in v6:
time: 113 us; the launch traced here: 112 us
  starting transfers between devices  37.5 us (33%)
  Pallas kernels  31.3 us (28%)
  waiting for transfers between devices  26.9 us (24%)
  between operations  13.6 us (12%)
  other arithmetic  1.82 us (2%)
    ppermute x6, starting transfers between devices, second_way(): return lax.ppermute(value, ('chan', 'stretch'), moves(by, 1))  22.5 us
    pallas_call x2, Pallas kernels, gate(): pl.pallas_call(functools.partial(filter_kernel, late), grid=(channels //...  18.4 us
    ppermute x6, waiting for transfers between devices, second_way(): return lax.ppermute(value, ('chan', 'stretch'), moves(by, 1))  16.5 us
    ppermute x3, starting transfers between devices, first_way(): return lax.ppermute(value, ('chan', 'stretch'), moves(by, 0))  10.1 us
    pallas_call x1, Pallas kernels, project(): pl.pallas_call(near_kernel, out_shape=pltpu.VMEM((tokens, columns), jnp.f...  6.78 us
    all_gather x1, waiting for transfers between devices, body(): weight = lax.all_gather(out_weight, 'stretch', axis=0, tiled=True)  5.49 us
    ppermute x1, starting transfers between devices, body(): lax.ppermute(pack, 'stretch', [(i, i + 1) for i in range(devices - 1)])  4.94 us
    ppermute x3, waiting for transfers between devices, first_way(): return lax.ppermute(value, ('chan', 'stretch'), moves(by, 0))  4.18 us
  transfers between devices with their start and end apart: 11, of which 8 were waited for; matrix products, arithmetic and copies ran while one was open for 2% of the time, Pallas kernels for 25%

profile of v6, /device:TPU:1, one launch (start us, length us, event | category | flops | bytes accessed | tf_op | source)
XLA Modules:
  0.0 112.0 jit_solution(16193691244930398956)
XLA Ops:
  6.5 0.0 copy-start.4
  6.5 0.0 all-gather.2.cloned.1.call-start
  6.5 0.7 all-gather.2.cloned.1.call-update
  7.3 2.4 %pack_tail.1 = bf16[320,512]{1,0:T(8,128)(2,1)} custom-call(bf16[512,512]{1,0:T(8,128)(2,1)} %refs_4_.3, bf16[512,512]{1,0:T(8,128)(2,1)} %refs_5_.3, bf16[512,512]{1,0:T(8,128)(2,1)} %refs_3_.1, s32[4,128]{1,0:T(4,128)} %bitcast.14), custom_call_target="tpu_custom_call" | custom-call | bytes 700000 | tf_op jit(solution)/shard_map/pack_tail/pallas_call | solution.py:175
  9.7 4.9 %collective-permute-start = (bf16[320,512]{1,0:T(8,128)(2,1)}, bf16[320,512]{1,0:T(8,128)(2,1)S(1)}, u32[]{:S(2)}, u32[]{:S(2)}) collective-permute-start(bf16[320,512]{1,0:T(8,128)(2,1)} %pack_tail.1), channel_id=1, source_target_pairs={{0,1},{1,2},{2,3},{3,4},{4,5},{5,6},{6,7},{7,8},{8,9},{9,10},{10,1... | collective-permute-start | bytes 983048 | tf_op jit(solution)/shard_map/ppermute | solution.py:356
  14.6 8.6 %gate_late.1.refs_0_ = bf16[512,512]{1,0:T(8,128)(2,1)} custom-call(bf16[512,512]{1,0:T(8,128)(2,1)} %refs_3_.1, bf16[512,512]{1,0:T(8,128)(2,1)} %refs_4_.3, bf16[512,512]{1,0:T(8,128)(2,1)} %refs_5_.3, s32[4,128]{1,0:T(4,128)} %bitcast.15, f32[3,7,512]{2,1,0:T(8,128)} %refs_7_.1, f32[128,512]{1,0:T(8,128)} %refs_8_.1, f32[1,512]{1,0:T(1,128)} %bitcast.17, ...), custom_call_target="tpu_custom_call" | custom-call | flops 134217728 | bytes 2097152 | tf_op jit(solution)/shard_map/gate_late/pallas_call | solution.py:204
  23.3 0.0 collective-permute-done.refs_1_.refs_2_
  23.3 0.0 copy-start.2
  23.3 0.7 copy-done.2
  24.0 9.8 %gate_early.1 = bf16[512,512]{1,0:T(8,128)(2,1)} custom-call(bf16[512,512]{1,0:T(8,128)(2,1)} %gate_late.1.refs_0_, bf16[320,512]{1,0:T(8,128)(2,1)} %copy-done.2, bf16[320,512]{1,0:T(8,128)(2,1)} %copy-done.2, bf16[512,512]{1,0:T(8,128)(2,1)} %refs_3_.1, bf16[512,512]{1,0:T(8,128)(2,1)} %refs_4_.3, ...), custom_call_target="tpu_custom_call", output_to_operand_aliasing={{}: (0, {})} | custom-call | flops 134217728 | bytes 2097152 | tf_op jit(solution)/shard_map/gate_early/pallas_call | solution.py:204
  33.8 3.2 %collective-permute-start.1 = (bf16[512,512]{1,0:T(8,128)(2,1)}, bf16[512,512]{1,0:T(8,128)(2,1)S(1)}, u32[]{:S(2)}, u32[]{:S(2)}) collective-permute-start(bf16[512,512]{1,0:T(8,128)(2,1)} %gate_early.1), channel_id=1, source_target_pairs={{0,32},{1,129},{2,34},{3,131},{4,36},{5,133},{6,38},{7,135},{8,40}... | collective-permute-start | bytes 1572872 | tf_op jit(solution)/shard_map/ppermute | solution.py:25
  37.0 3.4 %collective-permute-start.2 = (bf16[512,512]{1,0:T(8,128)(2,1)}, bf16[512,512]{1,0:T(8,128)(2,1)S(1)}, u32[]{:S(2)}, u32[]{:S(2)}) collective-permute-start(bf16[512,512]{1,0:T(8,128)(2,1)} %gate_early.1), channel_id=1, source_target_pairs={{0,96},{1,385},{2,98},{3,387},{4,100},{5,389},{6,102},{7,391},{8,1... | collective-permute-start | bytes 1572872 | tf_op jit(solution)/shard_map/ppermute | solution.py:25
  40.4 3.5 %collective-permute-start.3 = (bf16[512,512]{1,0:T(8,128)(2,1)}, bf16[512,512]{1,0:T(8,128)(2,1)S(1)}, u32[]{:S(2)}, u32[]{:S(2)}) collective-permute-start(bf16[512,512]{1,0:T(8,128)(2,1)} %gate_early.1), channel_id=1, source_target_pairs={{0,64},{1,257},{2,66},{3,259},{4,68},{5,261},{6,70},{7,263},{8,72}... | collective-permute-start | bytes 1572872 | tf_op jit(solution)/shard_map/ppermute | solution.py:25
  43.9 1.7 %collective-permute-done.1 = bf16[512,512]{1,0:T(8,128)(2,1)S(1)} collective-permute-done((bf16[512,512]{1,0:T(8,128)(2,1)}, bf16[512,512]{1,0:T(8,128)(2,1)S(1)}, u32[]{:S(2)}, u32[]{:S(2)}) %collective-permute-start.1) | collective-permute-done | bytes 524320 | tf_op jit(solution)/shard_map/ppermute | solution.py:25
  45.6 1.1 %pad_maximum_fusion.refs_0_ = bf16[2,512,512]{2,1,0:T(8,128)(2,1)S(1)} fusion(bf16[1,512,512]{2,1,0:T(8,128)(2,1)S(1)} %bitcast.13, bf16[1,512,512]{2,1,0:T(8,128)(2,1)} %bitcast.10), kind=kLoop, calls=%fused_computation | loop fusion | flops 524288 | bytes 2097152 | tf_op jit(solution)/shard_map/stack | solution.py:360
  46.8 0.0 copy-start
  46.8 3.1 %collective-permute-start.4 = (bf16[2,512,512]{2,1,0:T(8,128)(2,1)S(1)}, bf16[2,512,512]{2,1,0:T(8,128)(2,1)S(1)}, u32[]{:S(2)}, u32[]{:S(2)}) collective-permute-start(bf16[2,512,512]{2,1,0:T(8,128)(2,1)S(1)} %pad_maximum_fusion.refs_0_), channel_id=1, source_target_pairs={{0,128},{1,33},{2,130},{3,35},{4,132},{5,37},{6,134},{7,39},{8,136... | collective-permute-start | bytes 3145736 | tf_op jit(solution)/shard_map/ppermute | solution.py:29
  49.9 0.0 collective-permute-done.2
  49.9 2.5 %collective-permute-done.3 = bf16[512,512]{1,0:T(8,128)(2,1)S(1)} collective-permute-done((bf16[512,512]{1,0:T(8,128)(2,1)}, bf16[512,512]{1,0:T(8,128)(2,1)S(1)}, u32[]{:S(2)}, u32[]{:S(2)}) %collective-permute-start.3) | collective-permute-done | bytes 524320 | tf_op jit(solution)/shard_map/ppermute | solution.py:25
  52.4 0.1 pad_maximum_fusion.1.refs_1_
  52.5 0.0 copy-start.1
  52.5 5.6 %collective-permute-start.7 = (bf16[2,512,512]{2,1,0:T(8,128)(2,1)S(1)}, bf16[2,512,512]{2,1,0:T(8,128)(2,1)}, u32[]{:S(2)}, u32[]{:S(2)}) collective-permute-start(bf16[2,512,512]{2,1,0:T(8,128)(2,1)S(1)} %pad_maximum_fusion.1.refs_1_), channel_id=1, source_target_pairs={{0,384},{1,97},{2,386},{3,99},{4,388},{5,101},{6,390},{7,103},{8,3... | collective-permute-start | bytes 3145736 | tf_op jit(solution)/shard_map/ppermute | solution.py:29
  58.1 1.9 %collective-permute-start.5 = (bf16[2,512,512]{2,1,0:T(8,128)(2,1)S(1)}, bf16[2,512,512]{2,1,0:T(8,128)(2,1)}, u32[]{:S(2)}, u32[]{:S(2)}) collective-permute-start(bf16[2,512,512]{2,1,0:T(8,128)(2,1)S(1)} %pad_maximum_fusion.1.refs_1_), channel_id=1, source_target_pairs={{0,128},{1,33},{2,130},{3,35},{4,132},{5,37},{6,134},{7,39},{8,136... | collective-permute-start | bytes 3145736 | tf_op jit(solution)/shard_map/ppermute | solution.py:29
  60.0 4.6 %collective-permute-start.6 = (bf16[2,512,512]{2,1,0:T(8,128)(2,1)S(1)}, bf16[2,512,512]{2,1,0:T(8,128)(2,1)}, u32[]{:S(2)}, u32[]{:S(2)}) collective-permute-start(bf16[2,512,512]{2,1,0:T(8,128)(2,1)S(1)} %pad_maximum_fusion.refs_0_), channel_id=1, source_target_pairs={{0,384},{1,97},{2,386},{3,99},{4,388},{5,101},{6,390},{7,103},{8,3... | collective-permute-start | bytes 3145736 | tf_op jit(solution)/shard_map/ppermute | solution.py:29
  64.6 2.1 %collective-permute-done.4.refs_2_ = bf16[2,512,512]{2,1,0:T(8,128)(2,1)S(1)} collective-permute-done((bf16[2,512,512]{2,1,0:T(8,128)(2,1)S(1)}, bf16[2,512,512]{2,1,0:T(8,128)(2,1)S(1)}, u32[]{:S(2)}, u32[]{:S(2)}) %collective-permute-start.4) | collective-permute-done | bytes 1048608 | tf_op jit(solution)/shard_map/ppermute | solution.py:29
  66.7 0.0 copy-start.3
  66.7 1.9 %collective-permute-start.8 = (bf16[2,512,512]{2,1,0:T(8,128)(2,1)S(1)}, bf16[2,512,512]{2,1,0:T(8,128)(2,1)}, u32[]{:S(2)}, u32[]{:S(2)}) collective-permute-start(bf16[2,512,512]{2,1,0:T(8,128)(2,1)S(1)} %collective-permute-done.4.refs_2_), channel_id=1, source_target_pairs={{0,128},{1,33},{2,130},{3,35},{4,132},{5,37},{6,134},{7,39},{8,136... | collective-permute-start | bytes 3145736 | tf_op jit(solution)/shard_map/ppermute | solution.py:29
  68.7 1.2 %collective-permute-done.7.refs_5_ = bf16[2,512,512]{2,1,0:T(8,128)(2,1)} collective-permute-done((bf16[2,512,512]{2,1,0:T(8,128)(2,1)S(1)}, bf16[2,512,512]{2,1,0:T(8,128)(2,1)}, u32[]{:S(2)}, u32[]{:S(2)}) %collective-permute-start.7) | collective-permute-done | bytes 1048608 | tf_op jit(solution)/shard_map/ppermute | solution.py:29
  69.8 5.4 %collective-permute-start.9 = (bf16[2,512,512]{2,1,0:T(8,128)(2,1)}, bf16[2,512,512]{2,1,0:T(8,128)(2,1)}, u32[]{:S(2)}, u32[]{:S(2)}) collective-permute-start(bf16[2,512,512]{2,1,0:T(8,128)(2,1)} %collective-permute-done.7.refs_5_), channel_id=1, source_target_pairs={{0,384},{1,97},{2,386},{3,99},{4,388},{5,101},{6,390},{7,103},{8,3... | collective-permute-start | bytes 3145736 | tf_op jit(solution)/shard_map/ppermute | solution.py:29
  75.3 0.0 copy-done.4
  75.3 0.1 add_add_fusion
  75.4 0.1 add.51
  75.4 0.1 add.57
  75.5 0.5 fusion.places
  76.0 1.9 %collective-permute-done.5.refs_3_ = bf16[2,512,512]{2,1,0:T(8,128)(2,1)} collective-permute-done((bf16[2,512,512]{2,1,0:T(8,128)(2,1)S(1)}, bf16[2,512,512]{2,1,0:T(8,128)(2,1)}, u32[]{:S(2)}, u32[]{:S(2)}) %collective-permute-start.5) | collective-permute-done | bytes 1048608 | tf_op jit(solution)/shard_map/ppermute | solution.py:29
  78.0 3.1 %collective-permute-done.6.refs_4_ = bf16[2,512,512]{2,1,0:T(8,128)(2,1)} collective-permute-done((bf16[2,512,512]{2,1,0:T(8,128)(2,1)S(1)}, bf16[2,512,512]{2,1,0:T(8,128)(2,1)}, u32[]{:S(2)}, u32[]{:S(2)}) %collective-permute-start.6) | collective-permute-done | bytes 1048608 | tf_op jit(solution)/shard_map/ppermute | solution.py:29
  81.1 8.1 %collective-permute-done.8.refs_6_ = bf16[2,512,512]{2,1,0:T(8,128)(2,1)} collective-permute-done((bf16[2,512,512]{2,1,0:T(8,128)(2,1)S(1)}, bf16[2,512,512]{2,1,0:T(8,128)(2,1)}, u32[]{:S(2)}, u32[]{:S(2)}) %collective-permute-start.8) | collective-permute-done | bytes 1048608 | tf_op jit(solution)/shard_map/ppermute | solution.py:29
  89.2 5.5 %all-gather.2.cloned.1.call-done = bf16[8192,512]{1,0:T(8,128)(2,1)} async-done(((bf16[256,512]{1,0:T(8,128)(2,1)}), bf16[8192,512]{1,0:T(8,128)(2,1)}) %all-gather.2.cloned.1.call-update) | async-done | bytes 8388624 | tf_op jit(solution)/shard_map/all_gather | solution.py:343
  94.7 0.0 copy-done
  94.7 0.0 copy-done.1
  94.7 0.0 copy-done.3
  94.7 6.8 %project_near.1.total = f32[512,512]{1,0:T(8,128)S(1)} custom-call(s32[16]{0:T(128)} %fusion.places, bf16[2,512,512]{2,1,0:T(8,128)(2,1)} %copy-done, bf16[2,512,512]{2,1,0:T(8,128)(2,1)} %copy-done.1, bf16[2,512,512]{2,1,0:T(8,128)(2,1)} %copy-done.3, bf16[2,512,512]{2,1,0:T(8,128)(2,1)} %collective-permute-done.5.refs_3_, ...), custom_call_target="tpu_custom_call" | custom-call | flops 3758096384 | bytes 14680064 | tf_op jit(solution)/shard_map/project_near/pallas_call | solution.py:298
  101.5 0.0 collective-permute-done.9.panel
  101.5 3.6 %project_far.1 = bf16[512,512]{1,0:T(8,128)(2,1)} custom-call(s32[16]{0:T(128)} %fusion.places, f32[512,512]{1,0:T(8,128)S(1)} %project_near.1.total, bf16[2,512,512]{2,1,0:T(8,128)(2,1)} %collective-permute-done.9.panel, bf16[16,512,512]{2,1,0:T(8,128)(2,1)} %bitcast.9), custom_call_target="tpu_custom_call" | custom-call | flops 536870912 | bytes 2097152 | tf_op jit(solution)/shard_map/project_far/pallas_call | solution.py:314
Async XLA Ops:
  6.5 68.7 %copy-start.4 = (s32[4]{0:T(128)S(1)}, s32[4]{0:T(128)}, u32[]{:S(2)}) copy-start(s32[4]{0:T(128)} %constant.60.clone) | copy-start | bytes 52
  6.5 88.2 %all-gather.2.cloned.1.call-start = ((), (), s32[]{:S(2)}) async-start(), calls=%async_computation | async-start | bytes 8650752 | tf_op jit(solution)/shard_map/all_gather | solution.py:343
  9.7 13.6 %collective-permute-start = (bf16[320,512]{1,0:T(8,128)(2,1)}, bf16[320,512]{1,0:T(8,128)(2,1)S(1)}, u32[]{:S(2)}, u32[]{:S(2)}) collective-permute-start(bf16[320,512]{1,0:T(8,128)(2,1)} %pack_tail.1), channel_id=1, source_target_pairs={{0,1},{1,2},{2,3},{3,4},{4,5},{5,6},{6,7},{7,8},{8,9},{9,10},{10,1... | collective-permute-start | bytes 983048 | tf_op jit(solution)/shard_map/ppermute | solution.py:356
  23.3 0.8 copy-start.2
  33.8 11.8 %collective-permute-start.1 = (bf16[512,512]{1,0:T(8,128)(2,1)}, bf16[512,512]{1,0:T(8,128)(2,1)S(1)}, u32[]{:S(2)}, u32[]{:S(2)}) collective-permute-start(bf16[512,512]{1,0:T(8,128)(2,1)} %gate_early.1), channel_id=1, source_target_pairs={{0,32},{1,129},{2,34},{3,131},{4,36},{5,133},{6,38},{7,135},{8,40}... | collective-permute-start | bytes 1572872 | tf_op jit(solution)/shard_map/ppermute | solution.py:25
  37.0 12.9 %collective-permute-start.2 = (bf16[512,512]{1,0:T(8,128)(2,1)}, bf16[512,512]{1,0:T(8,128)(2,1)S(1)}, u32[]{:S(2)}, u32[]{:S(2)}) collective-permute-start(bf16[512,512]{1,0:T(8,128)(2,1)} %gate_early.1), channel_id=1, source_target_pairs={{0,96},{1,385},{2,98},{3,387},{4,100},{5,389},{6,102},{7,391},{8,1... | collective-permute-start | bytes 1572872 | tf_op jit(solution)/shard_map/ppermute | solution.py:25
  40.4 12.0 %collective-permute-start.3 = (bf16[512,512]{1,0:T(8,128)(2,1)}, bf16[512,512]{1,0:T(8,128)(2,1)S(1)}, u32[]{:S(2)}, u32[]{:S(2)}) collective-permute-start(bf16[512,512]{1,0:T(8,128)(2,1)} %gate_early.1), channel_id=1, source_target_pairs={{0,64},{1,257},{2,66},{3,259},{4,68},{5,261},{6,70},{7,263},{8,72}... | collective-permute-start | bytes 1572872 | tf_op jit(solution)/shard_map/ppermute | solution.py:25
  46.8 47.9 %copy-start = (bf16[2,512,512]{2,1,0:T(8,128)(2,1)}, bf16[2,512,512]{2,1,0:T(8,128)(2,1)S(1)}, u32[]{:S(2)}) copy-start(bf16[2,512,512]{2,1,0:T(8,128)(2,1)S(1)} %pad_maximum_fusion.refs_0_) | copy-start | bytes 3145732
  46.8 19.9 %collective-permute-start.4 = (bf16[2,512,512]{2,1,0:T(8,128)(2,1)S(1)}, bf16[2,512,512]{2,1,0:T(8,128)(2,1)S(1)}, u32[]{:S(2)}, u32[]{:S(2)}) collective-permute-start(bf16[2,512,512]{2,1,0:T(8,128)(2,1)S(1)} %pad_maximum_fusion.refs_0_), channel_id=1, source_target_pairs={{0,128},{1,33},{2,130},{3,35},{4,132},{5,37},{6,134},{7,39},{8,136... | collective-permute-start | bytes 3145736 | tf_op jit(solution)/shard_map/ppermute | solution.py:29
  52.5 42.2 %copy-start.1 = (bf16[2,512,512]{2,1,0:T(8,128)(2,1)}, bf16[2,512,512]{2,1,0:T(8,128)(2,1)S(1)}, u32[]{:S(2)}) copy-start(bf16[2,512,512]{2,1,0:T(8,128)(2,1)S(1)} %pad_maximum_fusion.1.refs_1_) | copy-start | bytes 3145732
  52.5 17.3 %collective-permute-start.7 = (bf16[2,512,512]{2,1,0:T(8,128)(2,1)S(1)}, bf16[2,512,512]{2,1,0:T(8,128)(2,1)}, u32[]{:S(2)}, u32[]{:S(2)}) collective-permute-start(bf16[2,512,512]{2,1,0:T(8,128)(2,1)S(1)} %pad_maximum_fusion.1.refs_1_), channel_id=1, source_target_pairs={{0,384},{1,97},{2,386},{3,99},{4,388},{5,101},{6,390},{7,103},{8,3... | collective-permute-start | bytes 3145736 | tf_op jit(solution)/shard_map/ppermute | solution.py:29
  58.1 19.9 %collective-permute-start.5 = (bf16[2,512,512]{2,1,0:T(8,128)(2,1)S(1)}, bf16[2,512,512]{2,1,0:T(8,128)(2,1)}, u32[]{:S(2)}, u32[]{:S(2)}) collective-permute-start(bf16[2,512,512]{2,1,0:T(8,128)(2,1)S(1)} %pad_maximum_fusion.1.refs_1_), channel_id=1, source_target_pairs={{0,128},{1,33},{2,130},{3,35},{4,132},{5,37},{6,134},{7,39},{8,136... | collective-permute-start | bytes 3145736 | tf_op jit(solution)/shard_map/ppermute | solution.py:29
  60.0 21.0 %collective-permute-start.6 = (bf16[2,512,512]{2,1,0:T(8,128)(2,1)S(1)}, bf16[2,512,512]{2,1,0:T(8,128)(2,1)}, u32[]{:S(2)}, u32[]{:S(2)}) collective-permute-start(bf16[2,512,512]{2,1,0:T(8,128)(2,1)S(1)} %pad_maximum_fusion.refs_0_), channel_id=1, source_target_pairs={{0,384},{1,97},{2,386},{3,99},{4,388},{5,101},{6,390},{7,103},{8,3... | collective-permute-start | bytes 3145736 | tf_op jit(solution)/shard_map/ppermute | solution.py:29
  66.7 28.0 %copy-start.3 = (bf16[2,512,512]{2,1,0:T(8,128)(2,1)}, bf16[2,512,512]{2,1,0:T(8,128)(2,1)S(1)}, u32[]{:S(2)}) copy-start(bf16[2,512,512]{2,1,0:T(8,128)(2,1)S(1)} %collective-permute-done.4.refs_2_) | copy-start | bytes 3145732
  66.7 22.5 %collective-permute-start.8 = (bf16[2,512,512]{2,1,0:T(8,128)(2,1)S(1)}, bf16[2,512,512]{2,1,0:T(8,128)(2,1)}, u32[]{:S(2)}, u32[]{:S(2)}) collective-permute-start(bf16[2,512,512]{2,1,0:T(8,128)(2,1)S(1)} %collective-permute-done.4.refs_2_), channel_id=1, source_target_pairs={{0,128},{1,33},{2,130},{3,35},{4,132},{5,37},{6,134},{7,39},{8,136... | collective-permute-start | bytes 3145736 | tf_op jit(solution)/shard_map/ppermute | solution.py:29
  69.8 31.7 %collective-permute-start.9 = (bf16[2,512,512]{2,1,0:T(8,128)(2,1)}, bf16[2,512,512]{2,1,0:T(8,128)(2,1)}, u32[]{:S(2)}, u32[]{:S(2)}) collective-permute-start(bf16[2,512,512]{2,1,0:T(8,128)(2,1)} %collective-permute-done.7.refs_5_), channel_id=1, source_target_pairs={{0,384},{1,97},{2,386},{3,99},{4,388},{5,101},{6,390},{7,103},{8,3... | collective-permute-start | bytes 3145736 | tf_op jit(solution)/shard_map/ppermute | solution.py:29
Sparse Core Ops, SparseCore 0:
  9.5 85.1 all-gather.1
